TPU v7x, 32 devices: a whole 2x2x4 slice. The times are simulated.
32 devices in a mesh: parts: 2 (over y), tensor: 4 (over z), dp: 4 (over x, core).
Axes of the slice: x: 2, y: 2, z: 4, core: 2. Of those that a mesh axis runs over, the one named last changes fastest.
Arguments:
- attention_output: bfloat16 [8192, 8192], P(('parts', 'dp'), 'tensor'), parts along dimension 0, may hold values from -6 to 6
- projection_output_gradient: bfloat16 [8192, 5120], P(('parts', 'dp'), 'tensor'), parts along dimension 0, may hold values from -6 to 6
- token_adapter_index: int32 [8192], P(('parts', 'dp')), parts along dimension 0, may hold values from 0 to 63
- owner_slot_adapter: int32 [64], replicated, may hold values from 0 to 63, each once
- output_projection_weight: bfloat16 [8192, 5120], P('tensor'), may hold values from -0.0625 to 0.0625
- adapter_down_weight: bfloat16 [64, 16, 8192], P(None, None, 'tensor'), may hold values from -0.0625 to 0.0625
- adapter_up_weight: bfloat16 [64, 16, 5120], P(None, None, 'tensor'), may hold values from -0.078125 to 0.078125
Outputs:
- attention_gradient: bfloat16 [8192, 8192], P(('parts', 'dp'), 'tensor'), parts along dimension 0
- grad_a: float32 [128, 16, 8192], P(('parts', 'dp'), None, 'tensor'), parts along dimension 0
- grad_b: float32 [128, 16, 5120], P(('parts', 'dp'), None, 'tensor'), parts along dimension 0
There are 2 independent parts, one for each index of `parts`. A program takes and returns all parts, laid end to end along the dimension named above; an argument that names none is the same for every part. Nothing has to cross between parts.
Inputs may be any that keep to these rules, and one draw needn't show every extreme that they name: `owner_slot_adapter`: each adapter appears exactly once.
All inputs are finite; a program needn't handle non-finite values.
Results may differ from a plain program's by a relative error of at most 0.0031.
Values may be sent and summed in bfloat16 or wider, within the bound.
No kernel may reach another device: no remote copies, remote signals or barrier semaphores. Data moves between devices by JAX's collectives and lax.ppermute only.
A program may use at most 192 MiB of HBM per device.

v0:
```python
import jax
import jax.numpy as jnp
from jax import lax
from jax.sharding import PartitionSpec as P

ADAPTER_SCALE = 2.0
OBJECTIVE_WEIGHT = 0.05


def pick_rows(selected, values):
    no_value = jnp.zeros((), values.dtype)
    return jnp.where(selected[:, :, None], values[:, None, :], no_value)


def per_device(
    attention_output,
    projection_output_gradient,
    token_adapter_index,
    owner_slot_adapter,
    output_projection_weight,
    adapter_down_weight,
    adapter_up_weight,
):
    adapter_list, rank_extent, attention_columns = adapter_down_weight.shape
    width_columns = adapter_up_weight.shape[2]
    row_count = attention_output.shape[0]
    row_dims = (((1,), (1,)), ((), ()))
    tok_dims = (((0,), (0,)), ((), ()))
    labels = jnp.arange(adapter_list, dtype=jnp.int32)
    chosen = token_adapter_index[:, None] == labels[None, :]
    input_rows = adapter_down_weight.reshape(adapter_list * rank_extent, attention_columns)
    output_rows = adapter_up_weight.reshape(adapter_list * rank_extent, width_columns)
    u_terms = lax.dot_general(
        attention_output, input_rows, row_dims, preferred_element_type=jnp.float32
    )
    u_terms = u_terms.reshape(row_count, adapter_list, rank_extent)
    g_terms = lax.dot_general(
        projection_output_gradient, output_rows, row_dims, preferred_element_type=jnp.float32
    )
    g_terms = g_terms.reshape(row_count, adapter_list, rank_extent)
    fzero = jnp.zeros((), jnp.float32)
    in_part = jnp.sum(jnp.where(chosen[:, :, None], u_terms, fzero), axis=1)
    out_part = jnp.sum(jnp.where(chosen[:, :, None], g_terms, fzero), axis=1)
    low_in, low_out = lax.psum((in_part, out_part), "tensor")
    in_bf = low_in.astype(jnp.bfloat16)
    out_bf = low_out.astype(jnp.bfloat16)
    g_wide = pick_rows(chosen, out_bf).reshape(row_count, adapter_list * rank_extent)
    adapter_contribution = jnp.dot(g_wide, input_rows, preferred_element_type=jnp.float32)
    full_grad = lax.all_gather(projection_output_gradient, "tensor", axis=1, tiled=True)
    frozen_contribution = lax.dot_general(
        full_grad, output_projection_weight, row_dims, preferred_element_type=jnp.float32
    )
    attention_gradient = (frozen_contribution + ADAPTER_SCALE * adapter_contribution).astype(
        jnp.bfloat16
    )
    owned_hot = token_adapter_index[:, None] == owner_slot_adapter[None, :]
    g_own = pick_rows(owned_hot, out_bf).reshape(row_count, adapter_list * rank_extent)
    u_own = pick_rows(owned_hot, in_bf).reshape(row_count, adapter_list * rank_extent)
    gradient_multiplier = ADAPTER_SCALE * OBJECTIVE_WEIGHT
    term_a = gradient_multiplier * lax.dot_general(
        g_own, attention_output, tok_dims, preferred_element_type=jnp.float32
    )
    term_b = gradient_multiplier * lax.dot_general(
        u_own, projection_output_gradient, tok_dims, preferred_element_type=jnp.float32
    )
    term_a = term_a.reshape(adapter_list, rank_extent, attention_columns)
    term_b = term_b.reshape(adapter_list, rank_extent, width_columns)
    total_a, total_b = lax.psum((term_a, term_b), "dp")
    own_count = adapter_list // lax.axis_size("dp")
    first_slot = lax.axis_index("dp") * own_count
    grad_a = lax.dynamic_slice_in_dim(total_a, first_slot, own_count, 0)
    grad_b = lax.dynamic_slice_in_dim(total_b, first_slot, own_count, 0)
    return (attention_gradient, grad_a, grad_b)


def solution(mesh):
    placed = (
        P(("parts", "dp"), "tensor"),
        P(("parts", "dp"), "tensor"),
        P(("parts", "dp")),
        P(),
        P("tensor", None),
        P(None, None, "tensor"),
        P(None, None, "tensor"),
    )
    return jax.shard_map(
        per_device,
        mesh=mesh,
        in_specs=placed,
        out_specs=(
            P(("parts", "dp"), "tensor"),
            P(("parts", "dp"), None, "tensor"),
            P(("parts", "dp"), None, "tensor"),
        ),
        check_vma=False,
    )
```

profile of v0, /device:TPU:0, one launch (start us, length us, event | category | flops | bytes accessed | tf_op | source)
XLA Modules:
  0.0 339.2 jit_solution(17890571800497980564)
XLA Ops:
  8.0 0.0 copy-start
  8.0 0.0 all-reduce.5.cloned.1.call-start
  8.1 0.9 broadcast_compare_fusion
  9.0 0.0 copy-start.2
  9.0 9.0 %select_reduce_fusion = f32[1024,16]{0,1:T(8,128)S(1)} fusion(pred[1024,64]{0,1:T(8,128)(4,1)S(1)} %get-tuple-element.10, bf16[64,16,2048]{2,1,0:T(8,128)(2,1)} %param.12, bf16[1024,2048]{1,0:T(8,128)(2,1)} %param.7), kind=kOutput, calls=%fused_computation.7 | convolution fusion | flops 4297048064 | bytes 8519680 | tf_op jit(solution)/shard_map/dot_general | solution.py:33
  18.0 0.0 copy-done
  18.0 3.5 %select_reduce_fusion.1 = f32[1024,16]{0,1:T(8,128)S(1)} fusion(pred[1024,64]{0,1:T(8,128)(4,1)S(1)} %get-tuple-element.10, bf16[64,16,1280]{2,1,0:T(8,128)(2,1)S(1)} %copy-done, bf16[1024,1280]{1,0:T(8,128)(2,1)S(1)} %copy-done.2), kind=kOutput, calls=%fused_computation.8 | convolution fusion | flops 2686435328 | bytes 5373952 | tf_op jit(solution)/shard_map/dot_general | solution.py:37
  21.6 23.2 %all-reduce.6 = (bf16[1024,16]{0,1:T(8,128)(2,1)S(1)}, bf16[1024,16]{0,1:T(8,128)(2,1)S(1)}) all-reduce(f32[1024,16]{0,1:T(8,128)S(1)} %select_reduce_fusion.1, f32[1024,16]{0,1:T(8,128)S(1)} %select_reduce_fusion), channel_id=1, replica_groups=mesh['parts'=2,'tensor'=4,'dp'=4] {'tensor'}, use_global_device_ids=true, to_apply=%region_1.2 | all-reduce | flops 32768 | bytes 196608 | tf_op jit(solution)/shard_map/psum | solution.py:44
  44.8 0.0 copy-start.4
  44.8 0.3 broadcast_select_fusion
  45.1 1.2 copy.15
  46.2 0.7 copy-done.4
  46.9 6.8 %convolution_multiply_fusion.1 = f32[1024,2048]{1,0:T(8,128)} fusion(bf16[1024,1024]{0,1:T(8,128)(2,1)S(1)} %bitcast.28, bf16[1024,2048]{1,0:T(8,128)(2,1)S(1)} %copy-done.4), kind=kOutput, calls=%fused_computation.4 | convolution fusion | flops 4297064448 | bytes 14680064 | tf_op jit(solution)/shard_map/dot_general | solution.py:60
  53.7 1.2 copy.17
  54.9 0.6 copy-done.3
  55.5 4.5 %convolution_multiply_fusion = f32[1024,1280]{1,0:T(8,128)} fusion(bf16[1024,1024]{0,1:T(8,128)(2,1)S(1)} %bitcast.29, bf16[1024,1280]{1,0:T(8,128)(2,1)S(1)} %copy-done.3), kind=kOutput, calls=%fused_computation.3 | convolution fusion | flops 2685665280 | bytes 9961472 | tf_op jit(solution)/shard_map/dot_general | solution.py:63
  60.0 0.0 all-reduce.5.cloned.1.call-update
  60.0 0.2 all-gather.2.cloned.1.call-start
  60.3 0.3 all-gather.2.cloned.1.call-update
  60.6 15.5 %fusion.5 = f32[1024,2048,1]{1,0,2:T(8,128)} fusion(bf16[64,16,2048]{2,1,0:T(8,128)(2,1)} %param.12, pred[1024,64]{0,1:T(8,128)(4,1)S(1)} %get-tuple-element.10, bf16[1024,16]{0,1:T(8,128)(2,1)S(1)} %get-tuple-element.5), kind=kOutput, calls=%fused_computation.10 | convolution fusion | flops 4296015872 | bytes 12681216 | tf_op jit(solution)/shard_map/dot_general | solution.py:48
  76.1 220.3 %all-reduce.5.cloned.1.call-done = (f32[64,16,2048]{2,1,0:T(8,128)}, f32[64,16,1280]{2,1,0:T(8,128)}) async-done(((f32[64,16,2048]{2,1,0:T(8,128)}, f32[64,16,1280]{2,1,0:T(8,128)}), (f32[64,16,2048]{2,1,0:T(8,128)}, f32[64,16,1280]{2,1,0:T(8,128)})) %all-reduce.5.cloned.1.call-update) | async-done | bytes 13631504 | tf_op jit(solution)/shard_map/psum | solution.py:68
  296.4 3.1 constant_dynamic-slice_fusion.1
  299.5 2.5 constant_dynamic-slice_fusion
  302.0 29.7 %fusion.1 = bf16[1024,2048]{1,0:T(8,128)(2,1)} fusion(f32[1024,2048,1]{1,0,2:T(8,128)} %fusion.5, bf16[1024,5120]{1,0:T(8,128)(2,1)} %all-gather.2.cloned.1.call-done, bf16[2048,5120]{1,0:T(8,128)(2,1)} %param.11), kind=kOutput, calls=%fused_computation.2 | convolution fusion | flops 21481127936 | bytes 44040192 | tf_op jit(solution)/shard_map/dot_general | solution.py:50
  (5 shorter events, 0.0 us)
Async XLA Ops:
  8.0 10.0 %copy-start = (bf16[64,16,1280]{2,1,0:T(8,128)(2,1)S(1)}, bf16[64,16,1280]{2,1,0:T(8,128)(2,1)}, u32[]{:S(2)}) copy-start(bf16[64,16,1280]{2,1,0:T(8,128)(2,1)} %param.13) | copy-start | bytes 7864324
  8.0 288.4 %all-reduce.5.cloned.1.call-start = ((), (), s32[]{:S(2)}) async-start(), calls=%async_computation.1 | async-start | bytes 27262976 | tf_op jit(solution)/shard_map/psum | solution.py:68
  9.0 9.0 %copy-start.2 = (bf16[1024,1280]{1,0:T(8,128)(2,1)S(1)}, bf16[1024,1280]{1,0:T(8,128)(2,1)}, u32[]{:S(2)}) copy-start(bf16[1024,1280]{1,0:T(8,128)(2,1)} %param.8) | copy-start | bytes 7864324
  44.8 2.2 copy-start.4
  53.7 1.7 copy-start.3
  60.0 242.0 %all-gather.2.cloned.1.call-start = ((), (), s32[]{:S(2)}) async-start(), calls=%async_computation | async-start | bytes 13107200 | tf_op jit(solution)/shard_map/all_gather | solution.py:49
  302.0 29.7 %copy-start.1 = (bf16[64,16,1280]{2,1,0:T(8,128)(2,1)S(1)}, bf16[64,16,1280]{2,1,0:T(8,128)(2,1)}, u32[]{:S(2)}) copy-start(bf16[64,16,1280]{2,1,0:T(8,128)(2,1)} %param.13) | copy-start | bytes 7864324
Sparse Core Ops, SparseCore 0:
  60.1 236.2 all-reduce.4
Sparse Core Ops, SparseCore 1:
  62.1 182.0 all-gather.1
where the time goes:
time: 340 us; the launch traced here: 339 us
  waiting for transfers between devices  221 us (65%)
  matrix products  69.1 us (20%)
  blocking collectives  23.2 us (7%)
  between operations  15.6 us (5%)
  local copies, waits for them, and re-layouts  9.25 us (3%)
    psum x1, waiting for transfers between devices, per_device(): total_a, total_b = lax.psum((term_a, term_b), 'dp')  220 us
    dot_general x1, matrix products, per_device(): lax.dot_general(full_grad, output_projection_weight, row_dims, preferred_...  29.7 us
    psum x1, blocking collectives, per_device(): low_in, low_out = lax.psum((in_part, out_part), 'tensor')  23.2 us
    dot_general x1, matrix products, per_device(): jnp.dot(g_wide, input_rows, preferred_element_type=jnp.float32)  15.5 us
    dot_general x1, matrix products, per_device(): lax.dot_general(attention_output, input_rows, row_dims, preferred_element...  8.99 us
  transfers between devices with their start and end apart: 2, of which 1 were waited for; matrix products, arithmetic and copies ran while one was open for 6% of the time, Pallas kernels for 0%

commit v1 on v0

v1 whole, which is shorter than its diff:
```python
import jax
import jax.numpy as jnp
from jax import lax
from jax.sharding import PartitionSpec as P

ADAPTER_SCALE = 2.0
OBJECTIVE_WEIGHT = 0.05


def pairs(size, distance):
    return [(i, i ^ distance) for i in range(size)]


def power_of_two(size):
    return size & (size - 1) == 0


def low_rank_part(rows, values, chosen):
    adapters, tokens = chosen.shape
    terms = lax.dot_general(
        rows, values, (((1,), (1,)), ((), ())), preferred_element_type=jnp.float32
    )
    terms = terms.reshape(adapters, -1, tokens)
    return jnp.sum(jnp.where(chosen[:, None, :], terms, jnp.zeros((), jnp.float32)), axis=0)


def spread(chosen, low):
    adapters, tokens = chosen.shape
    wide = jnp.where(chosen[:, None, :], low[None], jnp.zeros((), low.dtype))
    return wide.reshape(adapters * low.shape[0], tokens)


def sum_over_tensor(part, size):
    if not power_of_two(size) or size > 4:
        return lax.psum(part, "tensor")
    terms = [part] + [lax.ppermute(part, "tensor", pairs(size, d)) for d in range(1, size)]
    while len(terms) > 1:
        terms = [terms[i] + terms[i + 1] for i in range(0, len(terms), 2)]
    return terms[0]


def reduce_to_owner(term_a, term_b, size):
    if size != 4:
        return tuple(
            lax.psum_scatter(t, "dp", scatter_dimension=0, tiled=True) for t in (term_a, term_b)
        )
    for distance in (1, 2):
        half = term_a.shape[0] // 2
        got_a = lax.ppermute(term_a[:half], "dp", pairs(size, distance))
        got_b = lax.ppermute(term_b[:half], "dp", pairs(size, distance))
        term_a = term_a[half:] + got_a
        term_b = term_b[half:] + got_b
    return term_a, term_b


def per_device(
    attention_output,
    projection_output_gradient,
    token_adapter_index,
    owner_slot_adapter,
    output_projection_weight,
    adapter_down_weight,
    adapter_up_weight,
):
    adapters, rank, attention_columns = adapter_down_weight.shape
    width_columns = adapter_up_weight.shape[2]
    tokens = attention_output.shape[0]
    tensor_size = lax.axis_size("tensor")
    dp_size = lax.axis_size("dp")
    input_rows = adapter_down_weight.reshape(adapters * rank, attention_columns)
    output_rows = adapter_up_weight.reshape(adapters * rank, width_columns)
    labels = jnp.arange(adapters, dtype=jnp.int32)
    chosen = labels[:, None] == token_adapter_index[None, :]
    row_dims = (((1,), (1,)), ((), ()))

    full_gradient = lax.all_gather(projection_output_gradient, "tensor", axis=1, tiled=True)

    out_part = low_rank_part(output_rows, projection_output_gradient, chosen)
    in_part = low_rank_part(input_rows, attention_output, chosen)
    low = sum_over_tensor(jnp.concatenate([in_part, out_part], axis=0), tensor_size)
    low_b = low.astype(jnp.bfloat16)
    in_b, out_b = low_b[:rank], low_b[rank:]

    if dp_size == 4:
        order = jnp.array([3, 1, 2, 0], jnp.int32) ^ lax.axis_index("dp")
        slots = owner_slot_adapter.reshape(dp_size, -1)[order].reshape(-1)
    else:
        slots = owner_slot_adapter
    owned = slots[:, None] == token_adapter_index[None, :]
    multiplier = ADAPTER_SCALE * OBJECTIVE_WEIGHT
    term_a = multiplier * jnp.dot(
        spread(owned, out_b), attention_output, preferred_element_type=jnp.float32
    )
    term_b = multiplier * jnp.dot(
        spread(owned, in_b), projection_output_gradient, preferred_element_type=jnp.float32
    )
    grad_a, grad_b = reduce_to_owner(term_a, term_b, dp_size)
    grad_a = grad_a.reshape(-1, rank, attention_columns)
    grad_b = grad_b.reshape(-1, rank, width_columns)

    wide = spread(chosen, out_b)
    contribution = lax.dot_general(
        wide, input_rows, (((0,), (0,)), ((), ())), preferred_element_type=jnp.float32
    )
    frozen = lax.dot_general(
        full_gradient, output_projection_weight, row_dims, preferred_element_type=jnp.float32
    )
    attention_gradient = (frozen + ADAPTER_SCALE * contribution).astype(jnp.bfloat16)
    return attention_gradient, grad_a, grad_b


def solution(mesh):
    placed = (
        P(("parts", "dp"), "tensor"),
        P(("parts", "dp"), "tensor"),
        P(("parts", "dp")),
        P(),
        P("tensor", None),
        P(None, None, "tensor"),
        P(None, None, "tensor"),
    )
    return jax.shard_map(
        per_device,
        mesh=mesh,
        in_specs=placed,
        out_specs=(
            P(("parts", "dp"), "tensor"),
            P(("parts", "dp"), None, "tensor"),
            P(("parts", "dp"), None, "tensor"),
        ),
        check_vma=False,
    )
```

time: 340 us -> 243 us (0.71)
  waiting for transfers between devices: 221 us -> 156 us
  blocking collectives: 23.2 us -> 0 us
  matrix products: 69.1 us -> 54.1 us
  starting transfers between devices: 0.26 us -> 8.07 us
  local copies, waits for them, and re-layouts: 9.25 us -> 3.5 us
  other arithmetic: 1.23 us -> 6.33 us
    psum x1 -> x0, waiting for transfers between devices: 220 us -> none  [per_device(): total_a, total_b = lax.psum((term_a, term_b), 'dp')]
    ppermute x0 -> x7, waiting for transfers between devices: none -> 88.7 us  [the longest x2 43.3 us: reduce_to_owner(): got_a = lax.ppermute(term_a[:half], 'dp', pairs(size, distance))]
    all_gather x1, waiting for transfers between devices: 0.01 us -> 67.1 us  [per_device(): lax.all_gather(projection_output_gradient, 'tensor', axis=1, tiled=True)]
    psum x1 -> x0, blocking collectives: 23.2 us -> none  [per_device(): low_in, low_out = lax.psum((in_part, out_part), 'tensor')]
    dot_general x6, matrix products: 69.1 us -> 54.1 us  [the longest x1 29.7 us: per_device(): lax.dot_general(full_gradient, output_projection_weight, row_dims, prefer...]
    ppermute x0 -> x7, starting transfers between devices: none -> 8.03 us  [the longest x3 5.68 us: sum_over_tensor(): lax.ppermute(part, 'tensor', pairs(size, d))]
    dynamic_slice x2 -> x0, local copies, waits for them, and re-layouts: 5.6 us -> none  [the longest x1 3.13 us: per_device(): grad_a = lax.dynamic_slice_in_dim(total_a, first_slot, own_count, 0)]
    add x0 -> x4, other arithmetic: none -> 4.45 us  [the longest x2 2.72 us: reduce_to_owner(): term_a = term_a[half:] + got_a]
  transfers between devices with their start and end apart: 2 -> 8, of which waited for: 1 -> 5; matrix products, arithmetic and copies ran while one was open for 6% -> 14% of each run, Pallas kernels for 0% -> 0%
where the time goes in v1:
time: 243 us
  waiting for transfers between devices  156 us (64%)
  matrix products  54.1 us (22%)
  between operations  14.2 us (6%)
  starting transfers between devices  8.07 us (3%)
  other arithmetic  6.33 us (3%)
  local copies, waits for them, and re-layouts  3.5 us (1%)
    all_gather x1, waiting for transfers between devices, per_device(): lax.all_gather(projection_output_gradient, 'tensor', axis=1, tiled=True)  67.1 us
    ppermute x2, waiting for transfers between devices, reduce_to_owner(): got_a = lax.ppermute(term_a[:half], 'dp', pairs(size, distance))  43.3 us
    dot_general x1, matrix products, per_device(): lax.dot_general(full_gradient, output_projection_weight, row_dims, prefer...  29.7 us
    ppermute x2, waiting for transfers between devices, reduce_to_owner(): got_b = lax.ppermute(term_b[:half], 'dp', pairs(size, distance))  27.5 us
    ppermute x3, waiting for transfers between devices, sum_over_tensor(): lax.ppermute(part, 'tensor', pairs(size, d))  18 us
    dot_general x2, matrix products, low_rank_part(): lax.dot_general(rows, values, (((1,), (1,)), ((), ())), preferred_element...  9.79 us
    dot_general x1, matrix products, per_device(): lax.dot_general(wide, input_rows, (((0,), (0,)), ((), ())), preferred_ele...  7.12 us
    ppermute x3, starting transfers between devices, sum_over_tensor(): lax.ppermute(part, 'tensor', pairs(size, d))  5.68 us
  transfers between devices with their start and end apart: 8, of which 5 were waited for; matrix products, arithmetic and copies ran while one was open for 14% of the time, Pallas kernels for 0%

profile of v1, /device:TPU:0, one launch (start us, length us, event | category | flops | bytes accessed | tf_op | source)
XLA Modules:
  0.0 242.6 jit_solution(7790380838909350583)
XLA Ops:
  7.2 0.7 all-gather.2.cloned.1.call-update
  7.9 0.8 reshape.77
  8.7 0.7 compare_select_fusion
  9.4 0.6 gather_fusion
  10.0 0.8 broadcast_compare_fusion
  10.8 5.0 %select_reduce_fusion = f32[16,1024]{1,0:T(8,128)S(1)} fusion(pred[64,1024]{1,0:T(8,128)(4,1)S(1)} %get-tuple-element.8, bf16[64,16,1280]{2,1,0:T(8,128)(2,1)S(1)} %copy-done, bf16[1024,1280]{1,0:T(8,128)(2,1)} %param.9), kind=kOutput, calls=%fused_computation.9 | convolution fusion | flops 2686435328 | bytes 5373952 | tf_op jit(solution)/shard_map/dot_general | solution.py:20
  15.9 4.8 %select_reduce_fusion.1 = f32[16,1024]{1,0:T(8,128)S(1)} fusion(pred[64,1024]{1,0:T(8,128)(4,1)S(1)} %get-tuple-element.8, bf16[64,16,2048]{2,1,0:T(8,128)(2,1)S(1)} %copy-done.4, bf16[1024,2048]{1,0:T(8,128)(2,1)S(1)} %copy-done.3), kind=kOutput, calls=%fused_computation.10 | convolution fusion | flops 4297048064 | bytes 8519680 | tf_op jit(solution)/shard_map/dot_general | solution.py:20
  20.7 4.1 %collective-permute-start.1 = (f32[32,1024]{1,0:T(8,128)S(1)}, f32[32,1024]{1,0:T(8,128)S(1)}, u32[]{:S(2)}, u32[]{:S(2)}) collective-permute-start(f32[32,1024]{1,0:T(8,128)S(1)} %pad_maximum_fusion), channel_id=1, source_target_pairs={{0,8},{4,12},{8,0},{12,4},{1,9},{5,13},{9,1},{13,5},{2,10},{6,14},... | collective-permute-start | bytes 393224 | tf_op jit(solution)/shard_map/ppermute | solution.py:36
  24.8 1.3 collective-permute-start.2
  26.4 18.0 %collective-permute-done.1 = f32[32,1024]{1,0:T(8,128)S(1)} collective-permute-done((f32[32,1024]{1,0:T(8,128)S(1)}, f32[32,1024]{1,0:T(8,128)S(1)}, u32[]{:S(2)}, u32[]{:S(2)}) %collective-permute-start.1) | collective-permute-done | bytes 131104 | tf_op jit(solution)/shard_map/ppermute | solution.py:36
  44.8 4.5 %convolution_multiply_fusion.1 = f32[1024,2048]{1,0:T(8,128)S(1)} fusion(bf16[1024,1024]{1,0:T(8,128)(2,1)S(1)} %bitcast.31, bf16[1024,2048]{1,0:T(8,128)(2,1)S(1)} %copy-done.3), kind=kOutput, calls=%fused_computation.5 | convolution fusion | flops 4297064448 | bytes 14680064 | tf_op jit(solution)/shard_map/dot_general | solution.py:91
  49.7 1.4 copy-done.2
  51.0 2.9 %convolution_multiply_fusion = f32[1024,1280]{1,0:T(8,128)S(1)} fusion(bf16[1024,1024]{1,0:T(8,128)(2,1)S(1)} %bitcast.30, bf16[1024,1280]{1,0:T(8,128)(2,1)S(1)} %copy-done.2), kind=kOutput, calls=%fused_computation.4 | convolution fusion | flops 2685665280 | bytes 9961472 | tf_op jit(solution)/shard_map/dot_general | solution.py:94
  54.2 6.4 %collective-permute-done.5 = f32[512,1280]{1,0:T(8,128)S(1)} collective-permute-done((f32[512,1280]{1,0:T(8,128)S(1)}, f32[512,1280]{1,0:T(8,128)S(1)}, u32[]{:S(2)}, u32[]{:S(2)}) %collective-permute-start.5) | collective-permute-done | bytes 2621472 | tf_op jit(solution)/shard_map/ppermute | solution.py:50
  60.6 0.5 slice_add_fusion.1
  61.2 2.1 collective-permute-start.6
  63.3 1.1 slice_add_fusion
  64.7 7.1 %fusion.6 = f32[1024,2048,1]{1,0,2:T(8,128)} fusion(bf16[64,16,2048]{2,1,0:T(8,128)(2,1)S(1)} %copy-done.4, pred[64,1024]{1,0:T(8,128)(4,1)S(1)} %get-tuple-element.8, bf16[16,1024]{1,0:T(8,128)(2,1)S(1)} %get-tuple-element.6), kind=kOutput, calls=%fused_computation.15 | convolution fusion | flops 4296015872 | bytes 12681216 | tf_op jit(solution)/shard_map/dot_general | solution.py:102
  71.8 21.1 %collective-permute-done.6 = f32[256,1280]{1,0:T(8,128)S(1)} collective-permute-done((f32[256,1280]{1,0:T(8,128)S(1)}, f32[256,1280]{1,0:T(8,128)S(1)}, u32[]{:S(2)}, u32[]{:S(2)}) %collective-permute-start.6) | collective-permute-done | bytes 1310752 | tf_op jit(solution)/shard_map/ppermute | solution.py:50
  92.9 1.2 slice_add_fusion.3
  94.1 43.3 %collective-permute-done.4 = f32[256,2048]{1,0:T(8,128)S(1)} collective-permute-done((f32[256,2048]{1,0:T(8,128)S(1)}, f32[256,2048]{1,0:T(8,128)S(1)}, u32[]{:S(2)}, u32[]{:S(2)}) %collective-permute-start.4) | collective-permute-done | bytes 2097184 | tf_op jit(solution)/shard_map/ppermute | solution.py:49
  137.3 1.6 slice_add_fusion.2
  139.0 67.1 %all-gather.2.cloned.1.call-done = bf16[1024,5120]{1,0:T(8,128)(2,1)} async-done(((bf16[1024,1280]{1,0:T(8,128)(2,1)}), bf16[1024,5120]{1,0:T(8,128)(2,1)}) %all-gather.2.cloned.1.call-update) | async-done | bytes 10485776 | tf_op jit(solution)/shard_map/all_gather | solution.py:76
  206.1 29.7 %fusion.1 = bf16[1024,2048]{1,0:T(8,128)(2,1)} fusion(f32[1024,2048,1]{1,0,2:T(8,128)} %fusion.6, bf16[1024,5120]{1,0:T(8,128)(2,1)} %all-gather.2.cloned.1.call-done, bf16[2048,5120]{1,0:T(8,128)(2,1)} %param.12), kind=kOutput, calls=%fused_computation.3 | convolution fusion | flops 21481127936 | bytes 44040192 | tf_op jit(solution)/shard_map/dot_general | solution.py:105
  (27 shorter events, 1.7 us)
Async XLA Ops:
  7.2 3.6 %copy-start = (bf16[64,16,1280]{2,1,0:T(8,128)(2,1)S(1)}, bf16[64,16,1280]{2,1,0:T(8,128)(2,1)}, u32[]{:S(2)}) copy-start(bf16[64,16,1280]{2,1,0:T(8,128)(2,1)} %param.14) | copy-start | bytes 7864324
  7.2 198.9 %all-gather.2.cloned.1.call-start = ((), (), s32[]{:S(2)}) async-start(), calls=%async_computation | async-start | bytes 13107200 | tf_op jit(solution)/shard_map/all_gather | solution.py:76
  10.8 5.1 %copy-start.3 = (bf16[1024,2048]{1,0:T(8,128)(2,1)S(1)}, bf16[1024,2048]{1,0:T(8,128)(2,1)}, u32[]{:S(2)}) copy-start(bf16[1024,2048]{1,0:T(8,128)(2,1)} %param.8) | copy-start | bytes 12582916
  10.8 5.1 %copy-start.4 = (bf16[64,16,2048]{2,1,0:T(8,128)(2,1)S(1)}, bf16[64,16,2048]{2,1,0:T(8,128)(2,1)}, u32[]{:S(2)}) copy-start(bf16[64,16,2048]{2,1,0:T(8,128)(2,1)} %param.13) | copy-start | bytes 12582916
  20.7 23.6 %collective-permute-start.1 = (f32[32,1024]{1,0:T(8,128)S(1)}, f32[32,1024]{1,0:T(8,128)S(1)}, u32[]{:S(2)}, u32[]{:S(2)}) collective-permute-start(f32[32,1024]{1,0:T(8,128)S(1)} %pad_maximum_fusion), channel_id=1, source_target_pairs={{0,8},{4,12},{8,0},{12,4},{1,9},{5,13},{9,1},{13,5},{2,10},{6,14},... | collective-permute-start | bytes 393224 | tf_op jit(solution)/shard_map/ppermute | solution.py:36
  24.8 19.5 %collective-permute-start.2 = (f32[32,1024]{1,0:T(8,128)S(1)}, f32[32,1024]{1,0:T(8,128)S(1)}, u32[]{:S(2)}, u32[]{:S(2)}) collective-permute-start(f32[32,1024]{1,0:T(8,128)S(1)} %pad_maximum_fusion), channel_id=1, source_target_pairs={{0,12},{4,8},{8,4},{12,0},{1,13},{5,9},{9,5},{13,1},{2,14},{6,10},... | collective-permute-start | bytes 393224 | tf_op jit(solution)/shard_map/ppermute | solution.py:36
  26.1 18.2 %collective-permute-start = (f32[32,1024]{1,0:T(8,128)S(1)}, f32[32,1024]{1,0:T(8,128)S(1)}, u32[]{:S(2)}, u32[]{:S(2)}) collective-permute-start(f32[32,1024]{1,0:T(8,128)S(1)} %pad_maximum_fusion), channel_id=1, source_target_pairs={{0,4},{4,0},{8,12},{12,8},{1,5},{5,1},{9,13},{13,9},{2,6},{6,2},{1... | collective-permute-start | bytes 393224 | tf_op jit(solution)/shard_map/ppermute | solution.py:36
  49.3 1.7 copy-start.2
  49.6 13.7 %collective-permute-start.3 = (f32[512,2048]{1,0:T(8,128)S(1)}, f32[512,2048]{1,0:T(8,128)S(1)}, u32[]{:S(2)}, u32[]{:S(2)}) collective-permute-start(f32[512,2048]{1,0:T(8,128)S(1)} %slice.44), channel_id=1, source_target_pairs={{0,1},{1,0},{2,3},{3,2},{4,5},{5,4},{6,7},{7,6},{8,9},{9,8},{10,11... | collective-permute-start | bytes 12582920 | tf_op jit(solution)/shard_map/ppermute | solution.py:49
  54.1 6.4 %collective-permute-start.5 = (f32[512,1280]{1,0:T(8,128)S(1)}, f32[512,1280]{1,0:T(8,128)S(1)}, u32[]{:S(2)}, u32[]{:S(2)}) collective-permute-start(f32[512,1280]{1,0:T(8,128)S(1)} %slice.49), channel_id=1, source_target_pairs={{0,1},{1,0},{2,3},{3,2},{4,5},{5,4},{6,7},{7,6},{8,9},{9,8},{10,11... | collective-permute-start | bytes 7864328 | tf_op jit(solution)/shard_map/ppermute | solution.py:50
  61.2 31.7 %collective-permute-start.6 = (f32[256,1280]{1,0:T(8,128)S(1)}, f32[256,1280]{1,0:T(8,128)S(1)}, u32[]{:S(2)}, u32[]{:S(2)}) collective-permute-start(f32[256,1280]{1,0:T(8,128)S(1)} %slice.51), channel_id=1, source_target_pairs={{0,2},{1,3},{2,0},{3,1},{4,6},{5,7},{6,4},{7,5},{8,10},{9,11},{10,... | collective-permute-start | bytes 3932168 | tf_op jit(solution)/shard_map/ppermute | solution.py:50
  64.6 72.8 %collective-permute-start.4 = (f32[256,2048]{1,0:T(8,128)S(1)}, f32[256,2048]{1,0:T(8,128)S(1)}, u32[]{:S(2)}, u32[]{:S(2)}) collective-permute-start(f32[256,2048]{1,0:T(8,128)S(1)} %slice.46), channel_id=1, source_target_pairs={{0,2},{1,3},{2,0},{3,1},{4,6},{5,7},{6,4},{7,5},{8,10},{9,11},{10,... | collective-permute-start | bytes 6291464 | tf_op jit(solution)/shard_map/ppermute | solution.py:49
  206.1 29.7 %copy-start.1 = (bf16[64,16,1280]{2,1,0:T(8,128)(2,1)S(1)}, bf16[64,16,1280]{2,1,0:T(8,128)(2,1)}, u32[]{:S(2)}) copy-start(bf16[64,16,1280]{2,1,0:T(8,128)(2,1)} %param.14) | copy-start | bytes 7864324
Sparse Core Ops, SparseCore 0:
  9.6 196.4 all-gather.1

commit v2 on v1

--- a/solution.py
+++ b/solution.py
@@ -1,10 +1,21 @@
+import functools
+
 import jax
 import jax.numpy as jnp
 from jax import lax
+from jax.experimental import pallas as pl
+from jax.experimental.pallas import tpu as pltpu
 from jax.sharding import PartitionSpec as P
 
 ADAPTER_SCALE = 2.0
 OBJECTIVE_WEIGHT = 0.05
+
+TO_ENDS = [(1, 0), (2, 3)]
+MIDDLES = [(1, 2), (2, 1)]
+FLIP_X, FLIP_CORE = 2, 1
+LAST = (((1,), (1,)), ((), ()))
+FIRST = (((0,), (0,)), ((), ()))
+PLAIN = (((1,), (0,)), ((), ()))
 
 
 def pairs(size, distance):
@@ -53,7 +64,7 @@
     return term_a, term_b
 
 
-def per_device(
+def general_device(
     attention_output,
     projection_output_gradient,
     token_adapter_index,
@@ -109,6 +120,344 @@
     return attention_gradient, grad_a, grad_b
 
 
+def dot(a, b, dims):
+    return lax.dot_general(a, b, dims, preferred_element_type=jnp.float32)
+
+
+def kernel_call(body, **kwargs):
+    return pl.pallas_call(
+        body,
+        compiler_params=pltpu.CompilerParams(vmem_limit_bytes=56 << 20),
+        cost_estimate=pl.CostEstimate(flops=1 << 20, bytes_accessed=1 << 16, transcendentals=0),
+        **kwargs,
+    )
+
+
+def together(*arrays):
+    return lax.optimization_barrier(arrays)
+
+
+def whole(array):
+    return pl.BlockSpec(array.shape, lambda i, *_: (0,) * array.ndim)
+
+
+def low_rank_kernel(rank, _, index_ref, down_ref, values_ref, up_ref, gradient_ref, out_ref):
+    rows, tokens = down_ref.shape[0], values_ref.shape[0]
+    step = pl.program_id(0)
+
+    @pl.when(step == 0)
+    def _():
+        out_ref[...] = jnp.zeros_like(out_ref)
+
+    adapter = lax.broadcasted_iota(jnp.int32, (rows // rank, 1, tokens), 0) + step * (rows // rank)
+    chosen = adapter == index_ref[...][None]
+    for at, weight, values in ((0, down_ref, values_ref), (rank, up_ref, gradient_ref)):
+        terms = dot(weight[...], values[...], LAST).reshape(rows // rank, rank, tokens)
+        out_ref[at : at + rank] += jnp.sum(jnp.where(chosen, terms, 0.0), axis=0)
+
+
+def low_rank(after, index, down, values, up, gradient, rank):
+    tokens = values.shape[0]
+    rows = down.shape[0]
+    block = rows // 4
+    return kernel_call(
+        functools.partial(low_rank_kernel, rank),
+        grid=(4,),
+        in_specs=[
+            pl.BlockSpec(memory_space=pl.ANY),
+            whole(index),
+            pl.BlockSpec((block, down.shape[1]), lambda i: (i, 0)),
+            whole(values),
+            pl.BlockSpec((block, up.shape[1]), lambda i: (i, 0)),
+            whole(gradient),
+        ],
+        out_specs=pl.BlockSpec((2 * rank, tokens), lambda i: (0, 0)),
+        out_shape=jax.ShapeDtypeStruct((2 * rank, tokens), jnp.float32),
+    )(after, index, down, values, up, gradient)
+
+
+def spread_rows(labels, index, low):
+    wide = jnp.concatenate([low] * (labels.shape[0] // low.shape[0]), axis=0)
+    return jnp.where(labels == index, wide, 0.0).astype(jnp.bfloat16)
+
+
+def adapter_gradient_kernel(
+    slots_ref, index_ref, low0, low1, low2, low3, values_ref, gradient_ref, send_ref, keep_ref, low_ref
+):
+    step = pl.program_id(0)
+
+    @pl.when(step == 0)
+    def _():
+        low_ref[...] = (low0[...] + low1[...]) + (low2[...] + low3[...])
+
+    rank = low_ref.shape[0] // 2
+    low = low_ref[...].astype(jnp.bfloat16).astype(jnp.float32)
+    multiplier = ADAPTER_SCALE * OBJECTIVE_WEIGHT
+    a = multiplier * dot(
+        spread_rows(slots_ref[...], index_ref[...], low[rank:]), values_ref[...], PLAIN
+    )
+    b = multiplier * dot(
+        spread_rows(slots_ref[...], index_ref[...], low[:rank]), gradient_ref[...], PLAIN
+    )
+    split = a.shape[1]
+
+    @pl.when(step < 2)
+    def _():
+        send_ref[:, :split] = a
+        send_ref[:, split:] = b
+
+    @pl.when(step >= 2)
+    def _():
+        keep_ref[:, :split] = a
+        keep_ref[:, split:] = b
+
+
+def adapter_gradients(slots, index, low_terms, values, gradient):
+    rows = slots.shape[0]
+    block = rows // 4
+    width = values.shape[1] + gradient.shape[1]
+    half = jax.ShapeDtypeStruct((rows // 2, width), jnp.float32)
+    return kernel_call(
+        adapter_gradient_kernel,
+        grid=(4,),
+        in_specs=[
+            pl.BlockSpec((block, 1), lambda i: (i, 0)),
+            whole(index),
+            *(whole(term) for term in low_terms),
+            whole(values),
+            whole(gradient),
+        ],
+        out_specs=[
+            pl.BlockSpec((block, width), lambda i: (jnp.minimum(i, 1), 0)),
+            pl.BlockSpec((block, width), lambda i: (jnp.maximum(i - 2, 0), 0)),
+            whole(low_terms[0]),
+        ],
+        out_shape=[half, half, jax.ShapeDtypeStruct(low_terms[0].shape, jnp.float32)],
+    )(slots, index, *low_terms, values, gradient)
+
+
+def halves_kernel(keep_ref, got_ref, send_ref, out_ref):
+    total = keep_ref[...] + got_ref[...]
+
+    @pl.when(pl.program_id(0) < 2)
+    def _():
+        send_ref[...] = total.astype(send_ref.dtype)
+
+    @pl.when(pl.program_id(0) >= 2)
+    def _():
+        out_ref[...] = total
+
+
+def add_in_halves(keep, got):
+    rows, width = keep.shape
+    block = rows // 4
+    both = pl.BlockSpec((block, width), lambda i: (i, 0))
+    return kernel_call(
+        halves_kernel,
+        grid=(4,),
+        in_specs=[both, both],
+        out_specs=[
+            pl.BlockSpec((block, width), lambda i: (jnp.minimum(i, 1), 0)),
+            pl.BlockSpec((block, width), lambda i: (jnp.maximum(i - 2, 0), 0)),
+        ],
+        out_shape=[
+            jax.ShapeDtypeStruct((rows // 2, width), jnp.bfloat16),
+            jax.ShapeDtypeStruct((rows // 2, width), jnp.float32),
+        ],
+    )(keep, got)
+
+
+def owned_kernel(keep_ref, got_ref, a_ref, b_ref):
+    split = a_ref.shape[1]
+    a_ref[...] = keep_ref[:, :split] + got_ref[:, :split].astype(jnp.float32)
+    b_ref[...] = keep_ref[:, split:] + got_ref[:, split:].astype(jnp.float32)
+
+
+def owned_sums(keep, got, split):
+    rows, width = keep.shape
+    block = rows // 4
+    widths = (split, width - split)
+    return kernel_call(
+        owned_kernel,
+        grid=(4,),
+        in_specs=[pl.BlockSpec((block, width), lambda i: (i, 0))] * 2,
+        out_specs=[pl.BlockSpec((block, w), lambda i: (i, 0)) for w in widths],
+        out_shape=[jax.ShapeDtypeStruct((rows, w), jnp.float32) for w in widths],
+    )(keep, got)
+
+
+def rows_kernel(distances, with_adapters, here_ref, _, *refs):
+    start_count = 3 if with_adapters else 1
+    start_refs, refs = refs[:start_count], refs[start_count:]
+    arrays, (weight_ref, out_ref, *scratch) = refs[: len(distances)], refs[len(distances) :]
+    if with_adapters:
+        index_ref, low_ref, rows_ref = start_refs
+        (wide_ref,) = scratch
+
+        @pl.when(pl.program_id(0) == 0)
+        def _():
+            rank = low_ref.shape[0] // 2
+            labels = lax.broadcasted_iota(jnp.int32, wide_ref.shape[::-1], 0) // rank
+            low = low_ref[rank:].astype(jnp.bfloat16).astype(jnp.float32)
+            wide_ref[...] = spread_rows(labels, index_ref[...], low).T
+
+        total = ADAPTER_SCALE * dot(wide_ref[...], rows_ref[...], PLAIN)
+    else:
+        total = start_refs[0][...]
+    columns = arrays[0].shape[1]
+    blocks = {}
+    for distance, ref in zip(distances, arrays):
+        blocks[distance] = blocks[distance] + ref[...] if distance in blocks else ref[...]
+    for distance, block in blocks.items():
+        if weight_ref.shape[1] == columns:
+            total += dot(block, weight_ref[...], LAST)
+        else:
+            at = pl.multiple_of((here_ref[0] ^ distance) * columns, 128)
+            total += dot(block, weight_ref[:, pl.ds(at, columns)], LAST)
+    out_ref[...] = total.astype(out_ref.dtype)
+
+
+def add_products(here, before, start, blocks, weight, first, tokens):
+    step = blocks[0][1].shape[0]
+    features, width = weight.shape
+    block = 1024 if len(blocks) == 2 else 512
+    here_at = first // step
+    if before is None:
+        out, at = jax.ShapeDtypeStruct((step, features), jnp.float32), 0
+    else:
+        out, at = jax.ShapeDtypeStruct((tokens, features), jnp.bfloat16), here_at
+    distances, arrays = zip(*blocks)
+    if len(set(distances)) == 1:
+        weight_block = pl.BlockSpec(
+            (block, arrays[0].shape[1]), lambda i, here: (i, here[0] ^ distances[0])
+        )
+    else:
+        weight_block = pl.BlockSpec((block, width), lambda i, _: (i, 0))
+    with_adapters = isinstance(start, tuple)
+    if with_adapters:
+        index, low, rows = start
+        start_blocks = [
+            pl.BlockSpec((1, step), lambda i, _: (0, here_at)),
+            pl.BlockSpec((low.shape[0], step), lambda i, _: (0, here_at)),
+            pl.BlockSpec((rows.shape[0], block), lambda i, _: (0, i)),
+        ]
+        scratch = [pltpu.VMEM((step, rows.shape[0]), jnp.bfloat16)]
+    else:
+        start = (start,)
+        start_blocks = [pl.BlockSpec((step, block), lambda i, _: (0, i))]
+        scratch = []
+    return kernel_call(
+        functools.partial(rows_kernel, distances, with_adapters),
+        grid_spec=pltpu.PrefetchScalarGridSpec(
+            num_scalar_prefetch=1,
+            grid=(features // block,),
+            in_specs=[
+                pl.BlockSpec(memory_space=pl.ANY),
+                *start_blocks,
+                *(whole(b) for b in arrays),
+                weight_block,
+            ],
+            out_specs=pl.BlockSpec((step, block), lambda i, _: (at, i)),
+            scratch_shapes=scratch,
+        ),
+        out_shape=out,
+        input_output_aliases={} if before is None or before is here else {1: 0},
+    )(here, here if before is None else before, *start, *arrays, weight)
+
+
+def line_device(
+    attention_output,
+    projection_output_gradient,
+    token_adapter_index,
+    owner_slot_adapter,
+    output_projection_weight,
+    adapter_down_weight,
+    adapter_up_weight,
+):
+    adapters, rank, attention_columns = adapter_down_weight.shape
+    columns = adapter_up_weight.shape[2]
+    tokens = attention_output.shape[0]
+    here = lax.axis_index("tensor")[None]
+    down = adapter_down_weight.reshape(adapters * rank, attention_columns)
+    up = adapter_up_weight.reshape(adapters * rank, columns)
+    index = token_adapter_index[None, :]
+
+    step = tokens // 2
+    order = jnp.array([3, 1, 2, 0], jnp.int32) ^ lax.axis_index("dp")
+    slots = jnp.repeat(owner_slot_adapter.reshape(4, -1)[order].reshape(-1), rank)[:, None]
+    weight = output_projection_weight
+
+    def swap(block):
+        return lax.ppermute(block, "tensor", pairs(4, 1))
+
+    def cross(block):
+        return lax.ppermute(block, "tensor", MIDDLES)
+
+    def to_end(block):
+        return lax.ppermute(block, "tensor", TO_ENDS)
+
+    own = [projection_output_gradient[c * step : (c + 1) * step] for c in range(2)]
+    near, across, far, end_across, end_far = ({} for _ in range(5))
+
+    near[0], across[0], near[1] = swap(own[0]), cross(own[0]), swap(own[1])
+    low_part = low_rank(index, index, down, attention_output, up, projection_output_gradient, rank)
+    low_part, near[0], across[0] = together(low_part, near[0], across[0])
+    low_terms = [low_part] + [lax.ppermute(low_part, "tensor", pairs(4, d)) for d in (1, 2, 3)]
+    far[0] = cross(near[0])
+    near[1], far[0], across[0], own[1], *low_terms = together(
+        near[1], far[0], across[0], own[1], *low_terms
+    )
+    across[1], end_across[0] = cross(own[1]), to_end(across[0])
+    end_far[0], far[1] = to_end(far[0]), cross(near[1])
+    send, keep, low = adapter_gradients(
+        slots, index, low_terms, attention_output, projection_output_gradient
+    )
+    send, keep, end_across[0], across[1] = together(send, keep, end_across[0], across[1])
+    got = lax.ppermute(send, "dp", pairs(4, FLIP_CORE))
+    end_across[1] = to_end(across[1])
+    to_x, keep = add_in_halves(keep, got)
+    to_x, keep, end_far[0], far[1], index = together(to_x, keep, end_far[0], far[1], index)
+    got = lax.ppermute(to_x, "dp", pairs(4, FLIP_X))
+    end_far[1] = to_end(far[1])
+    result = add_products(
+        here,
+        here,
+        (index, low, down),
+        ((0, own[0]), (1, near[0]), (2, far[0]), (2, end_across[0]), (3, across[0]), (3, end_far[0])),
+        weight,
+        0,
+        tokens,
+    )
+    result, end_across[1], index, got = together(result, end_across[1], index, got)
+    grad_a, grad_b = owned_sums(keep, got, attention_columns)
+    base = add_products(
+        here,
+        None,
+        (index, low, down),
+        ((0, own[1]), (1, near[1]), (2, far[1]), (2, end_across[1])),
+        weight,
+        step,
+        tokens,
+    )
+    grad_a, grad_b, base, end_far[1], result = together(grad_a, grad_b, base, end_far[1], result)
+    result = add_products(
+        here, result, base, ((3, across[1]), (3, end_far[1])), weight, step, tokens
+    )
+    grad_a = grad_a.reshape(-1, rank, attention_columns)
+    grad_b = grad_b.reshape(-1, rank, columns)
+    return result, grad_a, grad_b
+
+
+def per_device(*arrays):
+    sizes = tuple(lax.axis_size(a) for a in ("parts", "tensor", "dp"))
+    tokens, attention_columns = arrays[0].shape
+    columns = arrays[1].shape[1]
+    fits = tokens % 1024 == 0 and attention_columns % 2048 == 0 and columns % 128 == 0
+    if sizes == (2, 4, 4) and fits:
+        return line_device(*arrays)
+    return general_device(*arrays)
+
+
 def solution(mesh):
     placed = (
         P(("parts", "dp"), "tensor"),

time: 243 us -> 219 us (0.901)
  Pallas kernels: 0 us -> 85 us
  waiting for transfers between devices: 156 us -> 96.1 us
  matrix products: 54.1 us -> 0 us
  starting transfers between devices: 8.07 us -> 28.7 us
  between operations: 14.2 us -> 0.75 us
  other arithmetic: 6.33 us -> 0.01 us
  local copies, waits for them, and re-layouts: 3.5 us -> 7.8 us
    pallas_call x0 -> x7, Pallas kernels: none -> 85 us  [the longest x3 45.2 us: add_products(): kernel_call(functools.partial(rows_kernel, distances, with_adapters), gri...]
    all_gather x1 -> x0, waiting for transfers between devices: 67.1 us -> none  [per_device(): lax.all_gather(projection_output_gradient, 'tensor', axis=1, tiled=True)]
    dot_general x6 -> x0, matrix products: 54.1 us -> none  [the longest x1 29.7 us: per_device(): lax.dot_general(full_gradient, output_projection_weight, row_dims, prefer...]
    ppermute x7 -> x15, starting transfers between devices: 8.03 us -> 28.7 us  [the longest x3 9.43 us: line_device(): lax.ppermute(low_part, 'tensor', pairs(4, d))]
    ppermute x7 -> x15, waiting for transfers between devices: 88.7 us -> 96.1 us  [the longest x4 39.5 us: to_end(): return lax.ppermute(block, 'tensor', TO_ENDS)]
    add x4 -> x0, other arithmetic: 4.45 us -> none  [the longest x2 2.72 us: reduce_to_owner(): term_a = term_a[half:] + got_a]
    unnamed x10 -> x24, local copies, waits for them, and re-layouts: 1.4 us -> 4.02 us
  transfers between devices with their start and end apart: 8 -> 15, of which waited for: 5 -> 10; matrix products, arithmetic and copies ran while one was open for 14% -> 1% of each run, Pallas kernels for 0% -> 36%
where the time goes in v2:
time: 219 us; the launch traced here: 218 us
  waiting for transfers between devices  96.1 us (44%)
  Pallas kernels  85 us (39%)
  starting transfers between devices  28.7 us (13%)
  local copies, waits for them, and re-layouts  7.8 us (4%)
    pallas_call x3, Pallas kernels, add_products(): kernel_call(functools.partial(rows_kernel, distances, with_adapters), gri...  45.2 us
    ppermute x4, waiting for transfers between devices, to_end(): return lax.ppermute(block, 'tensor', TO_ENDS)  39.5 us
    ppermute x2, waiting for transfers between devices, swap(): return lax.ppermute(block, 'tensor', pairs(4, 1))  30.3 us
    ppermute x3, waiting for transfers between devices, line_device(): lax.ppermute(low_part, 'tensor', pairs(4, d))  16.6 us
    pallas_call x1, Pallas kernels, adapter_gradients(): kernel_call(adapter_gradient_kernel, grid=(4,), in_specs=[pl.BlockSpec((b...  15.6 us
    pallas_call x1, Pallas kernels, low_rank(): kernel_call(functools.partial(low_rank_kernel, rank), grid=(4,), in_specs...  12.2 us
    ppermute x3, starting transfers between devices, line_device(): lax.ppermute(low_part, 'tensor', pairs(4, d))  9.43 us
    ppermute x1, waiting for transfers between devices, line_device(): got = lax.ppermute(send, 'dp', pairs(4, FLIP_CORE))  8.03 us
  transfers between devices with their start and end apart: 15, of which 10 were waited for; matrix products, arithmetic and copies ran while one was open for 1% of the time, Pallas kernels for 36%

profile of v2, /device:TPU:0, one launch (start us, length us, event | category | flops | bytes accessed | tf_op | source)
XLA Modules:
  0.0 218.4 jit_solution(10571754210105438995)
XLA Ops:
  0.6 1.9 fusion
  2.5 3.1 %collective-permute-start.1 = (bf16[512,1280]{1,0:T(8,128)(2,1)S(1)}, bf16[512,1280]{1,0:T(8,128)(2,1)S(1)}, u32[]{:S(2)}, u32[]{:S(2)}) collective-permute-start(bf16[512,1280]{1,0:T(8,128)(2,1)S(1)} %get-tuple-element.75.refs_3_), channel_id=1, source_target_pairs={{0,4},{4,0},{8,12},{12,8},{1,5},{5,1},{9,13},{13,9},{2,6},{6,2},{1... | collective-permute-start | bytes 3932168 | tf_op jit(solution)/shard_map/ppermute | solution.py:391
  5.6 1.8 collective-permute-start.2
  7.4 3.3 %collective-permute-start = (bf16[512,1280]{1,0:T(8,128)(2,1)S(1)}, bf16[512,1280]{1,0:T(8,128)(2,1)}, u32[]{:S(2)}, u32[]{:S(2)}) collective-permute-start(bf16[512,1280]{1,0:T(8,128)(2,1)S(1)} %get-tuple-element.49.refs_3_), channel_id=1, source_target_pairs={{0,4},{4,0},{8,12},{12,8},{1,5},{5,1},{9,13},{13,9},{2,6},{6,2},{1... | collective-permute-start | bytes 3932168 | tf_op jit(solution)/shard_map/ppermute | solution.py:391
  10.8 12.2 %shard_map.103.low0 = f32[32,1024]{1,0:T(8,128)} custom-call(s32[1,1024]{1,0:T(1,128)} %bitcast.10, s32[1,1024]{1,0:T(1,128)} %bitcast.11, bf16[1024,2048]{1,0:T(8,128)(2,1)} %bitcast.6, bf16[1024,2048]{1,0:T(8,128)(2,1)} %values_ref.3, bf16[1024,1280]{1,0:T(8,128)(2,1)} %bitcast.9, bf16[1024,1280]{1,0:T(8,128)(2,1)} %gradient_ref.3), custom_call_target="tpu_custom_call" | custom-call | flops 1048576 | bytes 65536 | tf_op jit(solution)/shard_map/pallas_call | solution.py:163
  22.9 12.3 %collective-permute-done.1.refs_4_ = bf16[512,1280]{1,0:T(8,128)(2,1)S(1)} collective-permute-done((bf16[512,1280]{1,0:T(8,128)(2,1)S(1)}, bf16[512,1280]{1,0:T(8,128)(2,1)S(1)}, u32[]{:S(2)}, u32[]{:S(2)}) %collective-permute-start.1) | collective-permute-done | bytes 1310752 | tf_op jit(solution)/shard_map/ppermute | solution.py:391
  36.0 7.0 %collective-permute-start.4 = (f32[32,1024]{1,0:T(8,128)}, f32[32,1024]{1,0:T(8,128)S(1)}, u32[]{:S(2)}, u32[]{:S(2)}) collective-permute-start(f32[32,1024]{1,0:T(8,128)} %shard_map.103.low0), channel_id=1, source_target_pairs={{0,4},{4,0},{8,12},{12,8},{1,5},{5,1},{9,13},{13,9},{2,6},{6,2},{1... | collective-permute-start | bytes 393224 | tf_op jit(solution)/shard_map/ppermute | solution.py:405
  43.0 2.4 %collective-permute-start.6 = (f32[32,1024]{1,0:T(8,128)}, f32[32,1024]{1,0:T(8,128)S(1)}, u32[]{:S(2)}, u32[]{:S(2)}) collective-permute-start(f32[32,1024]{1,0:T(8,128)} %shard_map.103.low0), channel_id=1, source_target_pairs={{0,12},{4,8},{8,4},{12,0},{1,13},{5,9},{9,5},{13,1},{2,14},{6,10},... | collective-permute-start | bytes 393224 | tf_op jit(solution)/shard_map/ppermute | solution.py:405
  45.4 18.0 %collective-permute-done.refs_4_ = bf16[512,1280]{1,0:T(8,128)(2,1)} collective-permute-done((bf16[512,1280]{1,0:T(8,128)(2,1)S(1)}, bf16[512,1280]{1,0:T(8,128)(2,1)}, u32[]{:S(2)}, u32[]{:S(2)}) %collective-permute-start) | collective-permute-done | bytes 1310752 | tf_op jit(solution)/shard_map/ppermute | solution.py:391
  63.4 2.4 %collective-permute-done.4.low1 = f32[32,1024]{1,0:T(8,128)S(1)} collective-permute-done((f32[32,1024]{1,0:T(8,128)}, f32[32,1024]{1,0:T(8,128)S(1)}, u32[]{:S(2)}, u32[]{:S(2)}) %collective-permute-start.4) | collective-permute-done | bytes 131104 | tf_op jit(solution)/shard_map/ppermute | solution.py:405
  65.8 14.3 %collective-permute-done.5.low2 = f32[32,1024]{1,0:T(8,128)S(1)} collective-permute-done((f32[32,1024]{1,0:T(8,128)}, f32[32,1024]{1,0:T(8,128)S(1)}, u32[]{:S(2)}, u32[]{:S(2)}) %collective-permute-start.5) | collective-permute-done | bytes 131104 | tf_op jit(solution)/shard_map/ppermute | solution.py:405
  85.1 15.6 %shard_map.104 = (f32[512,3328]{1,0:T(8,128)}, f32[512,3328]{1,0:T(8,128)}, f32[32,1024]{1,0:T(8,128)}) custom-call(s32[1024,1]{1,0:T(8,128)} %broadcast_in_dim_reshape.4.slots_ref, s32[1,1024]{1,0:T(1,128)} %bitcast.12, f32[32,1024]{1,0:T(8,128)} %shard_map.103.low0, f32[32,1024]{1,0:T(8,128)} %copy-done.7, f32[32,1024]{1,0:T(8,128)} %copy-done.8, ...), custom_call_target="tpu_custom_call" | custom-call | flops 1048576 | bytes 65536 | tf_op jit(solution)/shard_map/pallas_call | solution.py:220
  100.7 9.6 %collective-permute-done.7.refs_6_ = bf16[512,1280]{1,0:T(8,128)(2,1)} collective-permute-done((bf16[512,1280]{1,0:T(8,128)(2,1)}, bf16[512,1280]{1,0:T(8,128)(2,1)}, u32[]{:S(2)}, u32[]{:S(2)}) %collective-permute-start.7) | collective-permute-done | bytes 1310752 | tf_op jit(solution)/shard_map/ppermute | solution.py:397
  111.6 1.8 collective-permute-start.11
  113.4 8.0 %collective-permute-done.9.got_ref = f32[512,3328]{1,0:T(8,128)S(1)} collective-permute-done((f32[512,3328]{1,0:T(8,128)}, f32[512,3328]{1,0:T(8,128)S(1)}, u32[]{:S(2)}, u32[]{:S(2)}) %collective-permute-start.9) | collective-permute-done | bytes 6815776 | tf_op jit(solution)/shard_map/ppermute | solution.py:416
  121.4 2.9 %copy-done = f32[512,3328]{1,0:T(8,128)} copy-done((f32[512,3328]{1,0:T(8,128)}, f32[512,3328]{1,0:T(8,128)S(1)}, u32[]{:S(2)}) %copy-start) | copy-done | bytes 6815768
  124.3 7.4 %shard_map.105 = (bf16[256,3328]{1,0:T(8,128)(2,1)}, f32[256,3328]{1,0:T(8,128)}) custom-call(f32[512,3328]{1,0:T(8,128)} %get-tuple-element.50.keep_ref, f32[512,3328]{1,0:T(8,128)} %copy-done), custom_call_target="tpu_custom_call" | custom-call | flops 1048576 | bytes 65536 | tf_op jit(solution)/shard_map/pallas_call | solution.py:255
  131.7 14.0 %collective-permute-done.10.refs_8_ = bf16[512,1280]{1,0:T(8,128)(2,1)} collective-permute-done((bf16[512,1280]{1,0:T(8,128)(2,1)S(1)}, bf16[512,1280]{1,0:T(8,128)(2,1)}, u32[]{:S(2)}, u32[]{:S(2)}) %collective-permute-start.10) | collective-permute-done | bytes 1310752 | tf_op jit(solution)/shard_map/ppermute | solution.py:397
  149.9 20.1 %shard_map.106._ = bf16[1024,2048]{1,0:T(8,128)(2,1)} custom-call(s32[1]{0:T(128)} %bitcast.here_ref._, s32[1]{0:T(128)} %bitcast.here_ref._, s32[1,1024]{1,0:T(1,128)} %bitcast.13, f32[32,1024]{1,0:T(8,128)} %get-tuple-element.58.refs_1_, bf16[1024,2048]{1,0:T(8,128)(2,1)} %bitcast.7, bf16[512,1280]{1,0:T(8,128)(2,1)} %copy-done.1, ...), custom_call_target="tpu_custom_call" | custom-call | flops 1048576 | bytes 65536 | tf_op jit(solution)/shard_map/pallas_call | solution.py:349
  170.0 13.3 %collective-permute-done.12.refs_6_ = bf16[512,1280]{1,0:T(8,128)(2,1)} collective-permute-done((bf16[512,1280]{1,0:T(8,128)(2,1)}, bf16[512,1280]{1,0:T(8,128)(2,1)}, u32[]{:S(2)}, u32[]{:S(2)}) %collective-permute-start.12) | collective-permute-done | bytes 1310752 | tf_op jit(solution)/shard_map/ppermute | solution.py:397
  184.9 17.9 %shard_map.108.refs_0_ = f32[512,2048]{1,0:T(8,128)} custom-call(s32[1]{0:T(128)} %bitcast.here_ref._, s32[1]{0:T(128)} %bitcast.here_ref._, s32[1,1024]{1,0:T(1,128)} %bitcast.14, f32[32,1024]{1,0:T(8,128)} %get-tuple-element.58.refs_1_, bf16[1024,2048]{1,0:T(8,128)(2,1)} %bitcast.8, bf16[512,1280]{1,0:T(8,128)(2,1)} %copy-done.2, ...), custom_call_target="tpu_custom_call" | custom-call | flops 1048576 | bytes 65536 | tf_op jit(solution)/shard_map/pallas_call | solution.py:349
  202.8 4.6 %shard_map.107 = (f32[256,2048]{1,0:T(8,128)}, f32[256,1280]{1,0:T(8,128)}) custom-call(f32[256,3328]{1,0:T(8,128)} %get-tuple-element.56.keep_ref, bf16[256,3328]{1,0:T(8,128)(2,1)} %copy-done.3), custom_call_target="tpu_custom_call" | custom-call | flops 1048576 | bytes 65536 | tf_op jit(solution)/shard_map/pallas_call | solution.py:280
  207.4 2.6 %collective-permute-done.14.refs_2_ = bf16[512,1280]{1,0:T(8,128)(2,1)S(1)} collective-permute-done((bf16[512,1280]{1,0:T(8,128)(2,1)}, bf16[512,1280]{1,0:T(8,128)(2,1)S(1)}, u32[]{:S(2)}, u32[]{:S(2)}) %collective-permute-start.14) | collective-permute-done | bytes 1310752 | tf_op jit(solution)/shard_map/ppermute | solution.py:397
  211.1 7.3 %shard_map.109 = bf16[1024,2048]{1,0:T(8,128)(2,1)} custom-call(s32[1]{0:T(128)} %bitcast.here_ref._, bf16[1024,2048]{1,0:T(8,128)(2,1)} %shard_map.106._, f32[512,2048]{1,0:T(8,128)} %shard_map.108.refs_0_, bf16[512,1280]{1,0:T(8,128)(2,1)} %collective-permute-done.8.refs_1_, bf16[512,1280]{1,0:T(8,128)(2,1)} %copy-done.6, ...), custom_call_target="tpu_custom_call", output_to_operand_aliasing={{}: (1, {})} | custom-call | flops 1048576 | bytes 65536 | tf_op jit(solution)/shard_map/pallas_call | solution.py:349
  (45 shorter events, 14.0 us)
Async XLA Ops:
  2.5 20.4 %copy-start.1 = (bf16[512,1280]{1,0:T(8,128)(2,1)}, bf16[512,1280]{1,0:T(8,128)(2,1)S(1)}, u32[]{:S(2)}) copy-start(bf16[512,1280]{1,0:T(8,128)(2,1)S(1)} %get-tuple-element.75.refs_3_) | copy-start | bytes 3932164
  2.5 78.9 %copy-start.2 = (bf16[512,1280]{1,0:T(8,128)(2,1)}, bf16[512,1280]{1,0:T(8,128)(2,1)S(1)}, u32[]{:S(2)}) copy-start(bf16[512,1280]{1,0:T(8,128)(2,1)S(1)} %get-tuple-element.49.refs_3_) | copy-start | bytes 3932164
  2.5 32.7 %collective-permute-start.1 = (bf16[512,1280]{1,0:T(8,128)(2,1)S(1)}, bf16[512,1280]{1,0:T(8,128)(2,1)S(1)}, u32[]{:S(2)}, u32[]{:S(2)}) collective-permute-start(bf16[512,1280]{1,0:T(8,128)(2,1)S(1)} %get-tuple-element.75.refs_3_), channel_id=1, source_target_pairs={{0,4},{4,0},{8,12},{12,8},{1,5},{5,1},{9,13},{13,9},{2,6},{6,2},{1... | collective-permute-start | bytes 3932168 | tf_op jit(solution)/shard_map/ppermute | solution.py:391
  5.6 29.6 %collective-permute-start.2 = (bf16[512,1280]{1,0:T(8,128)(2,1)S(1)}, bf16[512,1280]{1,0:T(8,128)(2,1)}, u32[]{:S(2)}, u32[]{:S(2)}) collective-permute-start(bf16[512,1280]{1,0:T(8,128)(2,1)S(1)} %get-tuple-element.75.refs_3_), channel_id=1, source_target_pairs={{4,8},{8,4},{5,9},{9,5},{6,10},{10,6},{7,11},{11,7},{20,24},{24,20... | collective-permute-start | bytes 3932168 | tf_op jit(solution)/shard_map/ppermute | solution.py:394
  7.4 56.0 %collective-permute-start = (bf16[512,1280]{1,0:T(8,128)(2,1)S(1)}, bf16[512,1280]{1,0:T(8,128)(2,1)}, u32[]{:S(2)}, u32[]{:S(2)}) collective-permute-start(bf16[512,1280]{1,0:T(8,128)(2,1)S(1)} %get-tuple-element.49.refs_3_), channel_id=1, source_target_pairs={{0,4},{4,0},{8,12},{12,8},{1,5},{5,1},{9,13},{13,9},{2,6},{6,2},{1... | collective-permute-start | bytes 3932168 | tf_op jit(solution)/shard_map/ppermute | solution.py:391
  10.8 72.4 %copy-start.10 = (s32[64]{0:T(128)S(1)}, s32[64]{0:T(128)}, u32[]{:S(2)}) copy-start(s32[64]{0:T(128)} %param.11) | copy-start | bytes 772
  10.8 72.5 %copy-start.11 = (s32[4]{0:T(128)S(1)}, s32[4]{0:T(128)}, u32[]{:S(2)}) copy-start(s32[4]{0:T(128)} %constant.13.clone) | copy-start | bytes 52
  35.2 47.9 %copy-start.4 = (bf16[512,1280]{1,0:T(8,128)(2,1)}, bf16[512,1280]{1,0:T(8,128)(2,1)S(1)}, u32[]{:S(2)}) copy-start(bf16[512,1280]{1,0:T(8,128)(2,1)S(1)} %collective-permute-done.1.refs_4_) | copy-start | bytes 3932164
  35.2 44.8 %collective-permute-start.3 = (bf16[512,1280]{1,0:T(8,128)(2,1)S(1)}, bf16[512,1280]{1,0:T(8,128)(2,1)S(1)}, u32[]{:S(2)}, u32[]{:S(2)}) collective-permute-start(bf16[512,1280]{1,0:T(8,128)(2,1)S(1)} %collective-permute-done.1.refs_4_), channel_id=1, source_target_pairs={{4,8},{8,4},{5,9},{9,5},{6,10},{10,6},{7,11},{11,7},{20,24},{24,20... | collective-permute-start | bytes 3932168 | tf_op jit(solution)/shard_map/ppermute | solution.py:394
  36.0 29.8 %collective-permute-start.4 = (f32[32,1024]{1,0:T(8,128)}, f32[32,1024]{1,0:T(8,128)S(1)}, u32[]{:S(2)}, u32[]{:S(2)}) collective-permute-start(f32[32,1024]{1,0:T(8,128)} %shard_map.103.low0), channel_id=1, source_target_pairs={{0,4},{4,0},{8,12},{12,8},{1,5},{5,1},{9,13},{13,9},{2,6},{6,2},{1... | collective-permute-start | bytes 393224 | tf_op jit(solution)/shard_map/ppermute | solution.py:405
  43.0 37.1 %collective-permute-start.5 = (f32[32,1024]{1,0:T(8,128)}, f32[32,1024]{1,0:T(8,128)S(1)}, u32[]{:S(2)}, u32[]{:S(2)}) collective-permute-start(f32[32,1024]{1,0:T(8,128)} %shard_map.103.low0), channel_id=1, source_target_pairs={{0,8},{4,12},{8,0},{12,4},{1,9},{5,13},{9,1},{13,5},{2,10},{6,14},... | collective-permute-start | bytes 393224 | tf_op jit(solution)/shard_map/ppermute | solution.py:405
  43.0 37.1 %collective-permute-start.6 = (f32[32,1024]{1,0:T(8,128)}, f32[32,1024]{1,0:T(8,128)S(1)}, u32[]{:S(2)}, u32[]{:S(2)}) collective-permute-start(f32[32,1024]{1,0:T(8,128)} %shard_map.103.low0), channel_id=1, source_target_pairs={{0,12},{4,8},{8,4},{12,0},{1,13},{5,9},{9,5},{13,1},{2,14},{6,10},... | collective-permute-start | bytes 393224 | tf_op jit(solution)/shard_map/ppermute | solution.py:405
  65.8 19.2 %copy-start.7 = (f32[32,1024]{1,0:T(8,128)}, f32[32,1024]{1,0:T(8,128)S(1)}, u32[]{:S(2)}) copy-start(f32[32,1024]{1,0:T(8,128)S(1)} %collective-permute-done.4.low1) | copy-start | bytes 393220
  80.1 5.0 %copy-start.8 = (f32[32,1024]{1,0:T(8,128)}, f32[32,1024]{1,0:T(8,128)S(1)}, u32[]{:S(2)}) copy-start(f32[32,1024]{1,0:T(8,128)S(1)} %collective-permute-done.5.low2) | copy-start | bytes 393220
  80.1 30.2 %copy-start.5 = (bf16[512,1280]{1,0:T(8,128)(2,1)}, bf16[512,1280]{1,0:T(8,128)(2,1)S(1)}, u32[]{:S(2)}) copy-start(bf16[512,1280]{1,0:T(8,128)(2,1)S(1)} %collective-permute-done.3.refs_5_) | copy-start | bytes 3932164
  80.1 30.2 %collective-permute-start.7 = (bf16[512,1280]{1,0:T(8,128)(2,1)}, bf16[512,1280]{1,0:T(8,128)(2,1)}, u32[]{:S(2)}, u32[]{:S(2)}) collective-permute-start(bf16[512,1280]{1,0:T(8,128)(2,1)} %collective-permute-done.2.refs_7_), channel_id=1, source_target_pairs={{4,0},{8,12},{5,1},{9,13},{6,2},{10,14},{7,3},{11,15},{20,16},{24,... | collective-permute-start | bytes 3932168 | tf_op jit(solution)/shard_map/ppermute | solution.py:397
  81.4 28.9 %collective-permute-start.8 = (bf16[512,1280]{1,0:T(8,128)(2,1)S(1)}, bf16[512,1280]{1,0:T(8,128)(2,1)}, u32[]{:S(2)}, u32[]{:S(2)}) collective-permute-start(bf16[512,1280]{1,0:T(8,128)(2,1)S(1)} %get-tuple-element.49.refs_3_), channel_id=1, source_target_pairs={{4,8},{8,4},{5,9},{9,5},{6,10},{10,6},{7,11},{11,7},{20,24},{24,20... | collective-permute-start | bytes 3932168 | tf_op jit(solution)/shard_map/ppermute | solution.py:394
  110.3 11.1 %collective-permute-start.9 = (f32[512,3328]{1,0:T(8,128)}, f32[512,3328]{1,0:T(8,128)S(1)}, u32[]{:S(2)}, u32[]{:S(2)}) collective-permute-start(f32[512,3328]{1,0:T(8,128)} %get-tuple-element.51), channel_id=1, source_target_pairs={{0,1},{1,0},{2,3},{3,2},{4,5},{5,4},{6,7},{7,6},{8,9},{9,8},{10,11... | collective-permute-start | bytes 20447240 | tf_op jit(solution)/shard_map/ppermute | solution.py:416
  110.3 35.3 %collective-permute-start.10 = (bf16[512,1280]{1,0:T(8,128)(2,1)S(1)}, bf16[512,1280]{1,0:T(8,128)(2,1)}, u32[]{:S(2)}, u32[]{:S(2)}) collective-permute-start(bf16[512,1280]{1,0:T(8,128)(2,1)S(1)} %collective-permute-done.3.refs_5_), channel_id=1, source_target_pairs={{4,0},{8,12},{5,1},{9,13},{6,2},{10,14},{7,3},{11,15},{20,16},{24,... | collective-permute-start | bytes 3932168 | tf_op jit(solution)/shard_map/ppermute | solution.py:397
  111.6 34.0 %collective-permute-start.11 = (bf16[512,1280]{1,0:T(8,128)(2,1)}, bf16[512,1280]{1,0:T(8,128)(2,1)}, u32[]{:S(2)}, u32[]{:S(2)}) collective-permute-start(bf16[512,1280]{1,0:T(8,128)(2,1)} %collective-permute-done.refs_4_), channel_id=1, source_target_pairs={{4,8},{8,4},{5,9},{9,5},{6,10},{10,6},{7,11},{11,7},{20,24},{24,20... | collective-permute-start | bytes 3932168 | tf_op jit(solution)/shard_map/ppermute | solution.py:394
  145.6 39.2 %collective-permute-start.13 = (bf16[256,3328]{1,0:T(8,128)(2,1)}, bf16[256,3328]{1,0:T(8,128)(2,1)S(1)}, u32[]{:S(2)}, u32[]{:S(2)}) collective-permute-start(bf16[256,3328]{1,0:T(8,128)(2,1)} %get-tuple-element.62), channel_id=1, source_target_pairs={{0,2},{1,3},{2,0},{3,1},{4,6},{5,7},{6,4},{7,5},{8,10},{9,11},{10,... | collective-permute-start | bytes 5111816 | tf_op jit(solution)/shard_map/ppermute | solution.py:420
  147.1 36.2 %collective-permute-start.12 = (bf16[512,1280]{1,0:T(8,128)(2,1)}, bf16[512,1280]{1,0:T(8,128)(2,1)}, u32[]{:S(2)}, u32[]{:S(2)}) collective-permute-start(bf16[512,1280]{1,0:T(8,128)(2,1)} %collective-permute-done.8.refs_1_), channel_id=1, source_target_pairs={{4,0},{8,12},{5,1},{9,13},{6,2},{10,14},{7,3},{11,15},{20,16},{24,... | collective-permute-start | bytes 3932168 | tf_op jit(solution)/shard_map/ppermute | solution.py:397
  148.4 61.6 %collective-permute-start.14 = (bf16[512,1280]{1,0:T(8,128)(2,1)}, bf16[512,1280]{1,0:T(8,128)(2,1)S(1)}, u32[]{:S(2)}, u32[]{:S(2)}) collective-permute-start(bf16[512,1280]{1,0:T(8,128)(2,1)} %collective-permute-done.11.refs_5_), channel_id=1, source_target_pairs={{4,0},{8,12},{5,1},{9,13},{6,2},{10,14},{7,3},{11,15},{20,16},{24,... | collective-permute-start | bytes 3932168 | tf_op jit(solution)/shard_map/ppermute | solution.py:397
  184.9 17.9 %copy-start.3 = (bf16[256,3328]{1,0:T(8,128)(2,1)}, bf16[256,3328]{1,0:T(8,128)(2,1)S(1)}, u32[]{:S(2)}) copy-start(bf16[256,3328]{1,0:T(8,128)(2,1)S(1)} %collective-permute-done.13.got_ref) | copy-start | bytes 5111812
  (3 other events, 9.0 us)

commit v3 on v2

--- a/solution.py
+++ b/solution.py
@@ -9,6 +9,8 @@
 
 ADAPTER_SCALE = 2.0
 OBJECTIVE_WEIGHT = 0.05
+LAST_ROWS = 256
+FIRST_EIGHTHS = 3
 
 TO_ENDS = [(1, 0), (2, 3)]
 MIDDLES = [(1, 2), (2, 1)]
@@ -127,7 +129,7 @@
 def kernel_call(body, **kwargs):
     return pl.pallas_call(
         body,
-        compiler_params=pltpu.CompilerParams(vmem_limit_bytes=56 << 20),
+        compiler_params=pltpu.CompilerParams(vmem_limit_bytes=62 << 20),
         cost_estimate=pl.CostEstimate(flops=1 << 20, bytes_accessed=1 << 16, transcendentals=0),
         **kwargs,
     )
@@ -286,7 +288,8 @@
     )(keep, got)
 
 
-def rows_kernel(distances, with_adapters, here_ref, _, *refs):
+def rows_kernel(distances, first, here_ref, _, *refs):
+    with_adapters = first is not None
     start_count = 3 if with_adapters else 1
     start_refs, refs = refs[:start_count], refs[start_count:]
     arrays, (weight_ref, out_ref, *scratch) = refs[: len(distances)], refs[len(distances) :]
@@ -298,8 +301,9 @@
         def _():
             rank = low_ref.shape[0] // 2
             labels = lax.broadcasted_iota(jnp.int32, wide_ref.shape[::-1], 0) // rank
-            low = low_ref[rank:].astype(jnp.bfloat16).astype(jnp.float32)
-            wide_ref[...] = spread_rows(labels, index_ref[...], low).T
+            here_tokens = pl.ds(first, wide_ref.shape[0])
+            low = low_ref[rank:, here_tokens].astype(jnp.bfloat16).astype(jnp.float32)
+            wide_ref[...] = spread_rows(labels, index_ref[:, here_tokens], low).T
 
         total = ADAPTER_SCALE * dot(wide_ref[...], rows_ref[...], PLAIN)
     else:
@@ -317,15 +321,21 @@
     out_ref[...] = total.astype(out_ref.dtype)
 
 
-def add_products(here, before, start, blocks, weight, first, tokens):
-    step = blocks[0][1].shape[0]
+def add_products(here, before, start, blocks, weight, first, tokens, skip=0):
+    step = blocks[-1][1].shape[0]
     features, width = weight.shape
     block = 1024 if len(blocks) == 2 else 512
-    here_at = first // step
     if before is None:
-        out, at = jax.ShapeDtypeStruct((step, features), jnp.float32), 0
+        out = jax.ShapeDtypeStruct((step, features), jnp.float32)
+        out_block = pl.BlockSpec((step, block), lambda i, _: (0, i))
+    elif first == 0:
+        out = jax.ShapeDtypeStruct((tokens, features), jnp.bfloat16)
+        out_block = pl.BlockSpec((step, block), lambda i, _: (0, i))
     else:
-        out, at = jax.ShapeDtypeStruct((tokens, features), jnp.bfloat16), here_at
+        out = jax.ShapeDtypeStruct((tokens, features), jnp.bfloat16)
+        out_block = pl.BlockSpec(
+            (pl.Element(step), pl.Element(block)), lambda i, _: (first, i * block)
+        )
     distances, arrays = zip(*blocks)
     if len(set(distances)) == 1:
         weight_block = pl.BlockSpec(
@@ -337,27 +347,35 @@
     if with_adapters:
         index, low, rows = start
         start_blocks = [
-            pl.BlockSpec((1, step), lambda i, _: (0, here_at)),
-            pl.BlockSpec((low.shape[0], step), lambda i, _: (0, here_at)),
+            whole(index),
+            whole(low),
             pl.BlockSpec((rows.shape[0], block), lambda i, _: (0, i)),
         ]
         scratch = [pltpu.VMEM((step, rows.shape[0]), jnp.bfloat16)]
     else:
         start = (start,)
-        start_blocks = [pl.BlockSpec((step, block), lambda i, _: (0, i))]
+        start_blocks = [
+            pl.BlockSpec((pl.Element(step), pl.Element(block)), lambda i, _: (skip, i * block))
+        ]
         scratch = []
     return kernel_call(
-        functools.partial(rows_kernel, distances, with_adapters),
+        functools.partial(rows_kernel, distances, first if with_adapters else None),
         grid_spec=pltpu.PrefetchScalarGridSpec(
             num_scalar_prefetch=1,
             grid=(features // block,),
             in_specs=[
                 pl.BlockSpec(memory_space=pl.ANY),
                 *start_blocks,
-                *(whole(b) for b in arrays),
+                *(
+                    pl.BlockSpec(
+                        (pl.Element(step), pl.Element(b.shape[1])),
+                        lambda i, _, b=b: (skip if b.shape[0] > step else 0, 0),
+                    )
+                    for b in arrays
+                ),
                 weight_block,
             ],
-            out_specs=pl.BlockSpec((step, block), lambda i, _: (at, i)),
+            out_specs=out_block,
             scratch_shapes=scratch,
         ),
         out_shape=out,
@@ -382,7 +400,7 @@
     up = adapter_up_weight.reshape(adapters * rank, columns)
     index = token_adapter_index[None, :]
 
-    step = tokens // 2
+    cut = tokens * FIRST_EIGHTHS // 8
     order = jnp.array([3, 1, 2, 0], jnp.int32) ^ lax.axis_index("dp")
     slots = jnp.repeat(owner_slot_adapter.reshape(4, -1)[order].reshape(-1), rank)[:, None]
     weight = output_projection_weight
@@ -396,52 +414,63 @@
     def to_end(block):
         return lax.ppermute(block, "tensor", TO_ENDS)
 
-    own = [projection_output_gradient[c * step : (c + 1) * step] for c in range(2)]
+    own = [projection_output_gradient[:cut], projection_output_gradient[cut:]]
     near, across, far, end_across, end_far = ({} for _ in range(5))
 
-    near[0], across[0], near[1] = swap(own[0]), cross(own[0]), swap(own[1])
+    near[0], across[0] = swap(own[0]), cross(own[0])
     low_part = low_rank(index, index, down, attention_output, up, projection_output_gradient, rank)
-    low_part, near[0], across[0] = together(low_part, near[0], across[0])
     low_terms = [low_part] + [lax.ppermute(low_part, "tensor", pairs(4, d)) for d in (1, 2, 3)]
-    far[0] = cross(near[0])
-    near[1], far[0], across[0], own[1], *low_terms = together(
-        near[1], far[0], across[0], own[1], *low_terms
-    )
-    across[1], end_across[0] = cross(own[1]), to_end(across[0])
-    end_far[0], far[1] = to_end(far[0]), cross(near[1])
+    near[0], across[0], own[1], *low_terms = together(near[0], across[0], own[1], *low_terms)
+    near[1], far[0] = swap(own[1]), cross(near[0])
     send, keep, low = adapter_gradients(
         slots, index, low_terms, attention_output, projection_output_gradient
     )
-    send, keep, end_across[0], across[1] = together(send, keep, end_across[0], across[1])
+    send, keep, near[1], far[0], across[0], own[1], index = together(
+        send, keep, near[1], far[0], across[0], own[1], index
+    )
+    end_across[0], across[1] = to_end(across[0]), cross(own[1])
     got = lax.ppermute(send, "dp", pairs(4, FLIP_CORE))
+    end_far[0], far[1] = to_end(far[0]), cross(near[1])
+    to_x, keep = add_in_halves(keep, got)
+    to_x, keep, end_across[0], across[1], index = together(
+        to_x, keep, end_across[0], across[1], index
+    )
+    got = lax.ppermute(to_x, "dp", pairs(4, FLIP_X))
     end_across[1] = to_end(across[1])
-    to_x, keep = add_in_halves(keep, got)
-    to_x, keep, end_far[0], far[1], index = together(to_x, keep, end_far[0], far[1], index)
-    got = lax.ppermute(to_x, "dp", pairs(4, FLIP_X))
-    end_far[1] = to_end(far[1])
-    result = add_products(
+    base0 = add_products(
         here,
-        here,
+        None,
         (index, low, down),
-        ((0, own[0]), (1, near[0]), (2, far[0]), (2, end_across[0]), (3, across[0]), (3, end_far[0])),
+        ((0, own[0]), (1, near[0]), (2, far[0]), (2, end_across[0])),
         weight,
         0,
         tokens,
     )
-    result, end_across[1], index, got = together(result, end_across[1], index, got)
+    base0, end_far[0] = together(base0, end_far[0])
+    result = add_products(
+        here, here, base0, ((3, across[0]), (3, end_far[0])), weight, 0, tokens
+    )
+    result, far[1], index = together(result, far[1], index)
+    tail = far[1].shape[0] - LAST_ROWS
+    end_far[1], end_far[2] = to_end(far[1][:tail]), to_end(far[1][tail:])
     grad_a, grad_b = owned_sums(keep, got, attention_columns)
+    grad_a, grad_b, end_across[1], index = together(grad_a, grad_b, end_across[1], index)
     base = add_products(
         here,
         None,
         (index, low, down),
         ((0, own[1]), (1, near[1]), (2, far[1]), (2, end_across[1])),
         weight,
-        step,
+        cut,
         tokens,
     )
-    grad_a, grad_b, base, end_far[1], result = together(grad_a, grad_b, base, end_far[1], result)
+    base, end_far[1], result = together(base, end_far[1], result)
     result = add_products(
-        here, result, base, ((3, across[1]), (3, end_far[1])), weight, step, tokens
+        here, result, base, ((3, across[1]), (3, end_far[1])), weight, cut, tokens
+    )
+    result, end_far[2] = together(result, end_far[2])
+    result = add_products(
+        here, result, base, ((3, across[1]), (3, end_far[2])), weight, cut + tail, tokens, tail
     )
     grad_a = grad_a.reshape(-1, rank, attention_columns)
     grad_b = grad_b.reshape(-1, rank, columns)

time: 219 us -> 205 us (0.936)
  waiting for transfers between devices: 96.1 us -> 73.6 us
  Pallas kernels: 85 us -> 92.2 us
  local copies, waits for them, and re-layouts: 7.8 us -> 11.1 us
  starting transfers between devices: 28.7 us -> 26.4 us
    ppermute x2, waiting for transfers between devices: 30.3 us -> 15.8 us  [swap(): return lax.ppermute(block, 'tensor', pairs(4, 1))]
    pallas_call x3 -> x5, Pallas kernels: 45.2 us -> 52.4 us  [add_products(): kernel_call(functools.partial(rows_kernel, distances, first if with_adapt...]
    slice x1 -> x4, local copies, waits for them, and re-layouts: 1.88 us -> 7.95 us  [the longest x2 4.21 us: line_device(): end_far[1], end_far[2] = (to_end(far[1][:tail]), to_end(far[1][tail:]))]
    ppermute x4 -> x5, waiting for transfers between devices: 39.5 us -> 33.9 us  [to_end(): return lax.ppermute(block, 'tensor', TO_ENDS)]
    ppermute x3, starting transfers between devices: 9.43 us -> 5.91 us  [line_device(): lax.ppermute(low_part, 'tensor', pairs(4, d))]
    ppermute x1, waiting for transfers between devices: 8.03 us -> 4.89 us  [line_device(): got = lax.ppermute(send, 'dp', pairs(4, FLIP_CORE))]
    ppermute x1, waiting for transfers between devices: 1.6 us -> 4.48 us  [line_device(): got = lax.ppermute(to_x, 'dp', pairs(4, FLIP_X))]
    unnamed x24 -> x14, local copies, waits for them, and re-layouts: 4.02 us -> 1.25 us
  transfers between devices with their start and end apart: 15 -> 16, of which waited for: 10 -> 10; matrix products, arithmetic and copies ran while one was open for 1% -> 4% of each run, Pallas kernels for 36% -> 43%
where the time goes in v3:
time: 205 us; the launch traced here: 204 us
  Pallas kernels  92.2 us (45%)
  waiting for transfers between devices  73.6 us (36%)
  starting transfers between devices  26.4 us (13%)
  local copies, waits for them, and re-layouts  11.1 us (5%)
    pallas_call x5, Pallas kernels, add_products(): kernel_call(functools.partial(rows_kernel, distances, first if with_adapt...  52.4 us
    ppermute x5, waiting for transfers between devices, to_end(): return lax.ppermute(block, 'tensor', TO_ENDS)  33.9 us
    ppermute x2, waiting for transfers between devices, swap(): return lax.ppermute(block, 'tensor', pairs(4, 1))  15.8 us
    pallas_call x1, Pallas kernels, adapter_gradients(): kernel_call(adapter_gradient_kernel, grid=(4,), in_specs=[pl.BlockSpec((b...  15.6 us
    ppermute x3, waiting for transfers between devices, line_device(): lax.ppermute(low_part, 'tensor', pairs(4, d))  14.5 us
    pallas_call x1, Pallas kernels, low_rank(): kernel_call(functools.partial(low_rank_kernel, rank), grid=(4,), in_specs...  12.2 us
    pallas_call x1, Pallas kernels, add_in_halves(): kernel_call(halves_kernel, grid=(4,), in_specs=[both, both], out_specs=[p...  7.4 us
    ppermute x4, starting transfers between devices, cross(): return lax.ppermute(block, 'tensor', MIDDLES)  7.07 us
  transfers between devices with their start and end apart: 16, of which 10 were waited for; matrix products, arithmetic and copies ran while one was open for 4% of the time, Pallas kernels for 43%

profile of v3, /device:TPU:0, one launch (start us, length us, event | category | flops | bytes accessed | tf_op | source)
XLA Modules:
  0.0 204.0 jit_solution(16445803061327675048)
XLA Ops:
  0.6 2.2 %slice.12.refs_3_ = bf16[384,1280]{1,0:T(8,128)(2,1)} slice(bf16[1024,1280]{1,0:T(8,128)(2,1)} %gradient_ref.3), slice={[0:384], [0:1280]} | slice | bytes 1966080 | tf_op jit(solution)/shard_map/slice | solution.py:417
  2.8 3.0 %collective-permute-start = (bf16[384,1280]{1,0:T(8,128)(2,1)}, bf16[384,1280]{1,0:T(8,128)(2,1)}, u32[]{:S(2)}, u32[]{:S(2)}) collective-permute-start(bf16[384,1280]{1,0:T(8,128)(2,1)} %slice.12.refs_3_), channel_id=1, source_target_pairs={{0,4},{4,0},{8,12},{12,8},{1,5},{5,1},{9,13},{13,9},{2,6},{6,2},{1... | collective-permute-start | bytes 2949128 | tf_op jit(solution)/shard_map/ppermute | solution.py:409
  7.5 12.2 %shard_map.103.low0 = f32[32,1024]{1,0:T(8,128)} custom-call(s32[1,1024]{1,0:T(1,128)} %bitcast.10, s32[1,1024]{1,0:T(1,128)} %bitcast.11, bf16[1024,2048]{1,0:T(8,128)(2,1)} %bitcast.6, bf16[1024,2048]{1,0:T(8,128)(2,1)} %values_ref.3, bf16[1024,1280]{1,0:T(8,128)(2,1)} %bitcast.9, bf16[1024,1280]{1,0:T(8,128)(2,1)} %gradient_ref.3), custom_call_target="tpu_custom_call" | custom-call | flops 1048576 | bytes 65536 | tf_op jit(solution)/shard_map/pallas_call | solution.py:165
  19.6 3.5 %collective-permute-start.2 = (f32[32,1024]{1,0:T(8,128)}, f32[32,1024]{1,0:T(8,128)S(1)}, u32[]{:S(2)}, u32[]{:S(2)}) collective-permute-start(f32[32,1024]{1,0:T(8,128)} %shard_map.103.low0), channel_id=1, source_target_pairs={{0,4},{4,0},{8,12},{12,8},{1,5},{5,1},{9,13},{13,9},{2,6},{6,2},{1... | collective-permute-start | bytes 393224 | tf_op jit(solution)/shard_map/ppermute | solution.py:422
  23.1 2.4 %collective-permute-start.4 = (f32[32,1024]{1,0:T(8,128)}, f32[32,1024]{1,0:T(8,128)S(1)}, u32[]{:S(2)}, u32[]{:S(2)}) collective-permute-start(f32[32,1024]{1,0:T(8,128)} %shard_map.103.low0), channel_id=1, source_target_pairs={{0,12},{4,8},{8,4},{12,0},{1,13},{5,9},{9,5},{13,1},{2,14},{6,10},... | collective-permute-start | bytes 393224 | tf_op jit(solution)/shard_map/ppermute | solution.py:422
  27.1 4.0 %collective-permute-done.2.low1 = f32[32,1024]{1,0:T(8,128)S(1)} collective-permute-done((f32[32,1024]{1,0:T(8,128)}, f32[32,1024]{1,0:T(8,128)S(1)}, u32[]{:S(2)}, u32[]{:S(2)}) %collective-permute-start.2) | collective-permute-done | bytes 131104 | tf_op jit(solution)/shard_map/ppermute | solution.py:422
  31.2 10.4 %collective-permute-done.3.low2 = f32[32,1024]{1,0:T(8,128)S(1)} collective-permute-done((f32[32,1024]{1,0:T(8,128)}, f32[32,1024]{1,0:T(8,128)S(1)}, u32[]{:S(2)}, u32[]{:S(2)}) %collective-permute-start.3) | collective-permute-done | bytes 131104 | tf_op jit(solution)/shard_map/ppermute | solution.py:422
  41.6 2.3 %collective-permute-start.5 = (bf16[640,1280]{1,0:T(8,128)(2,1)S(1)}, bf16[640,1280]{1,0:T(8,128)(2,1)}, u32[]{:S(2)}, u32[]{:S(2)}) collective-permute-start(bf16[640,1280]{1,0:T(8,128)(2,1)S(1)} %slice.13.refs_3_), channel_id=1, source_target_pairs={{0,4},{4,0},{8,12},{12,8},{1,5},{5,1},{9,13},{13,9},{2,6},{6,2},{1... | collective-permute-start | bytes 4915208 | tf_op jit(solution)/shard_map/ppermute | solution.py:409
  47.5 15.6 %shard_map.104 = (f32[512,3328]{1,0:T(8,128)}, f32[512,3328]{1,0:T(8,128)}, f32[32,1024]{1,0:T(8,128)}) custom-call(s32[1024,1]{1,0:T(8,128)} %broadcast_in_dim_reshape.4.slots_ref, s32[1,1024]{1,0:T(1,128)} %bitcast.12, f32[32,1024]{1,0:T(8,128)} %shard_map.103.low0, f32[32,1024]{1,0:T(8,128)} %copy-done.2, f32[32,1024]{1,0:T(8,128)} %copy-done.3, ...), custom_call_target="tpu_custom_call" | custom-call | flops 1048576 | bytes 65536 | tf_op jit(solution)/shard_map/pallas_call | solution.py:222
  63.1 15.8 %collective-permute-done.5.refs_4_ = bf16[640,1280]{1,0:T(8,128)(2,1)} collective-permute-done((bf16[640,1280]{1,0:T(8,128)(2,1)S(1)}, bf16[640,1280]{1,0:T(8,128)(2,1)}, u32[]{:S(2)}, u32[]{:S(2)}) %collective-permute-start.5) | collective-permute-done | bytes 1638432 | tf_op jit(solution)/shard_map/ppermute | solution.py:409
  85.3 4.9 %collective-permute-done.7.got_ref = f32[512,3328]{1,0:T(8,128)} collective-permute-done((f32[512,3328]{1,0:T(8,128)}, f32[512,3328]{1,0:T(8,128)}, u32[]{:S(2)}, u32[]{:S(2)}) %collective-permute-start.7) | collective-permute-done | bytes 6815776 | tf_op jit(solution)/shard_map/ppermute | solution.py:432
  90.2 7.4 %shard_map.105 = (bf16[256,3328]{1,0:T(8,128)(2,1)}, f32[256,3328]{1,0:T(8,128)}) custom-call(f32[512,3328]{1,0:T(8,128)} %get-tuple-element.52.keep_ref, f32[512,3328]{1,0:T(8,128)} %collective-permute-done.7.got_ref), custom_call_target="tpu_custom_call" | custom-call | flops 1048576 | bytes 65536 | tf_op jit(solution)/shard_map/pallas_call | solution.py:257
  97.6 10.2 %collective-permute-done.8.refs_6_ = bf16[384,1280]{1,0:T(8,128)(2,1)} collective-permute-done((bf16[384,1280]{1,0:T(8,128)(2,1)}, bf16[384,1280]{1,0:T(8,128)(2,1)}, u32[]{:S(2)}, u32[]{:S(2)}) %collective-permute-start.8) | collective-permute-done | bytes 983072 | tf_op jit(solution)/shard_map/ppermute | solution.py:415
  110.6 14.8 %shard_map.107.refs_0_ = f32[384,2048]{1,0:T(8,128)} custom-call(s32[1]{0:T(128)} %bitcast.here_ref._, s32[1]{0:T(128)} %bitcast.here_ref._, s32[1,1024]{1,0:T(1,128)} %bitcast.13, f32[32,1024]{1,0:T(8,128)} %get-tuple-element.65.refs_1_, bf16[1024,2048]{1,0:T(8,128)(2,1)} %bitcast.7, bf16[384,1280]{1,0:T(8,128)(2,1)} %slice.12.refs_3_, ...), custom_call_target="tpu_custom_call" | custom-call | flops 1048576 | bytes 65536 | tf_op jit(solution)/shard_map/pallas_call | solution.py:361
  125.5 3.4 %collective-permute-done.12.refs_2_ = bf16[384,1280]{1,0:T(8,128)(2,1)} collective-permute-done((bf16[384,1280]{1,0:T(8,128)(2,1)}, bf16[384,1280]{1,0:T(8,128)(2,1)}, u32[]{:S(2)}, u32[]{:S(2)}) %collective-permute-start.12) | collective-permute-done | bytes 983072 | tf_op jit(solution)/shard_map/ppermute | solution.py:415
  128.9 6.1 %shard_map.108._ = bf16[1024,2048]{1,0:T(8,128)(2,1)} custom-call(s32[1]{0:T(128)} %bitcast.here_ref._, s32[1]{0:T(128)} %bitcast.here_ref._, f32[384,2048]{1,0:T(8,128)} %shard_map.107.refs_0_, bf16[384,1280]{1,0:T(8,128)(2,1)} %collective-permute-done.1.refs_1_, bf16[384,1280]{1,0:T(8,128)(2,1)} %collective-permute-done.12.refs_2_, bf16[2048,5120]{1,0:T(8,128)(2,1)} %refs_3_.5), custom_call_target="tpu_custom_call" | custom-call | flops 1048576 | bytes 65536 | tf_op jit(solution)/shard_map/pallas_call | solution.py:361
  135.0 2.2 %slice.14 = bf16[384,1280]{1,0:T(8,128)(2,1)} slice(bf16[640,1280]{1,0:T(8,128)(2,1)} %collective-permute-done.13.refs_5_), slice={[0:384], [0:1280]} | slice | bytes 1966080 | tf_op jit(solution)/shard_map/slice | solution.py:455
  142.0 4.5 %collective-permute-done.10.got_ref = bf16[256,3328]{1,0:T(8,128)(2,1)S(1)} collective-permute-done((bf16[256,3328]{1,0:T(8,128)(2,1)}, bf16[256,3328]{1,0:T(8,128)(2,1)S(1)}, u32[]{:S(2)}, u32[]{:S(2)}) %collective-permute-start.10) | collective-permute-done | bytes 1703968 | tf_op jit(solution)/shard_map/ppermute | solution.py:438
  147.7 4.6 %shard_map.106 = (f32[256,2048]{1,0:T(8,128)}, f32[256,1280]{1,0:T(8,128)}) custom-call(f32[256,3328]{1,0:T(8,128)} %get-tuple-element.59.keep_ref, bf16[256,3328]{1,0:T(8,128)(2,1)} %copy-done.1), custom_call_target="tpu_custom_call" | custom-call | flops 1048576 | bytes 65536 | tf_op jit(solution)/shard_map/pallas_call | solution.py:282
  152.3 11.7 %collective-permute-done.11.refs_6_ = bf16[640,1280]{1,0:T(8,128)(2,1)} collective-permute-done((bf16[640,1280]{1,0:T(8,128)(2,1)}, bf16[640,1280]{1,0:T(8,128)(2,1)}, u32[]{:S(2)}, u32[]{:S(2)}) %collective-permute-start.11) | collective-permute-done | bytes 1638432 | tf_op jit(solution)/shard_map/ppermute | solution.py:415
  164.0 20.0 %shard_map.109.refs_0_ = f32[640,2048]{1,0:T(8,128)} custom-call(s32[1]{0:T(128)} %bitcast.here_ref._, s32[1]{0:T(128)} %bitcast.here_ref._, s32[1,1024]{1,0:T(1,128)} %bitcast.14, f32[32,1024]{1,0:T(8,128)} %get-tuple-element.65.refs_1_, bf16[1024,2048]{1,0:T(8,128)(2,1)} %bitcast.8, bf16[640,1280]{1,0:T(8,128)(2,1)} %copy-done, ...), custom_call_target="tpu_custom_call" | custom-call | flops 1048576 | bytes 65536 | tf_op jit(solution)/shard_map/pallas_call | solution.py:361
  185.1 6.1 %shard_map.110._ = bf16[1024,2048]{1,0:T(8,128)(2,1)} custom-call(s32[1]{0:T(128)} %bitcast.here_ref._, bf16[1024,2048]{1,0:T(8,128)(2,1)} %shard_map.108._, f32[640,2048]{1,0:T(8,128)} %shard_map.109.refs_0_, bf16[640,1280]{1,0:T(8,128)(2,1)} %collective-permute-done.9.refs_1_, ...), custom_call_target="tpu_custom_call", output_to_operand_aliasing={{}: (1, {})} | custom-call | flops 1048576 | bytes 65536 | tf_op jit(solution)/shard_map/pallas_call | solution.py:361
  191.2 7.5 %collective-permute-done.15.refs_2_ = bf16[256,1280]{1,0:T(8,128)(2,1)} collective-permute-done((bf16[256,1280]{1,0:T(8,128)(2,1)}, bf16[256,1280]{1,0:T(8,128)(2,1)}, u32[]{:S(2)}, u32[]{:S(2)}) %collective-permute-start.15) | collective-permute-done | bytes 655392 | tf_op jit(solution)/shard_map/ppermute | solution.py:415
  198.7 5.2 %shard_map.111 = bf16[1024,2048]{1,0:T(8,128)(2,1)} custom-call(s32[1]{0:T(128)} %bitcast.here_ref._, bf16[1024,2048]{1,0:T(8,128)(2,1)} %shard_map.110._, f32[640,2048]{1,0:T(8,128)} %shard_map.109.refs_0_, bf16[640,1280]{1,0:T(8,128)(2,1)} %collective-permute-done.9.refs_1_, ...), custom_call_target="tpu_custom_call", output_to_operand_aliasing={{}: (1, {})} | custom-call | flops 1048576 | bytes 65536 | tf_op jit(solution)/shard_map/pallas_call | solution.py:361
  (42 shorter events, 22.9 us)
Async XLA Ops:
  2.8 38.8 %collective-permute-start = (bf16[384,1280]{1,0:T(8,128)(2,1)}, bf16[384,1280]{1,0:T(8,128)(2,1)}, u32[]{:S(2)}, u32[]{:S(2)}) collective-permute-start(bf16[384,1280]{1,0:T(8,128)(2,1)} %slice.12.refs_3_), channel_id=1, source_target_pairs={{0,4},{4,0},{8,12},{12,8},{1,5},{5,1},{9,13},{13,9},{2,6},{6,2},{1... | collective-permute-start | bytes 2949128 | tf_op jit(solution)/shard_map/ppermute | solution.py:409
  5.9 35.8 %collective-permute-start.1 = (bf16[384,1280]{1,0:T(8,128)(2,1)}, bf16[384,1280]{1,0:T(8,128)(2,1)}, u32[]{:S(2)}, u32[]{:S(2)}) collective-permute-start(bf16[384,1280]{1,0:T(8,128)(2,1)} %slice.12.refs_3_), channel_id=1, source_target_pairs={{4,8},{8,4},{5,9},{9,5},{6,10},{10,6},{7,11},{11,7},{20,24},{24,20... | collective-permute-start | bytes 2949128 | tf_op jit(solution)/shard_map/ppermute | solution.py:412
  19.6 25.9 %copy-start.5 = (s32[64]{0:T(128)S(1)}, s32[64]{0:T(128)}, u32[]{:S(2)}) copy-start(s32[64]{0:T(128)} %param.11) | copy-start | bytes 772
  19.6 26.0 %copy-start.6 = (s32[4]{0:T(128)S(1)}, s32[4]{0:T(128)}, u32[]{:S(2)}) copy-start(s32[4]{0:T(128)} %constant.13.clone) | copy-start | bytes 52
  19.6 11.5 %collective-permute-start.2 = (f32[32,1024]{1,0:T(8,128)}, f32[32,1024]{1,0:T(8,128)S(1)}, u32[]{:S(2)}, u32[]{:S(2)}) collective-permute-start(f32[32,1024]{1,0:T(8,128)} %shard_map.103.low0), channel_id=1, source_target_pairs={{0,4},{4,0},{8,12},{12,8},{1,5},{5,1},{9,13},{13,9},{2,6},{6,2},{1... | collective-permute-start | bytes 393224 | tf_op jit(solution)/shard_map/ppermute | solution.py:422
  23.1 18.5 %collective-permute-start.3 = (f32[32,1024]{1,0:T(8,128)}, f32[32,1024]{1,0:T(8,128)S(1)}, u32[]{:S(2)}, u32[]{:S(2)}) collective-permute-start(f32[32,1024]{1,0:T(8,128)} %shard_map.103.low0), channel_id=1, source_target_pairs={{0,8},{4,12},{8,0},{12,4},{1,9},{5,13},{9,1},{13,5},{2,10},{6,14},... | collective-permute-start | bytes 393224 | tf_op jit(solution)/shard_map/ppermute | solution.py:422
  23.1 18.5 %collective-permute-start.4 = (f32[32,1024]{1,0:T(8,128)}, f32[32,1024]{1,0:T(8,128)S(1)}, u32[]{:S(2)}, u32[]{:S(2)}) collective-permute-start(f32[32,1024]{1,0:T(8,128)} %shard_map.103.low0), channel_id=1, source_target_pairs={{0,12},{4,8},{8,4},{12,0},{1,13},{5,9},{9,5},{13,1},{2,14},{6,10},... | collective-permute-start | bytes 393224 | tf_op jit(solution)/shard_map/ppermute | solution.py:422
  27.1 51.9 %copy-start = (bf16[640,1280]{1,0:T(8,128)(2,1)}, bf16[640,1280]{1,0:T(8,128)(2,1)S(1)}, u32[]{:S(2)}) copy-start(bf16[640,1280]{1,0:T(8,128)(2,1)S(1)} %slice.13.refs_3_) | copy-start | bytes 4915204
  31.1 16.4 %copy-start.2 = (f32[32,1024]{1,0:T(8,128)}, f32[32,1024]{1,0:T(8,128)S(1)}, u32[]{:S(2)}) copy-start(f32[32,1024]{1,0:T(8,128)S(1)} %collective-permute-done.2.low1) | copy-start | bytes 393220
  41.6 5.9 %copy-start.3 = (f32[32,1024]{1,0:T(8,128)}, f32[32,1024]{1,0:T(8,128)S(1)}, u32[]{:S(2)}) copy-start(f32[32,1024]{1,0:T(8,128)S(1)} %collective-permute-done.3.low2) | copy-start | bytes 393220
  41.6 5.9 %copy-start.4 = (f32[32,1024]{1,0:T(8,128)}, f32[32,1024]{1,0:T(8,128)S(1)}, u32[]{:S(2)}) copy-start(f32[32,1024]{1,0:T(8,128)S(1)} %collective-permute-done.4.low3) | copy-start | bytes 393220
  41.6 37.3 %collective-permute-start.5 = (bf16[640,1280]{1,0:T(8,128)(2,1)S(1)}, bf16[640,1280]{1,0:T(8,128)(2,1)}, u32[]{:S(2)}, u32[]{:S(2)}) collective-permute-start(bf16[640,1280]{1,0:T(8,128)(2,1)S(1)} %slice.13.refs_3_), channel_id=1, source_target_pairs={{0,4},{4,0},{8,12},{12,8},{1,5},{5,1},{9,13},{13,9},{2,6},{6,2},{1... | collective-permute-start | bytes 4915208 | tf_op jit(solution)/shard_map/ppermute | solution.py:409
  43.9 19.2 %collective-permute-start.6 = (bf16[384,1280]{1,0:T(8,128)(2,1)}, bf16[384,1280]{1,0:T(8,128)(2,1)}, u32[]{:S(2)}, u32[]{:S(2)}) collective-permute-start(bf16[384,1280]{1,0:T(8,128)(2,1)} %collective-permute-done.refs_4_), channel_id=1, source_target_pairs={{4,8},{8,4},{5,9},{9,5},{6,10},{10,6},{7,11},{11,7},{20,24},{24,20... | collective-permute-start | bytes 2949128 | tf_op jit(solution)/shard_map/ppermute | solution.py:412
  78.9 11.3 %collective-permute-start.7 = (f32[512,3328]{1,0:T(8,128)}, f32[512,3328]{1,0:T(8,128)}, u32[]{:S(2)}, u32[]{:S(2)}) collective-permute-start(f32[512,3328]{1,0:T(8,128)} %get-tuple-element.53), channel_id=1, source_target_pairs={{0,1},{1,0},{2,3},{3,2},{4,5},{5,4},{6,7},{7,6},{8,9},{9,8},{10,11... | collective-permute-start | bytes 20447240 | tf_op jit(solution)/shard_map/ppermute | solution.py:432
  78.9 28.9 %collective-permute-start.9 = (bf16[640,1280]{1,0:T(8,128)(2,1)S(1)}, bf16[640,1280]{1,0:T(8,128)(2,1)}, u32[]{:S(2)}, u32[]{:S(2)}) collective-permute-start(bf16[640,1280]{1,0:T(8,128)(2,1)S(1)} %slice.13.refs_3_), channel_id=1, source_target_pairs={{4,8},{8,4},{5,9},{9,5},{6,10},{10,6},{7,11},{11,7},{20,24},{24,20... | collective-permute-start | bytes 4915208 | tf_op jit(solution)/shard_map/ppermute | solution.py:412
  80.9 27.0 %collective-permute-start.8 = (bf16[384,1280]{1,0:T(8,128)(2,1)}, bf16[384,1280]{1,0:T(8,128)(2,1)}, u32[]{:S(2)}, u32[]{:S(2)}) collective-permute-start(bf16[384,1280]{1,0:T(8,128)(2,1)} %collective-permute-done.1.refs_1_), channel_id=1, source_target_pairs={{4,0},{8,12},{5,1},{9,13},{6,2},{10,14},{7,3},{11,15},{20,16},{24,... | collective-permute-start | bytes 2949128 | tf_op jit(solution)/shard_map/ppermute | solution.py:415
  82.2 52.9 %collective-permute-start.13 = (bf16[640,1280]{1,0:T(8,128)(2,1)}, bf16[640,1280]{1,0:T(8,128)(2,1)}, u32[]{:S(2)}, u32[]{:S(2)}) collective-permute-start(bf16[640,1280]{1,0:T(8,128)(2,1)} %collective-permute-done.5.refs_4_), channel_id=1, source_target_pairs={{4,8},{8,4},{5,9},{9,5},{6,10},{10,6},{7,11},{11,7},{20,24},{24,20... | collective-permute-start | bytes 4915208 | tf_op jit(solution)/shard_map/ppermute | solution.py:412
  84.0 44.9 %collective-permute-start.12 = (bf16[384,1280]{1,0:T(8,128)(2,1)}, bf16[384,1280]{1,0:T(8,128)(2,1)}, u32[]{:S(2)}, u32[]{:S(2)}) collective-permute-start(bf16[384,1280]{1,0:T(8,128)(2,1)} %collective-permute-done.6.refs_5_), channel_id=1, source_target_pairs={{4,0},{8,12},{5,1},{9,13},{6,2},{10,14},{7,3},{11,15},{20,16},{24,... | collective-permute-start | bytes 2949128 | tf_op jit(solution)/shard_map/ppermute | solution.py:415
  107.8 38.7 %collective-permute-start.10 = (bf16[256,3328]{1,0:T(8,128)(2,1)}, bf16[256,3328]{1,0:T(8,128)(2,1)S(1)}, u32[]{:S(2)}, u32[]{:S(2)}) collective-permute-start(bf16[256,3328]{1,0:T(8,128)(2,1)} %get-tuple-element.60), channel_id=1, source_target_pairs={{0,2},{1,3},{2,0},{3,1},{4,6},{5,7},{6,4},{7,5},{8,10},{9,11},{10,... | collective-permute-start | bytes 5111816 | tf_op jit(solution)/shard_map/ppermute | solution.py:438
  109.3 54.7 %collective-permute-start.11 = (bf16[640,1280]{1,0:T(8,128)(2,1)}, bf16[640,1280]{1,0:T(8,128)(2,1)}, u32[]{:S(2)}, u32[]{:S(2)}) collective-permute-start(bf16[640,1280]{1,0:T(8,128)(2,1)} %collective-permute-done.9.refs_1_), channel_id=1, source_target_pairs={{4,0},{8,12},{5,1},{9,13},{6,2},{10,14},{7,3},{11,15},{20,16},{24,... | collective-permute-start | bytes 4915208 | tf_op jit(solution)/shard_map/ppermute | solution.py:415
  137.3 47.8 %collective-permute-start.14 = (bf16[384,1280]{1,0:T(8,128)(2,1)}, bf16[384,1280]{1,0:T(8,128)(2,1)}, u32[]{:S(2)}, u32[]{:S(2)}) collective-permute-start(bf16[384,1280]{1,0:T(8,128)(2,1)} %slice.14), channel_id=1, source_target_pairs={{4,0},{8,12},{5,1},{9,13},{6,2},{10,14},{7,3},{11,15},{20,16},{24,... | collective-permute-start | bytes 2949128 | tf_op jit(solution)/shard_map/ppermute | solution.py:415
  140.5 58.2 %collective-permute-start.15 = (bf16[256,1280]{1,0:T(8,128)(2,1)}, bf16[256,1280]{1,0:T(8,128)(2,1)}, u32[]{:S(2)}, u32[]{:S(2)}) collective-permute-start(bf16[256,1280]{1,0:T(8,128)(2,1)} %slice.15), channel_id=1, source_target_pairs={{4,0},{8,12},{5,1},{9,13},{6,2},{10,14},{7,3},{11,15},{20,16},{24,... | collective-permute-start | bytes 1966088 | tf_op jit(solution)/shard_map/ppermute | solution.py:415
  146.5 1.2 copy-start.1

commit v4 on v3

--- a/solution.py
+++ b/solution.py
@@ -10,6 +10,7 @@
 ADAPTER_SCALE = 2.0
 OBJECTIVE_WEIGHT = 0.05
 LAST_ROWS = 256
+PIECE = 128
 FIRST_EIGHTHS = 3
 
 TO_ENDS = [(1, 0), (2, 3)]
@@ -184,13 +185,15 @@
 
 
 def adapter_gradient_kernel(
-    slots_ref, index_ref, low0, low1, low2, low3, values_ref, gradient_ref, send_ref, keep_ref, low_ref
+    here_ref, slots_ref, index_ref, pair, crossed, from_middle, values_ref, gradient_ref, send_ref, keep_ref, low_ref
 ):
     step = pl.program_id(0)
 
     @pl.when(step == 0)
     def _():
-        low_ref[...] = (low0[...] + low1[...]) + (low2[...] + low3[...])
+        middle = (here_ref[0] == 1) | (here_ref[0] == 2)
+        total = pair[...] + crossed[...]
+        low_ref[...] = jnp.where(middle, total, from_middle[...])
 
     rank = low_ref.shape[0] // 2
     low = low_ref[...].astype(jnp.bfloat16).astype(jnp.float32)
@@ -214,28 +217,32 @@
         keep_ref[:, split:] = b
 
 
-def adapter_gradients(slots, index, low_terms, values, gradient):
+def adapter_gradients(here, slots, index, low_terms, values, gradient):
     rows = slots.shape[0]
     block = rows // 4
     width = values.shape[1] + gradient.shape[1]
     half = jax.ShapeDtypeStruct((rows // 2, width), jnp.float32)
+    low = jax.ShapeDtypeStruct(low_terms[0].shape, jnp.float32)
     return kernel_call(
         adapter_gradient_kernel,
-        grid=(4,),
-        in_specs=[
-            pl.BlockSpec((block, 1), lambda i: (i, 0)),
-            whole(index),
-            *(whole(term) for term in low_terms),
-            whole(values),
-            whole(gradient),
-        ],
-        out_specs=[
-            pl.BlockSpec((block, width), lambda i: (jnp.minimum(i, 1), 0)),
-            pl.BlockSpec((block, width), lambda i: (jnp.maximum(i - 2, 0), 0)),
-            whole(low_terms[0]),
-        ],
-        out_shape=[half, half, jax.ShapeDtypeStruct(low_terms[0].shape, jnp.float32)],
-    )(slots, index, *low_terms, values, gradient)
+        grid_spec=pltpu.PrefetchScalarGridSpec(
+            num_scalar_prefetch=1,
+            grid=(4,),
+            in_specs=[
+                pl.BlockSpec((block, 1), lambda i, _: (i, 0)),
+                whole(index),
+                *(whole(term) for term in low_terms),
+                whole(values),
+                whole(gradient),
+            ],
+            out_specs=[
+                pl.BlockSpec((block, width), lambda i, _: (jnp.minimum(i, 1), 0)),
+                pl.BlockSpec((block, width), lambda i, _: (jnp.maximum(i - 2, 0), 0)),
+                whole(low),
+            ],
+        ),
+        out_shape=[half, half, low],
+    )(here, slots, index, *low_terms, values, gradient)
 
 
 def halves_kernel(keep_ref, got_ref, send_ref, out_ref):
@@ -419,15 +426,26 @@
 
     near[0], across[0] = swap(own[0]), cross(own[0])
     low_part = low_rank(index, index, down, attention_output, up, projection_output_gradient, rank)
-    low_terms = [low_part] + [lax.ppermute(low_part, "tensor", pairs(4, d)) for d in (1, 2, 3)]
-    near[0], across[0], own[1], *low_terms = together(near[0], across[0], own[1], *low_terms)
-    near[1], far[0] = swap(own[1]), cross(near[0])
+    low_near = swap(low_part)
+    own_first, own_rest = own[1][:PIECE], own[1][PIECE:]
+    near[0], across[0], low_near, own_first = together(near[0], across[0], low_near, own_first)
+    near_first = swap(own_first)
+    pair = low_part + low_near
+    crossed = cross(pair)
+    pair, crossed, near[0] = together(pair, crossed, near[0])
+    from_middle = to_end(pair + crossed)
+    near_first, from_middle, own_rest, near[0] = together(
+        near_first, from_middle, own_rest, near[0]
+    )
+    near_rest, far[0] = swap(own_rest), cross(near[0])
+    low_terms = (pair, crossed, from_middle)
     send, keep, low = adapter_gradients(
-        slots, index, low_terms, attention_output, projection_output_gradient
-    )
-    send, keep, near[1], far[0], across[0], own[1], index = together(
-        send, keep, near[1], far[0], across[0], own[1], index
-    )
+        here, slots, index, low_terms, attention_output, projection_output_gradient
+    )
+    send, keep, near_rest, far[0], across[0], own[1], index = together(
+        send, keep, near_rest, far[0], across[0], own[1], index
+    )
+    near[1] = jnp.concatenate([near_first, near_rest], axis=0)
     end_across[0], across[1] = to_end(across[0]), cross(own[1])
     got = lax.ppermute(send, "dp", pairs(4, FLIP_CORE))
     end_far[0], far[1] = to_end(far[0]), cross(near[1])

time: 205 us -> 199 us (0.971)
  waiting for transfers between devices: 73.6 us -> 63.4 us
  local copies, waits for them, and re-layouts: 11.1 us -> 15.4 us
    ppermute x3 -> x0, waiting for transfers between devices: 14.5 us -> none  [line_device(): lax.ppermute(low_part, 'tensor', pairs(4, d))]
    ppermute x5 -> x6, waiting for transfers between devices: 33.9 us -> 42 us  [to_end(): return lax.ppermute(block, 'tensor', TO_ENDS)]
    ppermute x3 -> x0, starting transfers between devices: 5.91 us -> none  [line_device(): lax.ppermute(low_part, 'tensor', pairs(4, d))]
    ppermute x2 -> x4, starting transfers between devices: 5.3 us -> 9.38 us  [swap(): return lax.ppermute(block, 'tensor', pairs(4, 1))]
    slice x0 -> x2, local copies, waits for them, and re-layouts: none -> 3.45 us  [line_device(): own_first, own_rest = (own[1][:PIECE], own[1][PIECE:])]
    ppermute x1, waiting for transfers between devices: 4.89 us -> 1.64 us  [line_device(): got = lax.ppermute(send, 'dp', pairs(4, FLIP_CORE))]
    concatenate x0 -> x1, local copies, waits for them, and re-layouts: none -> 2.45 us  [line_device(): near[1] = jnp.concatenate([near_first, near_rest], axis=0)]
    slice x2, local copies, waits for them, and re-layouts: 3.75 us -> 1.37 us  [line_device(): own = [projection_output_gradient[:cut], projection_output_gradient[cut:]]]
  transfers between devices with their start and end apart: 16 -> 17, of which waited for: 10 -> 10; matrix products, arithmetic and copies ran while one was open for 4% -> 7% of each run, Pallas kernels for 43% -> 44%
where the time goes in v4:
time: 199 us; the launch traced here: 198 us
  Pallas kernels  92.2 us (46%)
  waiting for transfers between devices  63.4 us (32%)
  starting transfers between devices  25.6 us (13%)
  local copies, waits for them, and re-layouts  15.4 us (8%)
    pallas_call x5, Pallas kernels, add_products(): kernel_call(functools.partial(rows_kernel, distances, first if with_adapt...  52.4 us
    ppermute x6, waiting for transfers between devices, to_end(): return lax.ppermute(block, 'tensor', TO_ENDS)  42 us
    pallas_call x1, Pallas kernels, adapter_gradients(): kernel_call(adapter_gradient_kernel, grid_spec=pltpu.PrefetchScalarGridSp...  15.5 us
    ppermute x4, waiting for transfers between devices, swap(): return lax.ppermute(block, 'tensor', pairs(4, 1))  15.2 us
    pallas_call x1, Pallas kernels, low_rank(): kernel_call(functools.partial(low_rank_kernel, rank), grid=(4,), in_specs...  12.2 us
    ppermute x4, starting transfers between devices, swap(): return lax.ppermute(block, 'tensor', pairs(4, 1))  9.38 us
    ppermute x6, starting transfers between devices, to_end(): return lax.ppermute(block, 'tensor', TO_ENDS)  7.87 us
    pallas_call x1, Pallas kernels, add_in_halves(): kernel_call(halves_kernel, grid=(4,), in_specs=[both, both], out_specs=[p...  7.4 us
  transfers between devices with their start and end apart: 17, of which 10 were waited for; matrix products, arithmetic and copies ran while one was open for 7% of the time, Pallas kernels for 44%

profile of v4, /device:TPU:0, one launch (start us, length us, event | category | flops | bytes accessed | tf_op | source)
XLA Modules:
  0.0 198.3 jit_solution(13387834408092174337)
XLA Ops:
  1.9 3.1 %collective-permute-start = (bf16[384,1280]{1,0:T(8,128)(2,1)S(1)}, bf16[384,1280]{1,0:T(8,128)(2,1)}, u32[]{:S(2)}, u32[]{:S(2)}) collective-permute-start(bf16[384,1280]{1,0:T(8,128)(2,1)S(1)} %slice.20.refs_3_), channel_id=1, source_target_pairs={{0,4},{4,0},{8,12},{12,8},{1,5},{5,1},{9,13},{13,9},{2,6},{6,2},{1... | collective-permute-start | bytes 2949128 | tf_op jit(solution)/shard_map/ppermute | solution.py:416
  5.7 12.2 %shard_map.103 = f32[32,1024]{1,0:T(8,128)} custom-call(s32[1,1024]{1,0:T(1,128)} %bitcast.10, s32[1,1024]{1,0:T(1,128)} %bitcast.11, bf16[1024,2048]{1,0:T(8,128)(2,1)} %bitcast.6, bf16[1024,2048]{1,0:T(8,128)(2,1)} %values_ref.3, bf16[1024,1280]{1,0:T(8,128)(2,1)} %bitcast.9, bf16[1024,1280]{1,0:T(8,128)(2,1)} %gradient_ref.3), custom_call_target="tpu_custom_call" | custom-call | flops 1048576 | bytes 65536 | tf_op jit(solution)/shard_map/pallas_call | solution.py:166
  17.9 4.3 %collective-permute-start.2 = (f32[32,1024]{1,0:T(8,128)}, f32[32,1024]{1,0:T(8,128)S(1)}, u32[]{:S(2)}, u32[]{:S(2)}) collective-permute-start(f32[32,1024]{1,0:T(8,128)} %shard_map.103), channel_id=1, source_target_pairs={{0,4},{4,0},{8,12},{12,8},{1,5},{5,1},{9,13},{13,9},{2,6},{6,2},{1... | collective-permute-start | bytes 393224 | tf_op jit(solution)/shard_map/ppermute | solution.py:416
  23.3 6.3 %collective-permute-done.2 = f32[32,1024]{1,0:T(8,128)S(1)} collective-permute-done((f32[32,1024]{1,0:T(8,128)}, f32[32,1024]{1,0:T(8,128)S(1)}, u32[]{:S(2)}, u32[]{:S(2)}) %collective-permute-start.2) | collective-permute-done | bytes 131104 | tf_op jit(solution)/shard_map/ppermute | solution.py:416
  29.6 1.9 collective-permute-start.4
  34.5 2.5 %slice.22 = bf16[512,1280]{1,0:T(8,128)(2,1)} slice(bf16[1024,1280]{1,0:T(8,128)(2,1)} %gradient_ref.3), slice={[512:1024], [0:1280]} | slice | bytes 2621440 | tf_op jit(solution)/shard_map/slice | solution.py:430
  36.9 7.6 %collective-permute-done.5.from_middle = f32[32,1024]{1,0:T(8,128)S(1)} collective-permute-done((f32[32,1024]{1,0:T(8,128)S(1)}, f32[32,1024]{1,0:T(8,128)S(1)}, u32[]{:S(2)}, u32[]{:S(2)}) %collective-permute-start.5) | collective-permute-done | bytes 131104 | tf_op jit(solution)/shard_map/ppermute | solution.py:422
  48.3 15.5 %shard_map.104 = (f32[512,3328]{1,0:T(8,128)}, f32[512,3328]{1,0:T(8,128)}, f32[32,1024]{1,0:T(8,128)}) custom-call(s32[1]{0:T(128)} %bitcast.here_ref._, s32[1024,1]{1,0:T(8,128)} %broadcast_in_dim_reshape.4.slots_ref, s32[1,1024]{1,0:T(1,128)} %bitcast.12, f32[32,1024]{1,0:T(8,128)} %copy-done.4, f32[32,1024]{1,0:T(8,128)} %copy-done.6, ...), custom_call_target="tpu_custom_call" | custom-call | flops 1048576 | bytes 65536 | tf_op jit(solution)/shard_map/pallas_call | solution.py:226
  63.9 8.9 %collective-permute-done.6 = bf16[512,1280]{1,0:T(8,128)(2,1)} collective-permute-done((bf16[512,1280]{1,0:T(8,128)(2,1)}, bf16[512,1280]{1,0:T(8,128)(2,1)}, u32[]{:S(2)}, u32[]{:S(2)}) %collective-permute-start.6) | collective-permute-done | bytes 1310752 | tf_op jit(solution)/shard_map/ppermute | solution.py:416
  76.7 2.5 %constant_dynamic-update-slice_fusion.refs_4_ = bf16[640,1280]{1,0:T(8,128)(2,1)} fusion(bf16[640,1280]{1,0:T(8,128)(2,1)} %constant_dynamic-update-slice_fusion.1, bf16[512,1280]{1,0:T(8,128)(2,1)} %collective-permute-done.6), kind=kLoop, calls=%fused_computation.2 | loop fusion | bytes 2621440 | tf_op jit(solution)/shard_map/concatenate | solution.py:448
  84.1 7.4 %shard_map.105 = (bf16[256,3328]{1,0:T(8,128)(2,1)}, f32[256,3328]{1,0:T(8,128)}) custom-call(f32[512,3328]{1,0:T(8,128)} %get-tuple-element.59.keep_ref, f32[512,3328]{1,0:T(8,128)} %collective-permute-done.8.got_ref), custom_call_target="tpu_custom_call" | custom-call | flops 1048576 | bytes 65536 | tf_op jit(solution)/shard_map/pallas_call | solution.py:264
  91.5 10.7 %collective-permute-done.9.refs_6_ = bf16[384,1280]{1,0:T(8,128)(2,1)} collective-permute-done((bf16[384,1280]{1,0:T(8,128)(2,1)}, bf16[384,1280]{1,0:T(8,128)(2,1)}, u32[]{:S(2)}, u32[]{:S(2)}) %collective-permute-start.9) | collective-permute-done | bytes 983072 | tf_op jit(solution)/shard_map/ppermute | solution.py:422
  105.0 14.9 %shard_map.107.refs_0_ = f32[384,2048]{1,0:T(8,128)} custom-call(s32[1]{0:T(128)} %bitcast.here_ref._, s32[1]{0:T(128)} %bitcast.here_ref._, s32[1,1024]{1,0:T(1,128)} %bitcast.13, f32[32,1024]{1,0:T(8,128)} %get-tuple-element.72.refs_1_, bf16[1024,2048]{1,0:T(8,128)(2,1)} %bitcast.7, bf16[384,1280]{1,0:T(8,128)(2,1)} %copy-done.2, ...), custom_call_target="tpu_custom_call" | custom-call | flops 1048576 | bytes 65536 | tf_op jit(solution)/shard_map/pallas_call | solution.py:368
  119.8 3.4 %collective-permute-done.13.refs_2_ = bf16[384,1280]{1,0:T(8,128)(2,1)} collective-permute-done((bf16[384,1280]{1,0:T(8,128)(2,1)}, bf16[384,1280]{1,0:T(8,128)(2,1)}, u32[]{:S(2)}, u32[]{:S(2)}) %collective-permute-start.13) | collective-permute-done | bytes 983072 | tf_op jit(solution)/shard_map/ppermute | solution.py:422
  123.3 6.1 %shard_map.108._ = bf16[1024,2048]{1,0:T(8,128)(2,1)} custom-call(s32[1]{0:T(128)} %bitcast.here_ref._, s32[1]{0:T(128)} %bitcast.here_ref._, f32[384,2048]{1,0:T(8,128)} %shard_map.107.refs_0_, bf16[384,1280]{1,0:T(8,128)(2,1)} %copy-done.5, bf16[384,1280]{1,0:T(8,128)(2,1)} %collective-permute-done.13.refs_2_, bf16[2048,5120]{1,0:T(8,128)(2,1)} %refs_3_.5), custom_call_target="tpu_custom_call" | custom-call | flops 1048576 | bytes 65536 | tf_op jit(solution)/shard_map/pallas_call | solution.py:368
  129.4 2.2 %slice.24 = bf16[384,1280]{1,0:T(8,128)(2,1)} slice(bf16[640,1280]{1,0:T(8,128)(2,1)} %collective-permute-done.14.refs_5_), slice={[0:384], [0:1280]} | slice | bytes 1966080 | tf_op jit(solution)/shard_map/slice | solution.py:473
  132.9 2.0 slice.25
  136.4 4.5 %collective-permute-done.11.got_ref = bf16[256,3328]{1,0:T(8,128)(2,1)S(1)} collective-permute-done((bf16[256,3328]{1,0:T(8,128)(2,1)}, bf16[256,3328]{1,0:T(8,128)(2,1)S(1)}, u32[]{:S(2)}, u32[]{:S(2)}) %collective-permute-start.11) | collective-permute-done | bytes 1703968 | tf_op jit(solution)/shard_map/ppermute | solution.py:456
  142.1 4.6 %shard_map.106 = (f32[256,2048]{1,0:T(8,128)}, f32[256,1280]{1,0:T(8,128)}) custom-call(f32[256,3328]{1,0:T(8,128)} %get-tuple-element.66.keep_ref, bf16[256,3328]{1,0:T(8,128)(2,1)} %copy-done.3), custom_call_target="tpu_custom_call" | custom-call | flops 1048576 | bytes 65536 | tf_op jit(solution)/shard_map/pallas_call | solution.py:289
  146.7 11.7 %collective-permute-done.12.refs_6_ = bf16[640,1280]{1,0:T(8,128)(2,1)} collective-permute-done((bf16[640,1280]{1,0:T(8,128)(2,1)}, bf16[640,1280]{1,0:T(8,128)(2,1)}, u32[]{:S(2)}, u32[]{:S(2)}) %collective-permute-start.12) | collective-permute-done | bytes 1638432 | tf_op jit(solution)/shard_map/ppermute | solution.py:422
  158.4 20.0 %shard_map.109.refs_0_ = f32[640,2048]{1,0:T(8,128)} custom-call(s32[1]{0:T(128)} %bitcast.here_ref._, s32[1]{0:T(128)} %bitcast.here_ref._, s32[1,1024]{1,0:T(1,128)} %bitcast.14, f32[32,1024]{1,0:T(8,128)} %get-tuple-element.72.refs_1_, bf16[1024,2048]{1,0:T(8,128)(2,1)} %bitcast.8, bf16[640,1280]{1,0:T(8,128)(2,1)} %copy-done.1, ...), custom_call_target="tpu_custom_call" | custom-call | flops 1048576 | bytes 65536 | tf_op jit(solution)/shard_map/pallas_call | solution.py:368
  179.4 6.1 %shard_map.110._ = bf16[1024,2048]{1,0:T(8,128)(2,1)} custom-call(s32[1]{0:T(128)} %bitcast.here_ref._, bf16[1024,2048]{1,0:T(8,128)(2,1)} %shard_map.108._, f32[640,2048]{1,0:T(8,128)} %shard_map.109.refs_0_, bf16[640,1280]{1,0:T(8,128)(2,1)} %collective-permute-done.10.refs_1_, ...), custom_call_target="tpu_custom_call", output_to_operand_aliasing={{}: (1, {})} | custom-call | flops 1048576 | bytes 65536 | tf_op jit(solution)/shard_map/pallas_call | solution.py:368
  185.6 7.5 %collective-permute-done.16.refs_2_ = bf16[256,1280]{1,0:T(8,128)(2,1)} collective-permute-done((bf16[256,1280]{1,0:T(8,128)(2,1)}, bf16[256,1280]{1,0:T(8,128)(2,1)}, u32[]{:S(2)}, u32[]{:S(2)}) %collective-permute-start.16) | collective-permute-done | bytes 655392 | tf_op jit(solution)/shard_map/ppermute | solution.py:422
  193.1 5.2 %shard_map.111 = bf16[1024,2048]{1,0:T(8,128)(2,1)} custom-call(s32[1]{0:T(128)} %bitcast.here_ref._, bf16[1024,2048]{1,0:T(8,128)(2,1)} %shard_map.110._, f32[640,2048]{1,0:T(8,128)} %shard_map.109.refs_0_, bf16[640,1280]{1,0:T(8,128)(2,1)} %collective-permute-done.10.refs_1_, ...), custom_call_target="tpu_custom_call", output_to_operand_aliasing={{}: (1, {})} | custom-call | flops 1048576 | bytes 65536 | tf_op jit(solution)/shard_map/pallas_call | solution.py:368
  (56 shorter events, 26.2 us)
Async XLA Ops:
  1.9 16.0 %copy-start.2 = (bf16[384,1280]{1,0:T(8,128)(2,1)}, bf16[384,1280]{1,0:T(8,128)(2,1)S(1)}, u32[]{:S(2)}) copy-start(bf16[384,1280]{1,0:T(8,128)(2,1)S(1)} %slice.20.refs_3_) | copy-start | bytes 2949124
  1.9 27.7 %collective-permute-start = (bf16[384,1280]{1,0:T(8,128)(2,1)S(1)}, bf16[384,1280]{1,0:T(8,128)(2,1)}, u32[]{:S(2)}, u32[]{:S(2)}) collective-permute-start(bf16[384,1280]{1,0:T(8,128)(2,1)S(1)} %slice.20.refs_3_), channel_id=1, source_target_pairs={{0,4},{4,0},{8,12},{12,8},{1,5},{5,1},{9,13},{13,9},{2,6},{6,2},{1... | collective-permute-start | bytes 2949128 | tf_op jit(solution)/shard_map/ppermute | solution.py:416
  5.0 24.6 %collective-permute-start.1 = (bf16[384,1280]{1,0:T(8,128)(2,1)S(1)}, bf16[384,1280]{1,0:T(8,128)(2,1)S(1)}, u32[]{:S(2)}, u32[]{:S(2)}) collective-permute-start(bf16[384,1280]{1,0:T(8,128)(2,1)S(1)} %slice.20.refs_3_), channel_id=1, source_target_pairs={{4,8},{8,4},{5,9},{9,5},{6,10},{10,6},{7,11},{11,7},{20,24},{24,20... | collective-permute-start | bytes 2949128 | tf_op jit(solution)/shard_map/ppermute | solution.py:419
  17.9 11.7 %collective-permute-start.2 = (f32[32,1024]{1,0:T(8,128)}, f32[32,1024]{1,0:T(8,128)S(1)}, u32[]{:S(2)}, u32[]{:S(2)}) collective-permute-start(f32[32,1024]{1,0:T(8,128)} %shard_map.103), channel_id=1, source_target_pairs={{0,4},{4,0},{8,12},{12,8},{1,5},{5,1},{9,13},{13,9},{2,6},{6,2},{1... | collective-permute-start | bytes 393224 | tf_op jit(solution)/shard_map/ppermute | solution.py:416
  23.3 23.0 %copy-start = (bf16[1024,1280]{1,0:T(8,128)(2,1)S(1)}, bf16[1024,1280]{1,0:T(8,128)(2,1)}, u32[]{:S(2)}) copy-start(bf16[1024,1280]{1,0:T(8,128)(2,1)} %gradient_ref.3) | copy-start | bytes 7864324
  29.6 16.7 %copy-start.5 = (bf16[384,1280]{1,0:T(8,128)(2,1)}, bf16[384,1280]{1,0:T(8,128)(2,1)S(1)}, u32[]{:S(2)}) copy-start(bf16[384,1280]{1,0:T(8,128)(2,1)S(1)} %collective-permute-done.1.refs_1_) | copy-start | bytes 2949124
  29.6 15.0 %collective-permute-start.4 = (bf16[128,1280]{1,0:T(8,128)(2,1)S(1)}, bf16[128,1280]{1,0:T(8,128)(2,1)S(1)}, u32[]{:S(2)}, u32[]{:S(2)}) collective-permute-start(bf16[128,1280]{1,0:T(8,128)(2,1)S(1)} %slice.21), channel_id=1, source_target_pairs={{0,4},{4,0},{8,12},{12,8},{1,5},{5,1},{9,13},{13,9},{2,6},{6,2},{1... | collective-permute-start | bytes 983048 | tf_op jit(solution)/shard_map/ppermute | solution.py:416
  32.4 13.9 %copy-start.4 = (f32[32,1024]{1,0:T(8,128)}, f32[32,1024]{1,0:T(8,128)S(1)}, u32[]{:S(2)}) copy-start(f32[32,1024]{1,0:T(8,128)S(1)} %add.10.pair) | copy-start | bytes 393220
  32.5 0.7 collective-permute-start.3
  33.1 13.2 %copy-start.6 = (f32[32,1024]{1,0:T(8,128)}, f32[32,1024]{1,0:T(8,128)S(1)}, u32[]{:S(2)}) copy-start(f32[32,1024]{1,0:T(8,128)S(1)} %collective-permute-done.3.crossed) | copy-start | bytes 393220
  33.2 11.4 %collective-permute-start.5 = (f32[32,1024]{1,0:T(8,128)S(1)}, f32[32,1024]{1,0:T(8,128)S(1)}, u32[]{:S(2)}, u32[]{:S(2)}) collective-permute-start(f32[32,1024]{1,0:T(8,128)S(1)} %add.11), channel_id=1, source_target_pairs={{4,0},{8,12},{5,1},{9,13},{6,2},{10,14},{7,3},{11,15},{20,16},{24,... | collective-permute-start | bytes 393224 | tf_op jit(solution)/shard_map/ppermute | solution.py:422
  36.9 9.6 %copy-start.9 = (s32[4]{0:T(128)S(1)}, s32[4]{0:T(128)}, u32[]{:S(2)}) copy-start(s32[4]{0:T(128)} %constant.13.clone) | copy-start | bytes 52
  44.6 28.2 %collective-permute-start.6 = (bf16[512,1280]{1,0:T(8,128)(2,1)}, bf16[512,1280]{1,0:T(8,128)(2,1)}, u32[]{:S(2)}, u32[]{:S(2)}) collective-permute-start(bf16[512,1280]{1,0:T(8,128)(2,1)} %slice.22), channel_id=1, source_target_pairs={{0,4},{4,0},{8,12},{12,8},{1,5},{5,1},{9,13},{13,9},{2,6},{6,2},{1... | collective-permute-start | bytes 3932168 | tf_op jit(solution)/shard_map/ppermute | solution.py:416
  44.6 19.3 %collective-permute-start.7 = (bf16[384,1280]{1,0:T(8,128)(2,1)}, bf16[384,1280]{1,0:T(8,128)(2,1)}, u32[]{:S(2)}, u32[]{:S(2)}) collective-permute-start(bf16[384,1280]{1,0:T(8,128)(2,1)} %collective-permute-done.refs_4_), channel_id=1, source_target_pairs={{4,8},{8,4},{5,9},{9,5},{6,10},{10,6},{7,11},{11,7},{20,24},{24,20... | collective-permute-start | bytes 2949128 | tf_op jit(solution)/shard_map/ppermute | solution.py:419
  46.4 26.4 %copy-start.1 = (bf16[640,1280]{1,0:T(8,128)(2,1)}, bf16[640,1280]{1,0:T(8,128)(2,1)S(1)}, u32[]{:S(2)}) copy-start(bf16[640,1280]{1,0:T(8,128)(2,1)S(1)} %slice.23.refs_3_) | copy-start | bytes 4915204
  72.8 11.3 %collective-permute-start.8 = (f32[512,3328]{1,0:T(8,128)}, f32[512,3328]{1,0:T(8,128)}, u32[]{:S(2)}, u32[]{:S(2)}) collective-permute-start(f32[512,3328]{1,0:T(8,128)} %get-tuple-element.60), channel_id=1, source_target_pairs={{0,1},{1,0},{2,3},{3,2},{4,5},{5,4},{6,7},{7,6},{8,9},{9,8},{10,11... | collective-permute-start | bytes 20447240 | tf_op jit(solution)/shard_map/ppermute | solution.py:450
  72.8 29.4 %collective-permute-start.10 = (bf16[640,1280]{1,0:T(8,128)(2,1)S(1)}, bf16[640,1280]{1,0:T(8,128)(2,1)}, u32[]{:S(2)}, u32[]{:S(2)}) collective-permute-start(bf16[640,1280]{1,0:T(8,128)(2,1)S(1)} %slice.23.refs_3_), channel_id=1, source_target_pairs={{4,8},{8,4},{5,9},{9,5},{6,10},{10,6},{7,11},{11,7},{20,24},{24,20... | collective-permute-start | bytes 4915208 | tf_op jit(solution)/shard_map/ppermute | solution.py:419
  75.4 26.7 %collective-permute-start.9 = (bf16[384,1280]{1,0:T(8,128)(2,1)}, bf16[384,1280]{1,0:T(8,128)(2,1)}, u32[]{:S(2)}, u32[]{:S(2)}) collective-permute-start(bf16[384,1280]{1,0:T(8,128)(2,1)} %copy-done.5), channel_id=1, source_target_pairs={{4,0},{8,12},{5,1},{9,13},{6,2},{10,14},{7,3},{11,15},{20,16},{24,... | collective-permute-start | bytes 2949128 | tf_op jit(solution)/shard_map/ppermute | solution.py:422
  79.2 50.2 %collective-permute-start.14 = (bf16[640,1280]{1,0:T(8,128)(2,1)}, bf16[640,1280]{1,0:T(8,128)(2,1)}, u32[]{:S(2)}, u32[]{:S(2)}) collective-permute-start(bf16[640,1280]{1,0:T(8,128)(2,1)} %constant_dynamic-update-slice_fusion.refs_4_), channel_id=1, source_target_pairs={{4,8},{8,4},{5,9},{9,5},{6,10},{10,6},{7,11},{11,7},{20,24},{24,20... | collective-permute-start | bytes 4915208 | tf_op jit(solution)/shard_map/ppermute | solution.py:419
  81.1 42.1 %collective-permute-start.13 = (bf16[384,1280]{1,0:T(8,128)(2,1)}, bf16[384,1280]{1,0:T(8,128)(2,1)}, u32[]{:S(2)}, u32[]{:S(2)}) collective-permute-start(bf16[384,1280]{1,0:T(8,128)(2,1)} %collective-permute-done.7.refs_5_), channel_id=1, source_target_pairs={{4,0},{8,12},{5,1},{9,13},{6,2},{10,14},{7,3},{11,15},{20,16},{24,... | collective-permute-start | bytes 2949128 | tf_op jit(solution)/shard_map/ppermute | solution.py:422
  102.2 38.7 %collective-permute-start.11 = (bf16[256,3328]{1,0:T(8,128)(2,1)}, bf16[256,3328]{1,0:T(8,128)(2,1)S(1)}, u32[]{:S(2)}, u32[]{:S(2)}) collective-permute-start(bf16[256,3328]{1,0:T(8,128)(2,1)} %get-tuple-element.67), channel_id=1, source_target_pairs={{0,2},{1,3},{2,0},{3,1},{4,6},{5,7},{6,4},{7,5},{8,10},{9,11},{10,... | collective-permute-start | bytes 5111816 | tf_op jit(solution)/shard_map/ppermute | solution.py:456
  103.7 54.7 %collective-permute-start.12 = (bf16[640,1280]{1,0:T(8,128)(2,1)}, bf16[640,1280]{1,0:T(8,128)(2,1)}, u32[]{:S(2)}, u32[]{:S(2)}) collective-permute-start(bf16[640,1280]{1,0:T(8,128)(2,1)} %collective-permute-done.10.refs_1_), channel_id=1, source_target_pairs={{4,0},{8,12},{5,1},{9,13},{6,2},{10,14},{7,3},{11,15},{20,16},{24,... | collective-permute-start | bytes 4915208 | tf_op jit(solution)/shard_map/ppermute | solution.py:422
  131.6 47.8 %collective-permute-start.15 = (bf16[384,1280]{1,0:T(8,128)(2,1)}, bf16[384,1280]{1,0:T(8,128)(2,1)}, u32[]{:S(2)}, u32[]{:S(2)}) collective-permute-start(bf16[384,1280]{1,0:T(8,128)(2,1)} %slice.24), channel_id=1, source_target_pairs={{4,0},{8,12},{5,1},{9,13},{6,2},{10,14},{7,3},{11,15},{20,16},{24,... | collective-permute-start | bytes 2949128 | tf_op jit(solution)/shard_map/ppermute | solution.py:422
  134.9 58.2 %collective-permute-start.16 = (bf16[256,1280]{1,0:T(8,128)(2,1)}, bf16[256,1280]{1,0:T(8,128)(2,1)}, u32[]{:S(2)}, u32[]{:S(2)}) collective-permute-start(bf16[256,1280]{1,0:T(8,128)(2,1)} %slice.25), channel_id=1, source_target_pairs={{4,0},{8,12},{5,1},{9,13},{6,2},{10,14},{7,3},{11,15},{20,16},{24,... | collective-permute-start | bytes 1966088 | tf_op jit(solution)/shard_map/ppermute | solution.py:422
  (3 other events, 12.4 us)

commit v5 on v4

--- a/solution.py
+++ b/solution.py
@@ -10,7 +10,7 @@
 ADAPTER_SCALE = 2.0
 OBJECTIVE_WEIGHT = 0.05
 LAST_ROWS = 256
-PIECE = 128
+PIECE = 160
 FIRST_EIGHTHS = 3
 
 TO_ENDS = [(1, 0), (2, 3)]

time: 199 us -> 198 us (level)
  no operation moved by 1% of the time
where the time goes in v5:
time: 198 us
  Pallas kernels  92.1 us (47%)
  waiting for transfers between devices  61.8 us (31%)
  starting transfers between devices  25.7 us (13%)
  local copies, waits for them, and re-layouts  16.4 us (8%)
    pallas_call x5, Pallas kernels, add_products(): kernel_call(functools.partial(rows_kernel, distances, first if with_adapt...  52.3 us
    ppermute x6, waiting for transfers between devices, to_end(): return lax.ppermute(block, 'tensor', TO_ENDS)  43.2 us
    pallas_call x1, Pallas kernels, adapter_gradients(): kernel_call(adapter_gradient_kernel, grid_spec=pltpu.PrefetchScalarGridSp...  15.6 us
    ppermute x4, waiting for transfers between devices, swap(): return lax.ppermute(block, 'tensor', pairs(4, 1))  13.4 us
    pallas_call x1, Pallas kernels, low_rank(): kernel_call(functools.partial(low_rank_kernel, rank), grid=(4,), in_specs...  12.2 us
    ppermute x4, starting transfers between devices, swap(): return lax.ppermute(block, 'tensor', pairs(4, 1))  9.44 us
    ppermute x6, starting transfers between devices, to_end(): return lax.ppermute(block, 'tensor', TO_ENDS)  7.87 us
    pallas_call x1, Pallas kernels, add_in_halves(): kernel_call(halves_kernel, grid=(4,), in_specs=[both, both], out_specs=[p...  7.42 us
  transfers between devices with their start and end apart: 17, of which 10 were waited for; matrix products, arithmetic and copies ran while one was open for 7% of the time, Pallas kernels for 44%

profile of v5, /device:TPU:0, one launch (start us, length us, event | category | flops | bytes accessed | tf_op | source)
XLA Modules:
  0.0 197.7 jit_solution(7344972976331944868)
XLA Ops:
  1.9 3.1 %collective-permute-start = (bf16[384,1280]{1,0:T(8,128)(2,1)S(1)}, bf16[384,1280]{1,0:T(8,128)(2,1)}, u32[]{:S(2)}, u32[]{:S(2)}) collective-permute-start(bf16[384,1280]{1,0:T(8,128)(2,1)S(1)} %slice.20.refs_3_), channel_id=1, source_target_pairs={{0,4},{4,0},{8,12},{12,8},{1,5},{5,1},{9,13},{13,9},{2,6},{6,2},{1... | collective-permute-start | bytes 2949128 | tf_op jit(solution)/shard_map/ppermute | solution.py:416
  5.7 12.2 %shard_map.103 = f32[32,1024]{1,0:T(8,128)} custom-call(s32[1,1024]{1,0:T(1,128)} %bitcast.10, s32[1,1024]{1,0:T(1,128)} %bitcast.11, bf16[1024,2048]{1,0:T(8,128)(2,1)} %bitcast.6, bf16[1024,2048]{1,0:T(8,128)(2,1)} %values_ref.3, bf16[1024,1280]{1,0:T(8,128)(2,1)} %bitcast.9, bf16[1024,1280]{1,0:T(8,128)(2,1)} %gradient_ref.3), custom_call_target="tpu_custom_call" | custom-call | flops 1048576 | bytes 65536 | tf_op jit(solution)/shard_map/pallas_call | solution.py:166
  17.9 4.3 %collective-permute-start.2 = (f32[32,1024]{1,0:T(8,128)}, f32[32,1024]{1,0:T(8,128)S(1)}, u32[]{:S(2)}, u32[]{:S(2)}) collective-permute-start(f32[32,1024]{1,0:T(8,128)} %shard_map.103), channel_id=1, source_target_pairs={{0,4},{4,0},{8,12},{12,8},{1,5},{5,1},{9,13},{13,9},{2,6},{6,2},{1... | collective-permute-start | bytes 393224 | tf_op jit(solution)/shard_map/ppermute | solution.py:416
  23.3 6.3 %collective-permute-done.2 = f32[32,1024]{1,0:T(8,128)S(1)} collective-permute-done((f32[32,1024]{1,0:T(8,128)}, f32[32,1024]{1,0:T(8,128)S(1)}, u32[]{:S(2)}, u32[]{:S(2)}) %collective-permute-start.2) | collective-permute-done | bytes 131104 | tf_op jit(solution)/shard_map/ppermute | solution.py:416
  29.6 1.9 collective-permute-start.4
  34.5 2.4 %slice.22 = bf16[480,1280]{1,0:T(8,128)(2,1)} slice(bf16[1024,1280]{1,0:T(8,128)(2,1)} %gradient_ref.3), slice={[544:1024], [0:1280]} | slice | bytes 2457600 | tf_op jit(solution)/shard_map/slice | solution.py:430
  36.9 7.7 %collective-permute-done.5.from_middle = f32[32,1024]{1,0:T(8,128)S(1)} collective-permute-done((f32[32,1024]{1,0:T(8,128)S(1)}, f32[32,1024]{1,0:T(8,128)S(1)}, u32[]{:S(2)}, u32[]{:S(2)}) %collective-permute-start.5) | collective-permute-done | bytes 131104 | tf_op jit(solution)/shard_map/ppermute | solution.py:422
  48.4 15.6 %shard_map.104 = (f32[512,3328]{1,0:T(8,128)}, f32[512,3328]{1,0:T(8,128)}, f32[32,1024]{1,0:T(8,128)}) custom-call(s32[1]{0:T(128)} %bitcast.here_ref._, s32[1024,1]{1,0:T(8,128)} %broadcast_in_dim_reshape.4.slots_ref, s32[1,1024]{1,0:T(1,128)} %bitcast.12, f32[32,1024]{1,0:T(8,128)} %copy-done.4, f32[32,1024]{1,0:T(8,128)} %copy-done.6, ...), custom_call_target="tpu_custom_call" | custom-call | flops 1048576 | bytes 65536 | tf_op jit(solution)/shard_map/pallas_call | solution.py:226
  64.0 7.1 %collective-permute-done.6 = bf16[480,1280]{1,0:T(8,128)(2,1)} collective-permute-done((bf16[480,1280]{1,0:T(8,128)(2,1)}, bf16[480,1280]{1,0:T(8,128)(2,1)}, u32[]{:S(2)}, u32[]{:S(2)}) %collective-permute-start.6) | collective-permute-done | bytes 1228832 | tf_op jit(solution)/shard_map/ppermute | solution.py:416
  76.1 2.4 %constant_dynamic-update-slice_fusion.refs_4_ = bf16[640,1280]{1,0:T(8,128)(2,1)} fusion(bf16[640,1280]{1,0:T(8,128)(2,1)} %constant_dynamic-update-slice_fusion.1, bf16[480,1280]{1,0:T(8,128)(2,1)} %collective-permute-done.6), kind=kLoop, calls=%fused_computation.2 | loop fusion | bytes 2457600 | tf_op jit(solution)/shard_map/concatenate | solution.py:448
  82.4 7.4 %shard_map.105 = (bf16[256,3328]{1,0:T(8,128)(2,1)}, f32[256,3328]{1,0:T(8,128)}) custom-call(f32[512,3328]{1,0:T(8,128)} %get-tuple-element.59.keep_ref, f32[512,3328]{1,0:T(8,128)} %collective-permute-done.8.got_ref), custom_call_target="tpu_custom_call" | custom-call | flops 1048576 | bytes 65536 | tf_op jit(solution)/shard_map/pallas_call | solution.py:264
  89.8 11.8 %collective-permute-done.9.refs_6_ = bf16[384,1280]{1,0:T(8,128)(2,1)} collective-permute-done((bf16[384,1280]{1,0:T(8,128)(2,1)}, bf16[384,1280]{1,0:T(8,128)(2,1)}, u32[]{:S(2)}, u32[]{:S(2)}) %collective-permute-start.9) | collective-permute-done | bytes 983072 | tf_op jit(solution)/shard_map/ppermute | solution.py:422
  104.3 14.8 %shard_map.107.refs_0_ = f32[384,2048]{1,0:T(8,128)} custom-call(s32[1]{0:T(128)} %bitcast.here_ref._, s32[1]{0:T(128)} %bitcast.here_ref._, s32[1,1024]{1,0:T(1,128)} %bitcast.13, f32[32,1024]{1,0:T(8,128)} %get-tuple-element.72.refs_1_, bf16[1024,2048]{1,0:T(8,128)(2,1)} %bitcast.7, bf16[384,1280]{1,0:T(8,128)(2,1)} %copy-done.2, ...), custom_call_target="tpu_custom_call" | custom-call | flops 1048576 | bytes 65536 | tf_op jit(solution)/shard_map/pallas_call | solution.py:368
  119.1 3.5 %collective-permute-done.13.refs_2_ = bf16[384,1280]{1,0:T(8,128)(2,1)} collective-permute-done((bf16[384,1280]{1,0:T(8,128)(2,1)}, bf16[384,1280]{1,0:T(8,128)(2,1)}, u32[]{:S(2)}, u32[]{:S(2)}) %collective-permute-start.13) | collective-permute-done | bytes 983072 | tf_op jit(solution)/shard_map/ppermute | solution.py:422
  122.6 6.1 %shard_map.108._ = bf16[1024,2048]{1,0:T(8,128)(2,1)} custom-call(s32[1]{0:T(128)} %bitcast.here_ref._, s32[1]{0:T(128)} %bitcast.here_ref._, f32[384,2048]{1,0:T(8,128)} %shard_map.107.refs_0_, bf16[384,1280]{1,0:T(8,128)(2,1)} %copy-done.5, bf16[384,1280]{1,0:T(8,128)(2,1)} %collective-permute-done.13.refs_2_, bf16[2048,5120]{1,0:T(8,128)(2,1)} %refs_3_.5), custom_call_target="tpu_custom_call" | custom-call | flops 1048576 | bytes 65536 | tf_op jit(solution)/shard_map/pallas_call | solution.py:368
  128.8 2.2 %slice.24 = bf16[384,1280]{1,0:T(8,128)(2,1)} slice(bf16[640,1280]{1,0:T(8,128)(2,1)} %collective-permute-done.14.refs_5_), slice={[0:384], [0:1280]} | slice | bytes 1966080 | tf_op jit(solution)/shard_map/slice | solution.py:473
  132.3 2.0 slice.25
  135.7 4.5 %collective-permute-done.11.got_ref = bf16[256,3328]{1,0:T(8,128)(2,1)S(1)} collective-permute-done((bf16[256,3328]{1,0:T(8,128)(2,1)}, bf16[256,3328]{1,0:T(8,128)(2,1)S(1)}, u32[]{:S(2)}, u32[]{:S(2)}) %collective-permute-start.11) | collective-permute-done | bytes 1703968 | tf_op jit(solution)/shard_map/ppermute | solution.py:456
  141.4 4.6 %shard_map.106 = (f32[256,2048]{1,0:T(8,128)}, f32[256,1280]{1,0:T(8,128)}) custom-call(f32[256,3328]{1,0:T(8,128)} %get-tuple-element.66.keep_ref, bf16[256,3328]{1,0:T(8,128)(2,1)} %copy-done.3), custom_call_target="tpu_custom_call" | custom-call | flops 1048576 | bytes 65536 | tf_op jit(solution)/shard_map/pallas_call | solution.py:289
  146.1 11.7 %collective-permute-done.12.refs_6_ = bf16[640,1280]{1,0:T(8,128)(2,1)} collective-permute-done((bf16[640,1280]{1,0:T(8,128)(2,1)}, bf16[640,1280]{1,0:T(8,128)(2,1)}, u32[]{:S(2)}, u32[]{:S(2)}) %collective-permute-start.12) | collective-permute-done | bytes 1638432 | tf_op jit(solution)/shard_map/ppermute | solution.py:422
  157.7 19.9 %shard_map.109.refs_0_ = f32[640,2048]{1,0:T(8,128)} custom-call(s32[1]{0:T(128)} %bitcast.here_ref._, s32[1]{0:T(128)} %bitcast.here_ref._, s32[1,1024]{1,0:T(1,128)} %bitcast.14, f32[32,1024]{1,0:T(8,128)} %get-tuple-element.72.refs_1_, bf16[1024,2048]{1,0:T(8,128)(2,1)} %bitcast.8, bf16[640,1280]{1,0:T(8,128)(2,1)} %copy-done.1, ...), custom_call_target="tpu_custom_call" | custom-call | flops 1048576 | bytes 65536 | tf_op jit(solution)/shard_map/pallas_call | solution.py:368
  178.8 6.1 %shard_map.110._ = bf16[1024,2048]{1,0:T(8,128)(2,1)} custom-call(s32[1]{0:T(128)} %bitcast.here_ref._, bf16[1024,2048]{1,0:T(8,128)(2,1)} %shard_map.108._, f32[640,2048]{1,0:T(8,128)} %shard_map.109.refs_0_, bf16[640,1280]{1,0:T(8,128)(2,1)} %collective-permute-done.10.refs_1_, ...), custom_call_target="tpu_custom_call", output_to_operand_aliasing={{}: (1, {})} | custom-call | flops 1048576 | bytes 65536 | tf_op jit(solution)/shard_map/pallas_call | solution.py:368
  184.9 7.5 %collective-permute-done.16.refs_2_ = bf16[256,1280]{1,0:T(8,128)(2,1)} collective-permute-done((bf16[256,1280]{1,0:T(8,128)(2,1)}, bf16[256,1280]{1,0:T(8,128)(2,1)}, u32[]{:S(2)}, u32[]{:S(2)}) %collective-permute-start.16) | collective-permute-done | bytes 655392 | tf_op jit(solution)/shard_map/ppermute | solution.py:422
  192.4 5.2 %shard_map.111 = bf16[1024,2048]{1,0:T(8,128)(2,1)} custom-call(s32[1]{0:T(128)} %bitcast.here_ref._, bf16[1024,2048]{1,0:T(8,128)(2,1)} %shard_map.110._, f32[640,2048]{1,0:T(8,128)} %shard_map.109.refs_0_, bf16[640,1280]{1,0:T(8,128)(2,1)} %collective-permute-done.10.refs_1_, ...), custom_call_target="tpu_custom_call", output_to_operand_aliasing={{}: (1, {})} | custom-call | flops 1048576 | bytes 65536 | tf_op jit(solution)/shard_map/pallas_call | solution.py:368
  (58 shorter events, 26.5 us)
Async XLA Ops:
  1.9 16.0 %copy-start.2 = (bf16[384,1280]{1,0:T(8,128)(2,1)}, bf16[384,1280]{1,0:T(8,128)(2,1)S(1)}, u32[]{:S(2)}) copy-start(bf16[384,1280]{1,0:T(8,128)(2,1)S(1)} %slice.20.refs_3_) | copy-start | bytes 2949124
  1.9 27.7 %collective-permute-start = (bf16[384,1280]{1,0:T(8,128)(2,1)S(1)}, bf16[384,1280]{1,0:T(8,128)(2,1)}, u32[]{:S(2)}, u32[]{:S(2)}) collective-permute-start(bf16[384,1280]{1,0:T(8,128)(2,1)S(1)} %slice.20.refs_3_), channel_id=1, source_target_pairs={{0,4},{4,0},{8,12},{12,8},{1,5},{5,1},{9,13},{13,9},{2,6},{6,2},{1... | collective-permute-start | bytes 2949128 | tf_op jit(solution)/shard_map/ppermute | solution.py:416
  5.0 24.6 %collective-permute-start.1 = (bf16[384,1280]{1,0:T(8,128)(2,1)S(1)}, bf16[384,1280]{1,0:T(8,128)(2,1)S(1)}, u32[]{:S(2)}, u32[]{:S(2)}) collective-permute-start(bf16[384,1280]{1,0:T(8,128)(2,1)S(1)} %slice.20.refs_3_), channel_id=1, source_target_pairs={{4,8},{8,4},{5,9},{9,5},{6,10},{10,6},{7,11},{11,7},{20,24},{24,20... | collective-permute-start | bytes 2949128 | tf_op jit(solution)/shard_map/ppermute | solution.py:419
  17.9 11.7 %collective-permute-start.2 = (f32[32,1024]{1,0:T(8,128)}, f32[32,1024]{1,0:T(8,128)S(1)}, u32[]{:S(2)}, u32[]{:S(2)}) collective-permute-start(f32[32,1024]{1,0:T(8,128)} %shard_map.103), channel_id=1, source_target_pairs={{0,4},{4,0},{8,12},{12,8},{1,5},{5,1},{9,13},{13,9},{2,6},{6,2},{1... | collective-permute-start | bytes 393224 | tf_op jit(solution)/shard_map/ppermute | solution.py:416
  23.3 23.1 %copy-start = (bf16[1024,1280]{1,0:T(8,128)(2,1)S(1)}, bf16[1024,1280]{1,0:T(8,128)(2,1)}, u32[]{:S(2)}) copy-start(bf16[1024,1280]{1,0:T(8,128)(2,1)} %gradient_ref.3) | copy-start | bytes 7864324
  29.6 16.8 %copy-start.5 = (bf16[384,1280]{1,0:T(8,128)(2,1)}, bf16[384,1280]{1,0:T(8,128)(2,1)S(1)}, u32[]{:S(2)}) copy-start(bf16[384,1280]{1,0:T(8,128)(2,1)S(1)} %collective-permute-done.1.refs_1_) | copy-start | bytes 2949124
  29.6 15.0 %collective-permute-start.4 = (bf16[160,1280]{1,0:T(8,128)(2,1)S(1)}, bf16[160,1280]{1,0:T(8,128)(2,1)S(1)}, u32[]{:S(2)}, u32[]{:S(2)}) collective-permute-start(bf16[160,1280]{1,0:T(8,128)(2,1)S(1)} %slice.21), channel_id=1, source_target_pairs={{0,4},{4,0},{8,12},{12,8},{1,5},{5,1},{9,13},{13,9},{2,6},{6,2},{1... | collective-permute-start | bytes 1228808 | tf_op jit(solution)/shard_map/ppermute | solution.py:416
  32.4 14.0 %copy-start.4 = (f32[32,1024]{1,0:T(8,128)}, f32[32,1024]{1,0:T(8,128)S(1)}, u32[]{:S(2)}) copy-start(f32[32,1024]{1,0:T(8,128)S(1)} %add.10.pair) | copy-start | bytes 393220
  32.5 0.7 collective-permute-start.3
  33.1 13.3 %copy-start.6 = (f32[32,1024]{1,0:T(8,128)}, f32[32,1024]{1,0:T(8,128)S(1)}, u32[]{:S(2)}) copy-start(f32[32,1024]{1,0:T(8,128)S(1)} %collective-permute-done.3.crossed) | copy-start | bytes 393220
  33.2 11.4 %collective-permute-start.5 = (f32[32,1024]{1,0:T(8,128)S(1)}, f32[32,1024]{1,0:T(8,128)S(1)}, u32[]{:S(2)}, u32[]{:S(2)}) collective-permute-start(f32[32,1024]{1,0:T(8,128)S(1)} %add.11), channel_id=1, source_target_pairs={{4,0},{8,12},{5,1},{9,13},{6,2},{10,14},{7,3},{11,15},{20,16},{24,... | collective-permute-start | bytes 393224 | tf_op jit(solution)/shard_map/ppermute | solution.py:422
  36.9 9.7 %copy-start.10 = (s32[4]{0:T(128)S(1)}, s32[4]{0:T(128)}, u32[]{:S(2)}) copy-start(s32[4]{0:T(128)} %constant.13.clone) | copy-start | bytes 52
  44.6 26.5 %collective-permute-start.6 = (bf16[480,1280]{1,0:T(8,128)(2,1)}, bf16[480,1280]{1,0:T(8,128)(2,1)}, u32[]{:S(2)}, u32[]{:S(2)}) collective-permute-start(bf16[480,1280]{1,0:T(8,128)(2,1)} %slice.22), channel_id=1, source_target_pairs={{0,4},{4,0},{8,12},{12,8},{1,5},{5,1},{9,13},{13,9},{2,6},{6,2},{1... | collective-permute-start | bytes 3686408 | tf_op jit(solution)/shard_map/ppermute | solution.py:416
  44.6 19.4 %collective-permute-start.7 = (bf16[384,1280]{1,0:T(8,128)(2,1)}, bf16[384,1280]{1,0:T(8,128)(2,1)}, u32[]{:S(2)}, u32[]{:S(2)}) collective-permute-start(bf16[384,1280]{1,0:T(8,128)(2,1)} %collective-permute-done.refs_4_), channel_id=1, source_target_pairs={{4,8},{8,4},{5,9},{9,5},{6,10},{10,6},{7,11},{11,7},{20,24},{24,20... | collective-permute-start | bytes 2949128 | tf_op jit(solution)/shard_map/ppermute | solution.py:419
  46.5 24.6 %copy-start.1 = (bf16[640,1280]{1,0:T(8,128)(2,1)}, bf16[640,1280]{1,0:T(8,128)(2,1)S(1)}, u32[]{:S(2)}) copy-start(bf16[640,1280]{1,0:T(8,128)(2,1)S(1)} %slice.23.refs_3_) | copy-start | bytes 4915204
  71.1 11.3 %collective-permute-start.8 = (f32[512,3328]{1,0:T(8,128)}, f32[512,3328]{1,0:T(8,128)}, u32[]{:S(2)}, u32[]{:S(2)}) collective-permute-start(f32[512,3328]{1,0:T(8,128)} %get-tuple-element.60), channel_id=1, source_target_pairs={{0,1},{1,0},{2,3},{3,2},{4,5},{5,4},{6,7},{7,6},{8,9},{9,8},{10,11... | collective-permute-start | bytes 20447240 | tf_op jit(solution)/shard_map/ppermute | solution.py:450
  71.1 30.4 %collective-permute-start.10 = (bf16[640,1280]{1,0:T(8,128)(2,1)S(1)}, bf16[640,1280]{1,0:T(8,128)(2,1)}, u32[]{:S(2)}, u32[]{:S(2)}) collective-permute-start(bf16[640,1280]{1,0:T(8,128)(2,1)S(1)} %slice.23.refs_3_), channel_id=1, source_target_pairs={{4,8},{8,4},{5,9},{9,5},{6,10},{10,6},{7,11},{11,7},{20,24},{24,20... | collective-permute-start | bytes 4915208 | tf_op jit(solution)/shard_map/ppermute | solution.py:419
  74.8 26.7 %collective-permute-start.9 = (bf16[384,1280]{1,0:T(8,128)(2,1)}, bf16[384,1280]{1,0:T(8,128)(2,1)}, u32[]{:S(2)}, u32[]{:S(2)}) collective-permute-start(bf16[384,1280]{1,0:T(8,128)(2,1)} %copy-done.5), channel_id=1, source_target_pairs={{4,0},{8,12},{5,1},{9,13},{6,2},{10,14},{7,3},{11,15},{20,16},{24,... | collective-permute-start | bytes 2949128 | tf_op jit(solution)/shard_map/ppermute | solution.py:422
  78.5 50.3 %collective-permute-start.14 = (bf16[640,1280]{1,0:T(8,128)(2,1)}, bf16[640,1280]{1,0:T(8,128)(2,1)}, u32[]{:S(2)}, u32[]{:S(2)}) collective-permute-start(bf16[640,1280]{1,0:T(8,128)(2,1)} %constant_dynamic-update-slice_fusion.refs_4_), channel_id=1, source_target_pairs={{4,8},{8,4},{5,9},{9,5},{6,10},{10,6},{7,11},{11,7},{20,24},{24,20... | collective-permute-start | bytes 4915208 | tf_op jit(solution)/shard_map/ppermute | solution.py:419
  80.4 42.2 %collective-permute-start.13 = (bf16[384,1280]{1,0:T(8,128)(2,1)}, bf16[384,1280]{1,0:T(8,128)(2,1)}, u32[]{:S(2)}, u32[]{:S(2)}) collective-permute-start(bf16[384,1280]{1,0:T(8,128)(2,1)} %collective-permute-done.7.refs_5_), channel_id=1, source_target_pairs={{4,0},{8,12},{5,1},{9,13},{6,2},{10,14},{7,3},{11,15},{20,16},{24,... | collective-permute-start | bytes 2949128 | tf_op jit(solution)/shard_map/ppermute | solution.py:422
  101.5 38.7 %collective-permute-start.11 = (bf16[256,3328]{1,0:T(8,128)(2,1)}, bf16[256,3328]{1,0:T(8,128)(2,1)S(1)}, u32[]{:S(2)}, u32[]{:S(2)}) collective-permute-start(bf16[256,3328]{1,0:T(8,128)(2,1)} %get-tuple-element.67), channel_id=1, source_target_pairs={{0,2},{1,3},{2,0},{3,1},{4,6},{5,7},{6,4},{7,5},{8,10},{9,11},{10,... | collective-permute-start | bytes 5111816 | tf_op jit(solution)/shard_map/ppermute | solution.py:456
  103.0 54.7 %collective-permute-start.12 = (bf16[640,1280]{1,0:T(8,128)(2,1)}, bf16[640,1280]{1,0:T(8,128)(2,1)}, u32[]{:S(2)}, u32[]{:S(2)}) collective-permute-start(bf16[640,1280]{1,0:T(8,128)(2,1)} %collective-permute-done.10.refs_1_), channel_id=1, source_target_pairs={{4,0},{8,12},{5,1},{9,13},{6,2},{10,14},{7,3},{11,15},{20,16},{24,... | collective-permute-start | bytes 4915208 | tf_op jit(solution)/shard_map/ppermute | solution.py:422
  131.0 47.8 %collective-permute-start.15 = (bf16[384,1280]{1,0:T(8,128)(2,1)}, bf16[384,1280]{1,0:T(8,128)(2,1)}, u32[]{:S(2)}, u32[]{:S(2)}) collective-permute-start(bf16[384,1280]{1,0:T(8,128)(2,1)} %slice.24), channel_id=1, source_target_pairs={{4,0},{8,12},{5,1},{9,13},{6,2},{10,14},{7,3},{11,15},{20,16},{24,... | collective-permute-start | bytes 2949128 | tf_op jit(solution)/shard_map/ppermute | solution.py:422
  134.2 58.2 %collective-permute-start.16 = (bf16[256,1280]{1,0:T(8,128)(2,1)}, bf16[256,1280]{1,0:T(8,128)(2,1)}, u32[]{:S(2)}, u32[]{:S(2)}) collective-permute-start(bf16[256,1280]{1,0:T(8,128)(2,1)} %slice.25), channel_id=1, source_target_pairs={{4,0},{8,12},{5,1},{9,13},{6,2},{10,14},{7,3},{11,15},{20,16},{24,... | collective-permute-start | bytes 1966088 | tf_op jit(solution)/shard_map/ppermute | solution.py:422
  (4 other events, 18.6 us)

commit v6 on v5

--- a/solution.py
+++ b/solution.py
@@ -445,10 +445,12 @@
     send, keep, near_rest, far[0], across[0], own[1], index = together(
         send, keep, near_rest, far[0], across[0], own[1], index
     )
-    near[1] = jnp.concatenate([near_first, near_rest], axis=0)
     end_across[0], across[1] = to_end(across[0]), cross(own[1])
     got = lax.ppermute(send, "dp", pairs(4, FLIP_CORE))
-    end_far[0], far[1] = to_end(far[0]), cross(near[1])
+    end_far[0] = to_end(far[0])
+    got, near_first, near_rest = together(got, near_first, near_rest)
+    near[1] = jnp.concatenate([near_first, near_rest], axis=0)
+    far[1] = cross(near[1])
     to_x, keep = add_in_halves(keep, got)
     to_x, keep, end_across[0], across[1], index = together(
         to_x, keep, end_across[0], across[1], index

time: 198 us -> 197 us (level)
    ppermute x6, waiting for transfers between devices: 43.2 us -> 34 us  [to_end(): return lax.ppermute(block, 'tensor', TO_ENDS)]
    ppermute x1, waiting for transfers between devices: 0.66 us -> 8.1 us  [line_device(): got = lax.ppermute(send, 'dp', pairs(4, FLIP_CORE))]
  transfers between devices with their start and end apart: 17 -> 17, of which waited for: 10 -> 10; matrix products, arithmetic and copies ran while one was open for 7% -> 8% of each run, Pallas kernels for 44% -> 44%
where the time goes in v6:
time: 197 us; the launch traced here: 196 us
  Pallas kernels  92.1 us (47%)
  waiting for transfers between devices  59.9 us (30%)
  starting transfers between devices  25.6 us (13%)
  local copies, waits for them, and re-layouts  16.5 us (8%)
    pallas_call x5, Pallas kernels, add_products(): kernel_call(functools.partial(rows_kernel, distances, first if with_adapt...  52.3 us
    ppermute x6, waiting for transfers between devices, to_end(): return lax.ppermute(block, 'tensor', TO_ENDS)  34 us
    pallas_call x1, Pallas kernels, adapter_gradients(): kernel_call(adapter_gradient_kernel, grid_spec=pltpu.PrefetchScalarGridSp...  15.6 us
    ppermute x4, waiting for transfers between devices, swap(): return lax.ppermute(block, 'tensor', pairs(4, 1))  13.3 us
    pallas_call x1, Pallas kernels, low_rank(): kernel_call(functools.partial(low_rank_kernel, rank), grid=(4,), in_specs...  12.2 us
    ppermute x4, starting transfers between devices, swap(): return lax.ppermute(block, 'tensor', pairs(4, 1))  9.44 us
    ppermute x1, waiting for transfers between devices, line_device(): got = lax.ppermute(send, 'dp', pairs(4, FLIP_CORE))  8.1 us
    ppermute x6, starting transfers between devices, to_end(): return lax.ppermute(block, 'tensor', TO_ENDS)  7.87 us
  transfers between devices with their start and end apart: 17, of which 10 were waited for; matrix products, arithmetic and copies ran while one was open for 8% of the time, Pallas kernels for 44%

profile of v6, /device:TPU:0, one launch (start us, length us, event | category | flops | bytes accessed | tf_op | source)
XLA Modules:
  0.0 195.9 jit_solution(10677694303015858984)
XLA Ops:
  1.9 3.1 %collective-permute-start = (bf16[384,1280]{1,0:T(8,128)(2,1)S(1)}, bf16[384,1280]{1,0:T(8,128)(2,1)}, u32[]{:S(2)}, u32[]{:S(2)}) collective-permute-start(bf16[384,1280]{1,0:T(8,128)(2,1)S(1)} %slice.20.refs_3_), channel_id=1, source_target_pairs={{0,4},{4,0},{8,12},{12,8},{1,5},{5,1},{9,13},{13,9},{2,6},{6,2},{1... | collective-permute-start | bytes 2949128 | tf_op jit(solution)/shard_map/ppermute | solution.py:416
  5.7 12.2 %shard_map.103 = f32[32,1024]{1,0:T(8,128)} custom-call(s32[1,1024]{1,0:T(1,128)} %bitcast.10, s32[1,1024]{1,0:T(1,128)} %bitcast.11, bf16[1024,2048]{1,0:T(8,128)(2,1)} %bitcast.6, bf16[1024,2048]{1,0:T(8,128)(2,1)} %values_ref.3, bf16[1024,1280]{1,0:T(8,128)(2,1)} %bitcast.9, bf16[1024,1280]{1,0:T(8,128)(2,1)} %gradient_ref.3), custom_call_target="tpu_custom_call" | custom-call | flops 1048576 | bytes 65536 | tf_op jit(solution)/shard_map/pallas_call | solution.py:166
  17.9 4.3 %collective-permute-start.2 = (f32[32,1024]{1,0:T(8,128)}, f32[32,1024]{1,0:T(8,128)S(1)}, u32[]{:S(2)}, u32[]{:S(2)}) collective-permute-start(f32[32,1024]{1,0:T(8,128)} %shard_map.103), channel_id=1, source_target_pairs={{0,4},{4,0},{8,12},{12,8},{1,5},{5,1},{9,13},{13,9},{2,6},{6,2},{1... | collective-permute-start | bytes 393224 | tf_op jit(solution)/shard_map/ppermute | solution.py:416
  23.3 6.3 %collective-permute-done.2 = f32[32,1024]{1,0:T(8,128)S(1)} collective-permute-done((f32[32,1024]{1,0:T(8,128)}, f32[32,1024]{1,0:T(8,128)S(1)}, u32[]{:S(2)}, u32[]{:S(2)}) %collective-permute-start.2) | collective-permute-done | bytes 131104 | tf_op jit(solution)/shard_map/ppermute | solution.py:416
  34.5 2.4 %slice.22 = bf16[480,1280]{1,0:T(8,128)(2,1)} slice(bf16[1024,1280]{1,0:T(8,128)(2,1)} %gradient_ref.3), slice={[544:1024], [0:1280]} | slice | bytes 2457600 | tf_op jit(solution)/shard_map/slice | solution.py:430
  36.9 7.7 %collective-permute-done.5.from_middle = f32[32,1024]{1,0:T(8,128)S(1)} collective-permute-done((f32[32,1024]{1,0:T(8,128)S(1)}, f32[32,1024]{1,0:T(8,128)S(1)}, u32[]{:S(2)}, u32[]{:S(2)}) %collective-permute-start.5) | collective-permute-done | bytes 131104 | tf_op jit(solution)/shard_map/ppermute | solution.py:422
  48.4 15.6 %shard_map.104 = (f32[512,3328]{1,0:T(8,128)}, f32[512,3328]{1,0:T(8,128)}, f32[32,1024]{1,0:T(8,128)}) custom-call(s32[1]{0:T(128)} %bitcast.here_ref._, s32[1024,1]{1,0:T(8,128)} %broadcast_in_dim_reshape.4.slots_ref, s32[1,1024]{1,0:T(1,128)} %bitcast.12, f32[32,1024]{1,0:T(8,128)} %copy-done.4, f32[32,1024]{1,0:T(8,128)} %copy-done.6, ...), custom_call_target="tpu_custom_call" | custom-call | flops 1048576 | bytes 65536 | tf_op jit(solution)/shard_map/pallas_call | solution.py:226
  64.1 7.1 %collective-permute-done.6 = bf16[480,1280]{1,0:T(8,128)(2,1)} collective-permute-done((bf16[480,1280]{1,0:T(8,128)(2,1)}, bf16[480,1280]{1,0:T(8,128)(2,1)}, u32[]{:S(2)}, u32[]{:S(2)}) %collective-permute-start.6) | collective-permute-done | bytes 1228832 | tf_op jit(solution)/shard_map/ppermute | solution.py:416
  74.3 8.1 %collective-permute-done.8.got_ref = f32[512,3328]{1,0:T(8,128)} collective-permute-done((f32[512,3328]{1,0:T(8,128)}, f32[512,3328]{1,0:T(8,128)}, u32[]{:S(2)}, u32[]{:S(2)}) %collective-permute-start.8) | collective-permute-done | bytes 6815776 | tf_op jit(solution)/shard_map/ppermute | solution.py:449
  84.1 2.5 %constant_dynamic-update-slice_fusion.refs_4_ = bf16[640,1280]{1,0:T(8,128)(2,1)} fusion(bf16[640,1280]{1,0:T(8,128)(2,1)} %constant_dynamic-update-slice_fusion.1, bf16[480,1280]{1,0:T(8,128)(2,1)} %collective-permute-done.6), kind=kLoop, calls=%fused_computation.2 | loop fusion | bytes 2457600 | tf_op jit(solution)/shard_map/concatenate | solution.py:452
  89.8 7.4 %shard_map.105 = (bf16[256,3328]{1,0:T(8,128)(2,1)}, f32[256,3328]{1,0:T(8,128)}) custom-call(f32[512,3328]{1,0:T(8,128)} %get-tuple-element.62.keep_ref, f32[512,3328]{1,0:T(8,128)} %collective-permute-done.8.got_ref), custom_call_target="tpu_custom_call" | custom-call | flops 1048576 | bytes 65536 | tf_op jit(solution)/shard_map/pallas_call | solution.py:264
  97.2 2.5 %collective-permute-done.9.refs_6_ = bf16[384,1280]{1,0:T(8,128)(2,1)} collective-permute-done((bf16[384,1280]{1,0:T(8,128)(2,1)}, bf16[384,1280]{1,0:T(8,128)(2,1)}, u32[]{:S(2)}, u32[]{:S(2)}) %collective-permute-start.9) | collective-permute-done | bytes 983072 | tf_op jit(solution)/shard_map/ppermute | solution.py:422
  102.5 14.8 %shard_map.107.refs_0_ = f32[384,2048]{1,0:T(8,128)} custom-call(s32[1]{0:T(128)} %bitcast.here_ref._, s32[1]{0:T(128)} %bitcast.here_ref._, s32[1,1024]{1,0:T(1,128)} %bitcast.13, f32[32,1024]{1,0:T(8,128)} %get-tuple-element.78.refs_1_, bf16[1024,2048]{1,0:T(8,128)(2,1)} %bitcast.7, bf16[384,1280]{1,0:T(8,128)(2,1)} %copy-done.2, ...), custom_call_target="tpu_custom_call" | custom-call | flops 1048576 | bytes 65536 | tf_op jit(solution)/shard_map/pallas_call | solution.py:368
  117.3 3.5 %collective-permute-done.13.refs_2_ = bf16[384,1280]{1,0:T(8,128)(2,1)} collective-permute-done((bf16[384,1280]{1,0:T(8,128)(2,1)}, bf16[384,1280]{1,0:T(8,128)(2,1)}, u32[]{:S(2)}, u32[]{:S(2)}) %collective-permute-start.13) | collective-permute-done | bytes 983072 | tf_op jit(solution)/shard_map/ppermute | solution.py:422
  120.8 6.1 %shard_map.108._ = bf16[1024,2048]{1,0:T(8,128)(2,1)} custom-call(s32[1]{0:T(128)} %bitcast.here_ref._, s32[1]{0:T(128)} %bitcast.here_ref._, f32[384,2048]{1,0:T(8,128)} %shard_map.107.refs_0_, bf16[384,1280]{1,0:T(8,128)(2,1)} %copy-done.5, bf16[384,1280]{1,0:T(8,128)(2,1)} %collective-permute-done.13.refs_2_, bf16[2048,5120]{1,0:T(8,128)(2,1)} %refs_3_.5), custom_call_target="tpu_custom_call" | custom-call | flops 1048576 | bytes 65536 | tf_op jit(solution)/shard_map/pallas_call | solution.py:368
  126.9 2.2 %slice.24 = bf16[384,1280]{1,0:T(8,128)(2,1)} slice(bf16[640,1280]{1,0:T(8,128)(2,1)} %collective-permute-done.14.refs_5_), slice={[0:384], [0:1280]} | slice | bytes 1966080 | tf_op jit(solution)/shard_map/slice | solution.py:475
  130.4 2.0 %slice.25 = bf16[256,1280]{1,0:T(8,128)(2,1)} slice(bf16[640,1280]{1,0:T(8,128)(2,1)} %collective-permute-done.14.refs_5_), slice={[384:640], [0:1280]} | slice | bytes 1310720 | tf_op jit(solution)/shard_map/slice | solution.py:475
  133.9 4.4 %collective-permute-done.11.got_ref = bf16[256,3328]{1,0:T(8,128)(2,1)S(1)} collective-permute-done((bf16[256,3328]{1,0:T(8,128)(2,1)}, bf16[256,3328]{1,0:T(8,128)(2,1)S(1)}, u32[]{:S(2)}, u32[]{:S(2)}) %collective-permute-start.11) | collective-permute-done | bytes 1703968 | tf_op jit(solution)/shard_map/ppermute | solution.py:458
  139.6 4.6 %shard_map.106 = (f32[256,2048]{1,0:T(8,128)}, f32[256,1280]{1,0:T(8,128)}) custom-call(f32[256,3328]{1,0:T(8,128)} %get-tuple-element.72.keep_ref, bf16[256,3328]{1,0:T(8,128)(2,1)} %copy-done.3), custom_call_target="tpu_custom_call" | custom-call | flops 1048576 | bytes 65536 | tf_op jit(solution)/shard_map/pallas_call | solution.py:289
  144.2 11.7 %collective-permute-done.12.refs_6_ = bf16[640,1280]{1,0:T(8,128)(2,1)} collective-permute-done((bf16[640,1280]{1,0:T(8,128)(2,1)}, bf16[640,1280]{1,0:T(8,128)(2,1)}, u32[]{:S(2)}, u32[]{:S(2)}) %collective-permute-start.12) | collective-permute-done | bytes 1638432 | tf_op jit(solution)/shard_map/ppermute | solution.py:422
  155.9 19.9 %shard_map.109.refs_0_ = f32[640,2048]{1,0:T(8,128)} custom-call(s32[1]{0:T(128)} %bitcast.here_ref._, s32[1]{0:T(128)} %bitcast.here_ref._, s32[1,1024]{1,0:T(1,128)} %bitcast.14, f32[32,1024]{1,0:T(8,128)} %get-tuple-element.78.refs_1_, bf16[1024,2048]{1,0:T(8,128)(2,1)} %bitcast.8, bf16[640,1280]{1,0:T(8,128)(2,1)} %copy-done.1, ...), custom_call_target="tpu_custom_call" | custom-call | flops 1048576 | bytes 65536 | tf_op jit(solution)/shard_map/pallas_call | solution.py:368
  177.0 6.1 %shard_map.110._ = bf16[1024,2048]{1,0:T(8,128)(2,1)} custom-call(s32[1]{0:T(128)} %bitcast.here_ref._, bf16[1024,2048]{1,0:T(8,128)(2,1)} %shard_map.108._, f32[640,2048]{1,0:T(8,128)} %shard_map.109.refs_0_, bf16[640,1280]{1,0:T(8,128)(2,1)} %collective-permute-done.10.refs_1_, ...), custom_call_target="tpu_custom_call", output_to_operand_aliasing={{}: (1, {})} | custom-call | flops 1048576 | bytes 65536 | tf_op jit(solution)/shard_map/pallas_call | solution.py:368
  183.1 7.5 %collective-permute-done.16.refs_2_ = bf16[256,1280]{1,0:T(8,128)(2,1)} collective-permute-done((bf16[256,1280]{1,0:T(8,128)(2,1)}, bf16[256,1280]{1,0:T(8,128)(2,1)}, u32[]{:S(2)}, u32[]{:S(2)}) %collective-permute-start.16) | collective-permute-done | bytes 655392 | tf_op jit(solution)/shard_map/ppermute | solution.py:422
  190.6 5.2 %shard_map.111 = bf16[1024,2048]{1,0:T(8,128)(2,1)} custom-call(s32[1]{0:T(128)} %bitcast.here_ref._, bf16[1024,2048]{1,0:T(8,128)(2,1)} %shard_map.110._, f32[640,2048]{1,0:T(8,128)} %shard_map.109.refs_0_, bf16[640,1280]{1,0:T(8,128)(2,1)} %collective-permute-done.10.refs_1_, ...), custom_call_target="tpu_custom_call", output_to_operand_aliasing={{}: (1, {})} | custom-call | flops 1048576 | bytes 65536 | tf_op jit(solution)/shard_map/pallas_call | solution.py:368
  (58 shorter events, 27.6 us)
Async XLA Ops:
  1.9 16.0 %copy-start.2 = (bf16[384,1280]{1,0:T(8,128)(2,1)}, bf16[384,1280]{1,0:T(8,128)(2,1)S(1)}, u32[]{:S(2)}) copy-start(bf16[384,1280]{1,0:T(8,128)(2,1)S(1)} %slice.20.refs_3_) | copy-start | bytes 2949124
  1.9 27.7 %collective-permute-start = (bf16[384,1280]{1,0:T(8,128)(2,1)S(1)}, bf16[384,1280]{1,0:T(8,128)(2,1)}, u32[]{:S(2)}, u32[]{:S(2)}) collective-permute-start(bf16[384,1280]{1,0:T(8,128)(2,1)S(1)} %slice.20.refs_3_), channel_id=1, source_target_pairs={{0,4},{4,0},{8,12},{12,8},{1,5},{5,1},{9,13},{13,9},{2,6},{6,2},{1... | collective-permute-start | bytes 2949128 | tf_op jit(solution)/shard_map/ppermute | solution.py:416
  5.0 24.6 %collective-permute-start.1 = (bf16[384,1280]{1,0:T(8,128)(2,1)S(1)}, bf16[384,1280]{1,0:T(8,128)(2,1)S(1)}, u32[]{:S(2)}, u32[]{:S(2)}) collective-permute-start(bf16[384,1280]{1,0:T(8,128)(2,1)S(1)} %slice.20.refs_3_), channel_id=1, source_target_pairs={{4,8},{8,4},{5,9},{9,5},{6,10},{10,6},{7,11},{11,7},{20,24},{24,20... | collective-permute-start | bytes 2949128 | tf_op jit(solution)/shard_map/ppermute | solution.py:419
  17.9 11.7 %collective-permute-start.2 = (f32[32,1024]{1,0:T(8,128)}, f32[32,1024]{1,0:T(8,128)S(1)}, u32[]{:S(2)}, u32[]{:S(2)}) collective-permute-start(f32[32,1024]{1,0:T(8,128)} %shard_map.103), channel_id=1, source_target_pairs={{0,4},{4,0},{8,12},{12,8},{1,5},{5,1},{9,13},{13,9},{2,6},{6,2},{1... | collective-permute-start | bytes 393224 | tf_op jit(solution)/shard_map/ppermute | solution.py:416
  23.3 23.0 %copy-start = (bf16[1024,1280]{1,0:T(8,128)(2,1)S(1)}, bf16[1024,1280]{1,0:T(8,128)(2,1)}, u32[]{:S(2)}) copy-start(bf16[1024,1280]{1,0:T(8,128)(2,1)} %gradient_ref.3) | copy-start | bytes 7864324
  29.6 16.7 %copy-start.5 = (bf16[384,1280]{1,0:T(8,128)(2,1)}, bf16[384,1280]{1,0:T(8,128)(2,1)S(1)}, u32[]{:S(2)}) copy-start(bf16[384,1280]{1,0:T(8,128)(2,1)S(1)} %collective-permute-done.1.refs_1_) | copy-start | bytes 2949124
  29.6 15.0 %collective-permute-start.4 = (bf16[160,1280]{1,0:T(8,128)(2,1)S(1)}, bf16[160,1280]{1,0:T(8,128)(2,1)S(1)}, u32[]{:S(2)}, u32[]{:S(2)}) collective-permute-start(bf16[160,1280]{1,0:T(8,128)(2,1)S(1)} %slice.21), channel_id=1, source_target_pairs={{0,4},{4,0},{8,12},{12,8},{1,5},{5,1},{9,13},{13,9},{2,6},{6,2},{1... | collective-permute-start | bytes 1228808 | tf_op jit(solution)/shard_map/ppermute | solution.py:416
  32.4 14.0 %copy-start.4 = (f32[32,1024]{1,0:T(8,128)}, f32[32,1024]{1,0:T(8,128)S(1)}, u32[]{:S(2)}) copy-start(f32[32,1024]{1,0:T(8,128)S(1)} %add.10.pair) | copy-start | bytes 393220
  32.5 0.7 collective-permute-start.3
  33.1 13.3 %copy-start.6 = (f32[32,1024]{1,0:T(8,128)}, f32[32,1024]{1,0:T(8,128)S(1)}, u32[]{:S(2)}) copy-start(f32[32,1024]{1,0:T(8,128)S(1)} %collective-permute-done.3.crossed) | copy-start | bytes 393220
  33.2 11.4 %collective-permute-start.5 = (f32[32,1024]{1,0:T(8,128)S(1)}, f32[32,1024]{1,0:T(8,128)S(1)}, u32[]{:S(2)}, u32[]{:S(2)}) collective-permute-start(f32[32,1024]{1,0:T(8,128)S(1)} %add.11), channel_id=1, source_target_pairs={{4,0},{8,12},{5,1},{9,13},{6,2},{10,14},{7,3},{11,15},{20,16},{24,... | collective-permute-start | bytes 393224 | tf_op jit(solution)/shard_map/ppermute | solution.py:422
  36.9 9.7 %copy-start.10 = (s32[4]{0:T(128)S(1)}, s32[4]{0:T(128)}, u32[]{:S(2)}) copy-start(s32[4]{0:T(128)} %constant.13.clone) | copy-start | bytes 52
  44.6 26.5 %collective-permute-start.6 = (bf16[480,1280]{1,0:T(8,128)(2,1)}, bf16[480,1280]{1,0:T(8,128)(2,1)}, u32[]{:S(2)}, u32[]{:S(2)}) collective-permute-start(bf16[480,1280]{1,0:T(8,128)(2,1)} %slice.22), channel_id=1, source_target_pairs={{0,4},{4,0},{8,12},{12,8},{1,5},{5,1},{9,13},{13,9},{2,6},{6,2},{1... | collective-permute-start | bytes 3686408 | tf_op jit(solution)/shard_map/ppermute | solution.py:416
  44.6 19.4 %collective-permute-start.7 = (bf16[384,1280]{1,0:T(8,128)(2,1)}, bf16[384,1280]{1,0:T(8,128)(2,1)}, u32[]{:S(2)}, u32[]{:S(2)}) collective-permute-start(bf16[384,1280]{1,0:T(8,128)(2,1)} %collective-permute-done.refs_4_), channel_id=1, source_target_pairs={{4,8},{8,4},{5,9},{9,5},{6,10},{10,6},{7,11},{11,7},{20,24},{24,20... | collective-permute-start | bytes 2949128 | tf_op jit(solution)/shard_map/ppermute | solution.py:419
  46.4 24.7 %copy-start.1 = (bf16[640,1280]{1,0:T(8,128)(2,1)}, bf16[640,1280]{1,0:T(8,128)(2,1)S(1)}, u32[]{:S(2)}) copy-start(bf16[640,1280]{1,0:T(8,128)(2,1)S(1)} %slice.23.refs_3_) | copy-start | bytes 4915204
  71.1 11.3 %collective-permute-start.8 = (f32[512,3328]{1,0:T(8,128)}, f32[512,3328]{1,0:T(8,128)}, u32[]{:S(2)}, u32[]{:S(2)}) collective-permute-start(f32[512,3328]{1,0:T(8,128)} %get-tuple-element.63), channel_id=1, source_target_pairs={{0,1},{1,0},{2,3},{3,2},{4,5},{5,4},{6,7},{7,6},{8,9},{9,8},{10,11... | collective-permute-start | bytes 20447240 | tf_op jit(solution)/shard_map/ppermute | solution.py:449
  71.1 28.6 %collective-permute-start.10 = (bf16[640,1280]{1,0:T(8,128)(2,1)S(1)}, bf16[640,1280]{1,0:T(8,128)(2,1)}, u32[]{:S(2)}, u32[]{:S(2)}) collective-permute-start(bf16[640,1280]{1,0:T(8,128)(2,1)S(1)} %slice.23.refs_3_), channel_id=1, source_target_pairs={{4,8},{8,4},{5,9},{9,5},{6,10},{10,6},{7,11},{11,7},{20,24},{24,20... | collective-permute-start | bytes 4915208 | tf_op jit(solution)/shard_map/ppermute | solution.py:419
  73.0 26.7 %collective-permute-start.9 = (bf16[384,1280]{1,0:T(8,128)(2,1)}, bf16[384,1280]{1,0:T(8,128)(2,1)}, u32[]{:S(2)}, u32[]{:S(2)}) collective-permute-start(bf16[384,1280]{1,0:T(8,128)(2,1)} %copy-done.5), channel_id=1, source_target_pairs={{4,0},{8,12},{5,1},{9,13},{6,2},{10,14},{7,3},{11,15},{20,16},{24,... | collective-permute-start | bytes 2949128 | tf_op jit(solution)/shard_map/ppermute | solution.py:422
  86.7 40.3 %collective-permute-start.14 = (bf16[640,1280]{1,0:T(8,128)(2,1)}, bf16[640,1280]{1,0:T(8,128)(2,1)}, u32[]{:S(2)}, u32[]{:S(2)}) collective-permute-start(bf16[640,1280]{1,0:T(8,128)(2,1)} %constant_dynamic-update-slice_fusion.refs_4_), channel_id=1, source_target_pairs={{4,8},{8,4},{5,9},{9,5},{6,10},{10,6},{7,11},{11,7},{20,24},{24,20... | collective-permute-start | bytes 4915208 | tf_op jit(solution)/shard_map/ppermute | solution.py:419
  88.5 32.3 %collective-permute-start.13 = (bf16[384,1280]{1,0:T(8,128)(2,1)}, bf16[384,1280]{1,0:T(8,128)(2,1)}, u32[]{:S(2)}, u32[]{:S(2)}) collective-permute-start(bf16[384,1280]{1,0:T(8,128)(2,1)} %collective-permute-done.7.refs_5_), channel_id=1, source_target_pairs={{4,0},{8,12},{5,1},{9,13},{6,2},{10,14},{7,3},{11,15},{20,16},{24,... | collective-permute-start | bytes 2949128 | tf_op jit(solution)/shard_map/ppermute | solution.py:422
  99.7 38.7 %collective-permute-start.11 = (bf16[256,3328]{1,0:T(8,128)(2,1)}, bf16[256,3328]{1,0:T(8,128)(2,1)S(1)}, u32[]{:S(2)}, u32[]{:S(2)}) collective-permute-start(bf16[256,3328]{1,0:T(8,128)(2,1)} %get-tuple-element.73), channel_id=1, source_target_pairs={{0,2},{1,3},{2,0},{3,1},{4,6},{5,7},{6,4},{7,5},{8,10},{9,11},{10,... | collective-permute-start | bytes 5111816 | tf_op jit(solution)/shard_map/ppermute | solution.py:458
  101.2 54.7 %collective-permute-start.12 = (bf16[640,1280]{1,0:T(8,128)(2,1)}, bf16[640,1280]{1,0:T(8,128)(2,1)}, u32[]{:S(2)}, u32[]{:S(2)}) collective-permute-start(bf16[640,1280]{1,0:T(8,128)(2,1)} %collective-permute-done.10.refs_1_), channel_id=1, source_target_pairs={{4,0},{8,12},{5,1},{9,13},{6,2},{10,14},{7,3},{11,15},{20,16},{24,... | collective-permute-start | bytes 4915208 | tf_op jit(solution)/shard_map/ppermute | solution.py:422
  129.2 47.8 %collective-permute-start.15 = (bf16[384,1280]{1,0:T(8,128)(2,1)}, bf16[384,1280]{1,0:T(8,128)(2,1)}, u32[]{:S(2)}, u32[]{:S(2)}) collective-permute-start(bf16[384,1280]{1,0:T(8,128)(2,1)} %slice.24), channel_id=1, source_target_pairs={{4,0},{8,12},{5,1},{9,13},{6,2},{10,14},{7,3},{11,15},{20,16},{24,... | collective-permute-start | bytes 2949128 | tf_op jit(solution)/shard_map/ppermute | solution.py:422
  132.5 58.2 %collective-permute-start.16 = (bf16[256,1280]{1,0:T(8,128)(2,1)}, bf16[256,1280]{1,0:T(8,128)(2,1)}, u32[]{:S(2)}, u32[]{:S(2)}) collective-permute-start(bf16[256,1280]{1,0:T(8,128)(2,1)} %slice.25), channel_id=1, source_target_pairs={{4,0},{8,12},{5,1},{9,13},{6,2},{10,14},{7,3},{11,15},{20,16},{24,... | collective-permute-start | bytes 1966088 | tf_op jit(solution)/shard_map/ppermute | solution.py:422
  (4 other events, 18.5 us)

commit v7 on v6

--- a/solution.py
+++ b/solution.py
@@ -10,7 +10,7 @@
 ADAPTER_SCALE = 2.0
 OBJECTIVE_WEIGHT = 0.05
 LAST_ROWS = 256
-PIECE = 160
+PIECE = 192
 FIRST_EIGHTHS = 3
 
 TO_ENDS = [(1, 0), (2, 3)]

time: 197 us -> 197 us (level)
  no operation moved by 1% of the time
where the time goes in v7:
time: 197 us; the launch traced here: 196 us
  Pallas kernels  92.1 us (47%)
  waiting for transfers between devices  60 us (30%)
  starting transfers between devices  25.5 us (13%)
  local copies, waits for them, and re-layouts  16.5 us (8%)
    pallas_call x5, Pallas kernels, add_products(): kernel_call(functools.partial(rows_kernel, distances, first if with_adapt...  52.3 us
    ppermute x6, waiting for transfers between devices, to_end(): return lax.ppermute(block, 'tensor', TO_ENDS)  34.4 us
    pallas_call x1, Pallas kernels, adapter_gradients(): kernel_call(adapter_gradient_kernel, grid_spec=pltpu.PrefetchScalarGridSp...  15.7 us
    ppermute x4, waiting for transfers between devices, swap(): return lax.ppermute(block, 'tensor', pairs(4, 1))  13 us
    pallas_call x1, Pallas kernels, low_rank(): kernel_call(functools.partial(low_rank_kernel, rank), grid=(4,), in_specs...  12.2 us
    ppermute x4, starting transfers between devices, swap(): return lax.ppermute(block, 'tensor', pairs(4, 1))  9.44 us
    ppermute x1, waiting for transfers between devices, line_device(): got = lax.ppermute(send, 'dp', pairs(4, FLIP_CORE))  8.1 us
    ppermute x6, starting transfers between devices, to_end(): return lax.ppermute(block, 'tensor', TO_ENDS)  7.87 us
  transfers between devices with their start and end apart: 17, of which 10 were waited for; matrix products, arithmetic and copies ran while one was open for 8% of the time, Pallas kernels for 44%

profile of v7, /device:TPU:0, one launch (start us, length us, event | category | flops | bytes accessed | tf_op | source)
XLA Modules:
  0.0 195.9 jit_solution(584587486093343680)
XLA Ops:
  1.9 3.1 %collective-permute-start = (bf16[384,1280]{1,0:T(8,128)(2,1)S(1)}, bf16[384,1280]{1,0:T(8,128)(2,1)}, u32[]{:S(2)}, u32[]{:S(2)}) collective-permute-start(bf16[384,1280]{1,0:T(8,128)(2,1)S(1)} %slice.20.refs_3_), channel_id=1, source_target_pairs={{0,4},{4,0},{8,12},{12,8},{1,5},{5,1},{9,13},{13,9},{2,6},{6,2},{1... | collective-permute-start | bytes 2949128 | tf_op jit(solution)/shard_map/ppermute | solution.py:416
  5.7 12.2 %shard_map.103 = f32[32,1024]{1,0:T(8,128)} custom-call(s32[1,1024]{1,0:T(1,128)} %bitcast.10, s32[1,1024]{1,0:T(1,128)} %bitcast.11, bf16[1024,2048]{1,0:T(8,128)(2,1)} %bitcast.6, bf16[1024,2048]{1,0:T(8,128)(2,1)} %values_ref.3, bf16[1024,1280]{1,0:T(8,128)(2,1)} %bitcast.9, bf16[1024,1280]{1,0:T(8,128)(2,1)} %gradient_ref.3), custom_call_target="tpu_custom_call" | custom-call | flops 1048576 | bytes 65536 | tf_op jit(solution)/shard_map/pallas_call | solution.py:166
  17.9 4.3 %collective-permute-start.2 = (f32[32,1024]{1,0:T(8,128)}, f32[32,1024]{1,0:T(8,128)S(1)}, u32[]{:S(2)}, u32[]{:S(2)}) collective-permute-start(f32[32,1024]{1,0:T(8,128)} %shard_map.103), channel_id=1, source_target_pairs={{0,4},{4,0},{8,12},{12,8},{1,5},{5,1},{9,13},{13,9},{2,6},{6,2},{1... | collective-permute-start | bytes 393224 | tf_op jit(solution)/shard_map/ppermute | solution.py:416
  23.3 6.2 %collective-permute-done.2 = f32[32,1024]{1,0:T(8,128)S(1)} collective-permute-done((f32[32,1024]{1,0:T(8,128)}, f32[32,1024]{1,0:T(8,128)S(1)}, u32[]{:S(2)}, u32[]{:S(2)}) %collective-permute-start.2) | collective-permute-done | bytes 131104 | tf_op jit(solution)/shard_map/ppermute | solution.py:416
  34.5 2.3 %slice.22 = bf16[448,1280]{1,0:T(8,128)(2,1)} slice(bf16[1024,1280]{1,0:T(8,128)(2,1)} %gradient_ref.3), slice={[576:1024], [0:1280]} | slice | bytes 2293760 | tf_op jit(solution)/shard_map/slice | solution.py:430
  36.8 8.0 %collective-permute-done.5.from_middle = f32[32,1024]{1,0:T(8,128)S(1)} collective-permute-done((f32[32,1024]{1,0:T(8,128)S(1)}, f32[32,1024]{1,0:T(8,128)S(1)}, u32[]{:S(2)}, u32[]{:S(2)}) %collective-permute-start.5) | collective-permute-done | bytes 131104 | tf_op jit(solution)/shard_map/ppermute | solution.py:422
  48.7 15.7 %shard_map.104 = (f32[512,3328]{1,0:T(8,128)}, f32[512,3328]{1,0:T(8,128)}, f32[32,1024]{1,0:T(8,128)}) custom-call(s32[1]{0:T(128)} %bitcast.here_ref._, s32[1024,1]{1,0:T(8,128)} %broadcast_in_dim_reshape.4.slots_ref, s32[1,1024]{1,0:T(1,128)} %bitcast.12, f32[32,1024]{1,0:T(8,128)} %copy-done.4, f32[32,1024]{1,0:T(8,128)} %copy-done.6, ...), custom_call_target="tpu_custom_call" | custom-call | flops 1048576 | bytes 65536 | tf_op jit(solution)/shard_map/pallas_call | solution.py:226
  64.4 6.8 %collective-permute-done.6 = bf16[448,1280]{1,0:T(8,128)(2,1)} collective-permute-done((bf16[448,1280]{1,0:T(8,128)(2,1)}, bf16[448,1280]{1,0:T(8,128)(2,1)}, u32[]{:S(2)}, u32[]{:S(2)}) %collective-permute-start.6) | collective-permute-done | bytes 1146912 | tf_op jit(solution)/shard_map/ppermute | solution.py:416
  74.3 8.1 %collective-permute-done.8.got_ref = f32[512,3328]{1,0:T(8,128)} collective-permute-done((f32[512,3328]{1,0:T(8,128)}, f32[512,3328]{1,0:T(8,128)}, u32[]{:S(2)}, u32[]{:S(2)}) %collective-permute-start.8) | collective-permute-done | bytes 6815776 | tf_op jit(solution)/shard_map/ppermute | solution.py:449
  84.2 2.5 %constant_dynamic-update-slice_fusion.refs_4_ = bf16[640,1280]{1,0:T(8,128)(2,1)} fusion(bf16[640,1280]{1,0:T(8,128)(2,1)} %constant_dynamic-update-slice_fusion.1, bf16[448,1280]{1,0:T(8,128)(2,1)} %collective-permute-done.6), kind=kLoop, calls=%fused_computation.2 | loop fusion | bytes 2293760 | tf_op jit(solution)/shard_map/concatenate | solution.py:452
  89.8 7.4 %shard_map.105 = (bf16[256,3328]{1,0:T(8,128)(2,1)}, f32[256,3328]{1,0:T(8,128)}) custom-call(f32[512,3328]{1,0:T(8,128)} %get-tuple-element.62.keep_ref, f32[512,3328]{1,0:T(8,128)} %collective-permute-done.8.got_ref), custom_call_target="tpu_custom_call" | custom-call | flops 1048576 | bytes 65536 | tf_op jit(solution)/shard_map/pallas_call | solution.py:264
  97.2 2.5 %collective-permute-done.9.refs_6_ = bf16[384,1280]{1,0:T(8,128)(2,1)} collective-permute-done((bf16[384,1280]{1,0:T(8,128)(2,1)}, bf16[384,1280]{1,0:T(8,128)(2,1)}, u32[]{:S(2)}, u32[]{:S(2)}) %collective-permute-start.9) | collective-permute-done | bytes 983072 | tf_op jit(solution)/shard_map/ppermute | solution.py:422
  102.4 14.8 %shard_map.107.refs_0_ = f32[384,2048]{1,0:T(8,128)} custom-call(s32[1]{0:T(128)} %bitcast.here_ref._, s32[1]{0:T(128)} %bitcast.here_ref._, s32[1,1024]{1,0:T(1,128)} %bitcast.13, f32[32,1024]{1,0:T(8,128)} %get-tuple-element.78.refs_1_, bf16[1024,2048]{1,0:T(8,128)(2,1)} %bitcast.7, bf16[384,1280]{1,0:T(8,128)(2,1)} %copy-done.2, ...), custom_call_target="tpu_custom_call" | custom-call | flops 1048576 | bytes 65536 | tf_op jit(solution)/shard_map/pallas_call | solution.py:368
  117.2 3.5 %collective-permute-done.13.refs_2_ = bf16[384,1280]{1,0:T(8,128)(2,1)} collective-permute-done((bf16[384,1280]{1,0:T(8,128)(2,1)}, bf16[384,1280]{1,0:T(8,128)(2,1)}, u32[]{:S(2)}, u32[]{:S(2)}) %collective-permute-start.13) | collective-permute-done | bytes 983072 | tf_op jit(solution)/shard_map/ppermute | solution.py:422
  120.8 6.2 %shard_map.108._ = bf16[1024,2048]{1,0:T(8,128)(2,1)} custom-call(s32[1]{0:T(128)} %bitcast.here_ref._, s32[1]{0:T(128)} %bitcast.here_ref._, f32[384,2048]{1,0:T(8,128)} %shard_map.107.refs_0_, bf16[384,1280]{1,0:T(8,128)(2,1)} %copy-done.5, bf16[384,1280]{1,0:T(8,128)(2,1)} %collective-permute-done.13.refs_2_, bf16[2048,5120]{1,0:T(8,128)(2,1)} %refs_3_.5), custom_call_target="tpu_custom_call" | custom-call | flops 1048576 | bytes 65536 | tf_op jit(solution)/shard_map/pallas_call | solution.py:368
  126.9 2.2 %slice.24 = bf16[384,1280]{1,0:T(8,128)(2,1)} slice(bf16[640,1280]{1,0:T(8,128)(2,1)} %collective-permute-done.14.refs_5_), slice={[0:384], [0:1280]} | slice | bytes 1966080 | tf_op jit(solution)/shard_map/slice | solution.py:475
  130.5 2.0 %slice.25 = bf16[256,1280]{1,0:T(8,128)(2,1)} slice(bf16[640,1280]{1,0:T(8,128)(2,1)} %collective-permute-done.14.refs_5_), slice={[384:640], [0:1280]} | slice | bytes 1310720 | tf_op jit(solution)/shard_map/slice | solution.py:475
  133.9 4.4 %collective-permute-done.11.got_ref = bf16[256,3328]{1,0:T(8,128)(2,1)S(1)} collective-permute-done((bf16[256,3328]{1,0:T(8,128)(2,1)}, bf16[256,3328]{1,0:T(8,128)(2,1)S(1)}, u32[]{:S(2)}, u32[]{:S(2)}) %collective-permute-start.11) | collective-permute-done | bytes 1703968 | tf_op jit(solution)/shard_map/ppermute | solution.py:458
  139.6 4.6 %shard_map.106 = (f32[256,2048]{1,0:T(8,128)}, f32[256,1280]{1,0:T(8,128)}) custom-call(f32[256,3328]{1,0:T(8,128)} %get-tuple-element.72.keep_ref, bf16[256,3328]{1,0:T(8,128)(2,1)} %copy-done.3), custom_call_target="tpu_custom_call" | custom-call | flops 1048576 | bytes 65536 | tf_op jit(solution)/shard_map/pallas_call | solution.py:289
  144.2 11.7 %collective-permute-done.12.refs_6_ = bf16[640,1280]{1,0:T(8,128)(2,1)} collective-permute-done((bf16[640,1280]{1,0:T(8,128)(2,1)}, bf16[640,1280]{1,0:T(8,128)(2,1)}, u32[]{:S(2)}, u32[]{:S(2)}) %collective-permute-start.12) | collective-permute-done | bytes 1638432 | tf_op jit(solution)/shard_map/ppermute | solution.py:422
  155.9 19.9 %shard_map.109.refs_0_ = f32[640,2048]{1,0:T(8,128)} custom-call(s32[1]{0:T(128)} %bitcast.here_ref._, s32[1]{0:T(128)} %bitcast.here_ref._, s32[1,1024]{1,0:T(1,128)} %bitcast.14, f32[32,1024]{1,0:T(8,128)} %get-tuple-element.78.refs_1_, bf16[1024,2048]{1,0:T(8,128)(2,1)} %bitcast.8, bf16[640,1280]{1,0:T(8,128)(2,1)} %copy-done.1, ...), custom_call_target="tpu_custom_call" | custom-call | flops 1048576 | bytes 65536 | tf_op jit(solution)/shard_map/pallas_call | solution.py:368
  177.0 6.2 %shard_map.110._ = bf16[1024,2048]{1,0:T(8,128)(2,1)} custom-call(s32[1]{0:T(128)} %bitcast.here_ref._, bf16[1024,2048]{1,0:T(8,128)(2,1)} %shard_map.108._, f32[640,2048]{1,0:T(8,128)} %shard_map.109.refs_0_, bf16[640,1280]{1,0:T(8,128)(2,1)} %collective-permute-done.10.refs_1_, ...), custom_call_target="tpu_custom_call", output_to_operand_aliasing={{}: (1, {})} | custom-call | flops 1048576 | bytes 65536 | tf_op jit(solution)/shard_map/pallas_call | solution.py:368
  183.1 7.5 %collective-permute-done.16.refs_2_ = bf16[256,1280]{1,0:T(8,128)(2,1)} collective-permute-done((bf16[256,1280]{1,0:T(8,128)(2,1)}, bf16[256,1280]{1,0:T(8,128)(2,1)}, u32[]{:S(2)}, u32[]{:S(2)}) %collective-permute-start.16) | collective-permute-done | bytes 655392 | tf_op jit(solution)/shard_map/ppermute | solution.py:422
  190.6 5.2 %shard_map.111 = bf16[1024,2048]{1,0:T(8,128)(2,1)} custom-call(s32[1]{0:T(128)} %bitcast.here_ref._, bf16[1024,2048]{1,0:T(8,128)(2,1)} %shard_map.110._, f32[640,2048]{1,0:T(8,128)} %shard_map.109.refs_0_, bf16[640,1280]{1,0:T(8,128)(2,1)} %collective-permute-done.10.refs_1_, ...), custom_call_target="tpu_custom_call", output_to_operand_aliasing={{}: (1, {})} | custom-call | flops 1048576 | bytes 65536 | tf_op jit(solution)/shard_map/pallas_call | solution.py:368
  (58 shorter events, 27.6 us)
Async XLA Ops:
  1.9 16.0 %copy-start.2 = (bf16[384,1280]{1,0:T(8,128)(2,1)}, bf16[384,1280]{1,0:T(8,128)(2,1)S(1)}, u32[]{:S(2)}) copy-start(bf16[384,1280]{1,0:T(8,128)(2,1)S(1)} %slice.20.refs_3_) | copy-start | bytes 2949124
  1.9 27.7 %collective-permute-start = (bf16[384,1280]{1,0:T(8,128)(2,1)S(1)}, bf16[384,1280]{1,0:T(8,128)(2,1)}, u32[]{:S(2)}, u32[]{:S(2)}) collective-permute-start(bf16[384,1280]{1,0:T(8,128)(2,1)S(1)} %slice.20.refs_3_), channel_id=1, source_target_pairs={{0,4},{4,0},{8,12},{12,8},{1,5},{5,1},{9,13},{13,9},{2,6},{6,2},{1... | collective-permute-start | bytes 2949128 | tf_op jit(solution)/shard_map/ppermute | solution.py:416
  5.0 24.6 %collective-permute-start.1 = (bf16[384,1280]{1,0:T(8,128)(2,1)S(1)}, bf16[384,1280]{1,0:T(8,128)(2,1)S(1)}, u32[]{:S(2)}, u32[]{:S(2)}) collective-permute-start(bf16[384,1280]{1,0:T(8,128)(2,1)S(1)} %slice.20.refs_3_), channel_id=1, source_target_pairs={{4,8},{8,4},{5,9},{9,5},{6,10},{10,6},{7,11},{11,7},{20,24},{24,20... | collective-permute-start | bytes 2949128 | tf_op jit(solution)/shard_map/ppermute | solution.py:419
  17.9 11.7 %collective-permute-start.2 = (f32[32,1024]{1,0:T(8,128)}, f32[32,1024]{1,0:T(8,128)S(1)}, u32[]{:S(2)}, u32[]{:S(2)}) collective-permute-start(f32[32,1024]{1,0:T(8,128)} %shard_map.103), channel_id=1, source_target_pairs={{0,4},{4,0},{8,12},{12,8},{1,5},{5,1},{9,13},{13,9},{2,6},{6,2},{1... | collective-permute-start | bytes 393224 | tf_op jit(solution)/shard_map/ppermute | solution.py:416
  23.3 23.3 %copy-start = (bf16[1024,1280]{1,0:T(8,128)(2,1)S(1)}, bf16[1024,1280]{1,0:T(8,128)(2,1)}, u32[]{:S(2)}) copy-start(bf16[1024,1280]{1,0:T(8,128)(2,1)} %gradient_ref.3) | copy-start | bytes 7864324
  29.6 17.0 %copy-start.5 = (bf16[384,1280]{1,0:T(8,128)(2,1)}, bf16[384,1280]{1,0:T(8,128)(2,1)S(1)}, u32[]{:S(2)}) copy-start(bf16[384,1280]{1,0:T(8,128)(2,1)S(1)} %collective-permute-done.1.refs_1_) | copy-start | bytes 2949124
  29.6 15.3 %collective-permute-start.4 = (bf16[192,1280]{1,0:T(8,128)(2,1)S(1)}, bf16[192,1280]{1,0:T(8,128)(2,1)S(1)}, u32[]{:S(2)}, u32[]{:S(2)}) collective-permute-start(bf16[192,1280]{1,0:T(8,128)(2,1)S(1)} %slice.21), channel_id=1, source_target_pairs={{0,4},{4,0},{8,12},{12,8},{1,5},{5,1},{9,13},{13,9},{2,6},{6,2},{1... | collective-permute-start | bytes 1474568 | tf_op jit(solution)/shard_map/ppermute | solution.py:416
  32.4 14.3 %copy-start.4 = (f32[32,1024]{1,0:T(8,128)}, f32[32,1024]{1,0:T(8,128)S(1)}, u32[]{:S(2)}) copy-start(f32[32,1024]{1,0:T(8,128)S(1)} %add.10.pair) | copy-start | bytes 393220
  32.5 0.7 collective-permute-start.3
  33.1 13.6 %copy-start.6 = (f32[32,1024]{1,0:T(8,128)}, f32[32,1024]{1,0:T(8,128)S(1)}, u32[]{:S(2)}) copy-start(f32[32,1024]{1,0:T(8,128)S(1)} %collective-permute-done.3.crossed) | copy-start | bytes 393220
  33.2 11.7 %collective-permute-start.5 = (f32[32,1024]{1,0:T(8,128)S(1)}, f32[32,1024]{1,0:T(8,128)S(1)}, u32[]{:S(2)}, u32[]{:S(2)}) collective-permute-start(f32[32,1024]{1,0:T(8,128)S(1)} %add.11), channel_id=1, source_target_pairs={{4,0},{8,12},{5,1},{9,13},{6,2},{10,14},{7,3},{11,15},{20,16},{24,... | collective-permute-start | bytes 393224 | tf_op jit(solution)/shard_map/ppermute | solution.py:422
  36.8 10.0 %copy-start.10 = (s32[4]{0:T(128)S(1)}, s32[4]{0:T(128)}, u32[]{:S(2)}) copy-start(s32[4]{0:T(128)} %constant.13.clone) | copy-start | bytes 52
  44.9 26.2 %collective-permute-start.6 = (bf16[448,1280]{1,0:T(8,128)(2,1)}, bf16[448,1280]{1,0:T(8,128)(2,1)}, u32[]{:S(2)}, u32[]{:S(2)}) collective-permute-start(bf16[448,1280]{1,0:T(8,128)(2,1)} %slice.22), channel_id=1, source_target_pairs={{0,4},{4,0},{8,12},{12,8},{1,5},{5,1},{9,13},{13,9},{2,6},{6,2},{1... | collective-permute-start | bytes 3440648 | tf_op jit(solution)/shard_map/ppermute | solution.py:416
  44.9 19.4 %collective-permute-start.7 = (bf16[384,1280]{1,0:T(8,128)(2,1)}, bf16[384,1280]{1,0:T(8,128)(2,1)}, u32[]{:S(2)}, u32[]{:S(2)}) collective-permute-start(bf16[384,1280]{1,0:T(8,128)(2,1)} %collective-permute-done.refs_4_), channel_id=1, source_target_pairs={{4,8},{8,4},{5,9},{9,5},{6,10},{10,6},{7,11},{11,7},{20,24},{24,20... | collective-permute-start | bytes 2949128 | tf_op jit(solution)/shard_map/ppermute | solution.py:419
  46.7 24.4 %copy-start.1 = (bf16[640,1280]{1,0:T(8,128)(2,1)}, bf16[640,1280]{1,0:T(8,128)(2,1)S(1)}, u32[]{:S(2)}) copy-start(bf16[640,1280]{1,0:T(8,128)(2,1)S(1)} %slice.23.refs_3_) | copy-start | bytes 4915204
  71.1 11.3 %collective-permute-start.8 = (f32[512,3328]{1,0:T(8,128)}, f32[512,3328]{1,0:T(8,128)}, u32[]{:S(2)}, u32[]{:S(2)}) collective-permute-start(f32[512,3328]{1,0:T(8,128)} %get-tuple-element.63), channel_id=1, source_target_pairs={{0,1},{1,0},{2,3},{3,2},{4,5},{5,4},{6,7},{7,6},{8,9},{9,8},{10,11... | collective-permute-start | bytes 20447240 | tf_op jit(solution)/shard_map/ppermute | solution.py:449
  71.1 28.6 %collective-permute-start.10 = (bf16[640,1280]{1,0:T(8,128)(2,1)S(1)}, bf16[640,1280]{1,0:T(8,128)(2,1)}, u32[]{:S(2)}, u32[]{:S(2)}) collective-permute-start(bf16[640,1280]{1,0:T(8,128)(2,1)S(1)} %slice.23.refs_3_), channel_id=1, source_target_pairs={{4,8},{8,4},{5,9},{9,5},{6,10},{10,6},{7,11},{11,7},{20,24},{24,20... | collective-permute-start | bytes 4915208 | tf_op jit(solution)/shard_map/ppermute | solution.py:419
  73.0 26.7 %collective-permute-start.9 = (bf16[384,1280]{1,0:T(8,128)(2,1)}, bf16[384,1280]{1,0:T(8,128)(2,1)}, u32[]{:S(2)}, u32[]{:S(2)}) collective-permute-start(bf16[384,1280]{1,0:T(8,128)(2,1)} %copy-done.5), channel_id=1, source_target_pairs={{4,0},{8,12},{5,1},{9,13},{6,2},{10,14},{7,3},{11,15},{20,16},{24,... | collective-permute-start | bytes 2949128 | tf_op jit(solution)/shard_map/ppermute | solution.py:422
  86.7 40.3 %collective-permute-start.14 = (bf16[640,1280]{1,0:T(8,128)(2,1)}, bf16[640,1280]{1,0:T(8,128)(2,1)}, u32[]{:S(2)}, u32[]{:S(2)}) collective-permute-start(bf16[640,1280]{1,0:T(8,128)(2,1)} %constant_dynamic-update-slice_fusion.refs_4_), channel_id=1, source_target_pairs={{4,8},{8,4},{5,9},{9,5},{6,10},{10,6},{7,11},{11,7},{20,24},{24,20... | collective-permute-start | bytes 4915208 | tf_op jit(solution)/shard_map/ppermute | solution.py:419
  88.5 32.3 %collective-permute-start.13 = (bf16[384,1280]{1,0:T(8,128)(2,1)}, bf16[384,1280]{1,0:T(8,128)(2,1)}, u32[]{:S(2)}, u32[]{:S(2)}) collective-permute-start(bf16[384,1280]{1,0:T(8,128)(2,1)} %collective-permute-done.7.refs_5_), channel_id=1, source_target_pairs={{4,0},{8,12},{5,1},{9,13},{6,2},{10,14},{7,3},{11,15},{20,16},{24,... | collective-permute-start | bytes 2949128 | tf_op jit(solution)/shard_map/ppermute | solution.py:422
  99.7 38.7 %collective-permute-start.11 = (bf16[256,3328]{1,0:T(8,128)(2,1)}, bf16[256,3328]{1,0:T(8,128)(2,1)S(1)}, u32[]{:S(2)}, u32[]{:S(2)}) collective-permute-start(bf16[256,3328]{1,0:T(8,128)(2,1)} %get-tuple-element.73), channel_id=1, source_target_pairs={{0,2},{1,3},{2,0},{3,1},{4,6},{5,7},{6,4},{7,5},{8,10},{9,11},{10,... | collective-permute-start | bytes 5111816 | tf_op jit(solution)/shard_map/ppermute | solution.py:458
  101.2 54.7 %collective-permute-start.12 = (bf16[640,1280]{1,0:T(8,128)(2,1)}, bf16[640,1280]{1,0:T(8,128)(2,1)}, u32[]{:S(2)}, u32[]{:S(2)}) collective-permute-start(bf16[640,1280]{1,0:T(8,128)(2,1)} %collective-permute-done.10.refs_1_), channel_id=1, source_target_pairs={{4,0},{8,12},{5,1},{9,13},{6,2},{10,14},{7,3},{11,15},{20,16},{24,... | collective-permute-start | bytes 4915208 | tf_op jit(solution)/shard_map/ppermute | solution.py:422
  129.2 47.8 %collective-permute-start.15 = (bf16[384,1280]{1,0:T(8,128)(2,1)}, bf16[384,1280]{1,0:T(8,128)(2,1)}, u32[]{:S(2)}, u32[]{:S(2)}) collective-permute-start(bf16[384,1280]{1,0:T(8,128)(2,1)} %slice.24), channel_id=1, source_target_pairs={{4,0},{8,12},{5,1},{9,13},{6,2},{10,14},{7,3},{11,15},{20,16},{24,... | collective-permute-start | bytes 2949128 | tf_op jit(solution)/shard_map/ppermute | solution.py:422
  132.5 58.1 %collective-permute-start.16 = (bf16[256,1280]{1,0:T(8,128)(2,1)}, bf16[256,1280]{1,0:T(8,128)(2,1)}, u32[]{:S(2)}, u32[]{:S(2)}) collective-permute-start(bf16[256,1280]{1,0:T(8,128)(2,1)} %slice.25), channel_id=1, source_target_pairs={{4,0},{8,12},{5,1},{9,13},{6,2},{10,14},{7,3},{11,15},{20,16},{24,... | collective-permute-start | bytes 1966088 | tf_op jit(solution)/shard_map/ppermute | solution.py:422
  (4 other events, 18.8 us)
